TPU v7x, 128 devices: a whole 4x4x4 slice. The times are simulated.
128 devices in a mesh: section: 8 (over x, core), ctx: 16 (over z, y).
Axes of the slice: x: 4, y: 4, z: 4, core: 2. Of those that a mesh axis runs over, the one named last changes fastest.
Arguments:
- segment_input: bfloat16 [8, 2048, 8192], P('section', 'ctx'), may hold values from -6 to 6
- queries: bfloat16 [8, 2048, 8192], P('section', 'ctx'), may hold values from -6 to 6
- keys: bfloat16 [8, 2048, 1024], P('section', 'ctx'), may hold values from -6 to 6
- values: bfloat16 [8, 2048, 1024], P('section', 'ctx'), may hold values from -6 to 6
- cotangent: bfloat16 [8, 2048, 8192], P('section', 'ctx'), may hold values from -6 to 6
- selected: int32 [8, 2048], P('section', 'ctx'), may hold values from 0 to 127, as said below
- counts: int32 [8, 16], P('section', 'ctx'), may hold values from 1 to 128, as said below
Outputs:
- next_input: bfloat16 [8, 2048, 8192], P('section', 'ctx')
- query_grad: bfloat16 [8, 2048, 8192], P('section', 'ctx')
- key_grad: bfloat16 [8, 2048, 1024], P('section', 'ctx')
- value_grad: bfloat16 [8, 2048, 1024], P('section', 'ctx')
Inputs may be any that keep to these rules, and one draw needn't show every extreme that they name: Layers of odd index are dense: every count is 128. Layers of even index are routed: counts are at most 32. Each block of 128 entries is a permutation of the block-local indices; its first count entries are the selected ones, in increasing order.
All inputs are finite; a program needn't handle non-finite values.
Results may differ from a plain program's by a relative error of at most 0.019.
Values may be sent and summed in bfloat16 or wider, within the bound.
No kernel may reach another device: no remote copies, remote signals or barrier semaphores. Data moves between devices by JAX's collectives and lax.ppermute only.
A program may use at most 128 MiB of HBM per device.

v0:
```python
import jax
import jax.numpy as jnp
from jax import lax
from jax.sharding import PartitionSpec as P

KV_HEADS = 8
HEAD_DIM = 128


masked_value = -1000000000.0


def from_behind(array, axis, by):
    length = lax.axis_size(axis)
    pairs = [(i, i + by) for i in range(length) if 0 <= i + by < length]
    return lax.ppermute(array, axis, pairs)


def masked_scores(query_group, key_group, query_place, key_place):
    scaling = query_group.shape[-1] ** (-0.5)
    allowed = (key_place[None, :] <= query_place[:, None]) & (key_place[None, :] >= 0)
    scores = (
        jnp.einsum("qih,kh->qik", query_group, key_group, preferred_element_type=jnp.float32)
        * scaling
    )
    return jnp.where(allowed[:, None, :], scores, masked_value)


def attend_group(query_group, key_group, value_group, query_place, key_place):
    scores = masked_scores(query_group, key_group, query_place, key_place)
    maxima = jnp.max(scores, axis=-1, keepdims=True)
    weights = jnp.exp(scores - maxima)
    totals = jnp.sum(weights, axis=-1, keepdims=True)
    prob_b = (weights / totals).astype(jnp.bfloat16)
    output = jnp.einsum("qik,kh->qih", prob_b, value_group, preferred_element_type=jnp.float32)
    return (output, maxima[..., 0], totals[..., 0])


def score_parts(
    query_group,
    key_group,
    value_group,
    query_place,
    key_place,
    output_group,
    maxima,
    totals,
    out_grad,
):
    scores = masked_scores(query_group, key_group, query_place, key_place)
    weights = jnp.exp(scores - maxima[..., None]) / totals[..., None]
    along = jnp.einsum("qih,kh->qik", out_grad, value_group, preferred_element_type=jnp.float32)
    deltas = jnp.sum(out_grad.astype(jnp.float32) * output_group, axis=-1)
    score_grad = (weights * (along - deltas[..., None])).astype(jnp.bfloat16)
    return (weights.astype(jnp.bfloat16), score_grad)


def both_grads(
    query_group,
    key_group,
    value_group,
    query_place,
    key_place,
    output_group,
    maxima,
    totals,
    out_grad,
):
    scaling = query_group.shape[-1] ** (-0.5)
    prob_b, score_grad = score_parts(
        query_group,
        key_group,
        value_group,
        query_place,
        key_place,
        output_group,
        maxima,
        totals,
        out_grad,
    )
    query_grad = (
        jnp.einsum("qik,kh->qih", score_grad, key_group, preferred_element_type=jnp.float32)
        * scaling
    )
    key_grad = (
        jnp.einsum("qik,qih->kh", score_grad, query_group, preferred_element_type=jnp.float32)
        * scaling
    )
    value_grad = jnp.einsum("qik,qih->kh", prob_b, out_grad, preferred_element_type=jnp.float32)
    return (query_grad, key_grad, value_grad)


def head_groups(matrix):
    return matrix.reshape(matrix.shape[0], KV_HEADS, -1, HEAD_DIM).transpose(1, 0, 2, 3)


def pair_groups(key_value):
    count_rows = key_value.shape[0]
    width = KV_HEADS * HEAD_DIM
    key_group = key_value[:, :width].reshape(count_rows, KV_HEADS, HEAD_DIM).transpose(1, 0, 2)
    value_group = key_value[:, width:].reshape(count_rows, KV_HEADS, HEAD_DIM).transpose(1, 0, 2)
    return (key_group, value_group)


def merge_heads(stacked):
    return stacked.transpose(1, 0, 2, 3).reshape(stacked.shape[1], -1)


def merge_groups(stacked):
    return stacked.transpose(1, 0, 2).reshape(stacked.shape[1], -1)


def forward(query_sel, key_value, query_place, key_place):
    key_group, value_group = pair_groups(key_value)
    output, maxima, totals = lax.map(
        lambda items: attend_group(items[0], items[1], items[2], query_place, key_place),
        (head_groups(query_sel), key_group, value_group),
    )
    return (merge_heads(output), maxima, totals)


def per_group(
    grad_fn, query_sel, key_value, query_place, key_place, output, maxima, totals, out_grad
):
    key_group, value_group = pair_groups(key_value)
    return lax.map(
        lambda items: grad_fn(
            items[0],
            items[1],
            items[2],
            query_place,
            key_place,
            items[3],
            items[4],
            items[5],
            items[6],
        ),
        (
            head_groups(query_sel),
            key_group,
            value_group,
            head_groups(output),
            maxima,
            totals,
            head_groups(out_grad),
        ),
    )


def body(segment_input, queries, keys, values, cotangent, selected, counts):
    rows = segment_input.shape[1]
    slot_ids = jnp.arange(rows, dtype=jnp.int32)
    is_valid = slot_ids < counts[0, 0]
    chooser = (selected[0][:, None] == slot_ids[None, :]) & is_valid[:, None]
    onehot = chooser.astype(jnp.bfloat16)
    inverse = jnp.zeros((rows,), jnp.int32).at[selected[0]].set(slot_ids)
    token_valid = inverse < counts[0, 0]

    def gather_rows(matrix):
        return jnp.dot(onehot, matrix[0], preferred_element_type=jnp.float32).astype(jnp.bfloat16)

    def place_rows(matrix):
        return jnp.where(token_valid[:, None], jnp.take(matrix, inverse, axis=0), 0.0)

    query_sel = gather_rows(queries)
    own_pairs = jnp.concatenate([gather_rows(keys), gather_rows(values)], 1)
    position = jnp.where(is_valid, lax.axis_index("ctx") * rows + selected[0], -1)
    key_value, key_place = (
        lax.all_gather(own_pairs, "ctx", axis=0, tiled=True),
        lax.all_gather(position, "ctx", axis=0, tiled=True),
    )
    output, maxima, totals = forward(query_sel, key_value, position, key_place)
    attn_b = output.astype(jnp.bfloat16)
    placed = jnp.dot(onehot.T, attn_b, preferred_element_type=jnp.float32)
    updated = (segment_input[0].astype(jnp.float32) + placed).astype(jnp.bfloat16)
    next_input = from_behind(updated, "section", 1)
    out_grad = gather_rows(cotangent)
    query_stack, key_stack, value_stack = per_group(
        both_grads, query_sel, key_value, position, key_place, output, maxima, totals, out_grad
    )
    query_grad = merge_heads(query_stack)
    pair_term = jnp.concatenate([merge_groups(key_stack), merge_groups(value_stack)], 1)
    pair_grad = lax.psum_scatter(
        pair_term.astype(jnp.bfloat16), "ctx", scatter_dimension=0, tiled=True
    ).astype(jnp.float32)
    query_rows = place_rows(query_grad).astype(jnp.bfloat16)
    pair_rows = place_rows(pair_grad)
    width = pair_rows.shape[1] // 2
    return (
        next_input[None],
        query_rows[None],
        pair_rows[:, :width].astype(jnp.bfloat16)[None],
        pair_rows[:, width:].astype(jnp.bfloat16)[None],
    )


def solution(mesh):
    placed = (
        P("section", "ctx", None),
        P("section", "ctx", None),
        P("section", "ctx", None),
        P("section", "ctx", None),
        P("section", "ctx", None),
        P("section", "ctx"),
        P("section", "ctx"),
    )
    return jax.shard_map(
        body,
        mesh=mesh,
        in_specs=placed,
        out_specs=(
            P("section", "ctx", None),
            P("section", "ctx", None),
            P("section", "ctx", None),
            P("section", "ctx", None),
        ),
        check_vma=False,
    )
```

profile of v0, /device:TPU:1, one launch (start us, length us, event | category | flops | bytes accessed | tf_op | source)
XLA Modules:
  0.0 419.6 jit_solution(13789873598682588359)
XLA Ops:
  17.7 20.1 %all-gather = s32[16,1,128]{2,1,0:T(1,128)S(1)} all-gather(s32[1,1,128]{2,1,0:T(1,128)S(1)} %fusion.85), channel_id=1, replica_groups=mesh['section'=8,'ctx'=16] {'ctx'}, dimensions={0}, use_global_device_ids=true | all-gather | bytes 8704 | tf_op jit(solution)/shard_map/all_gather | solution.py:170
  39.7 6.9 %copy_bitcast_fusion.3 = (bf16[8,128,8,128]{3,1,2,0:T(8,128)(2,1)}, bf16[8,128,8,128]{3,1,2,0:T(8,128)(2,1)}) fusion(bf16[128,8,8,128]{3,2,1,0:T(8,128)(2,1)} %bitcast.239, bf16[128,8,8,128]{3,2,1,0:T(8,128)(2,1)} %bitcast.238), kind=kLoop, calls=%fused_computation.83 | loop fusion | bytes 8388608 | tf_op jit(solution)/shard_map/transpose | solution.py:94
  46.5 39.1 %all-gather.3.cloned.1.call-done = bf16[2048,2048]{1,0:T(8,128)(2,1)} async-done(((bf16[128,2048]{1,0:T(8,128)(2,1)}), bf16[2048,2048]{1,0:T(8,128)(2,1)}) %all-gather.3.cloned.1.call-update) | async-done | bytes 8388624 | tf_op jit(solution)/shard_map/all_gather | solution.py:169
  85.6 4.4 %slice_bitcast_fusion = (bf16[256,8,8,128]{3,2,1,0:T(8,128)(2,1)S(1)}, bf16[256,8,8,128]{3,2,1,0:T(8,128)(2,1)S(1)}) fusion(bf16[2048,2048]{1,0:T(8,128)(2,1)} %all-gather.3.cloned.1.call-done), kind=kLoop, calls=%fused_computation.74 | loop fusion | bytes 16777216
  90.1 5.3 %bitcast_bitcast_fusion = (bf16[8,2048,128]{2,1,0:T(8,128)(2,1)}, bf16[8,2048,128]{2,1,0:T(8,128)(2,1)}) fusion(bf16[256,8,8,128]{3,2,1,0:T(8,128)(2,1)S(1)} %get-tuple-element.178, bf16[256,8,8,128]{3,2,1,0:T(8,128)(2,1)S(1)} %get-tuple-element.179), kind=kLoop, calls=%fused_computation.72 | loop fusion | bytes 16777216 | tf_op jit(solution)/shard_map/transpose | solution.py:101
  95.4 75.7 %while.30 = (s32[]{:T(128)}, f32[8,128,8,128]{3,1,2,0:T(8,128)}, f32[8,128,8]{1,2,0:T(8,128)S(1)}, f32[8,128,8]{1,2,0:T(8,128)S(1)}, s32[2048]{0:T(1024)S(1)}, /...) while((s32[]{:T(128)}, f32[8,128,8,128]{3,1,2,0:T(8,128)}, ...), condition=%wide.region_3.4_spmd.clone, body=%wide.region_0.3_spmd.sunk.clone | while | flops 1099431936 | bytes 28109408 | solution.py:115
  95.6 2.8 fusion.125
  100.6 4.2 %fusion.127 = f32[8,128,8,128]{3,1,2,0:T(8,128)} fusion(f32[8,128,8,128]{3,1,2,0:T(8,128)} %get-tuple-element.398, s32[]{:T(128)} %get-tuple-element.397, f32[128,8,2048]{2,0,1:T(8,128)S(1)} %get-tuple-element.344, f32[128,8]{0,1:T(8,128)S(1)} %fusion.126, f32[128,8]{0,1:T(8,128)S(1)} %get-tuple-element.345, ...), kind=kOutput, calls=%fused_computation.10.clone.1.clone | convolution fusion | flops 547356672 | bytes 9708544 | tf_op jit(solution)/shard_map/while/body/eval_jaxpr/qik,kh->qih/dot_general | solution.py:35
  105.1 2.8 fusion.125
  110.1 4.2 %fusion.127 = f32[8,128,8,128]{3,1,2,0:T(8,128)} fusion(f32[8,128,8,128]{3,1,2,0:T(8,128)} %get-tuple-element.398, s32[]{:T(128)} %get-tuple-element.397, f32[128,8,2048]{2,0,1:T(8,128)S(1)} %get-tuple-element.344, f32[128,8]{0,1:T(8,128)S(1)} %fusion.126, f32[128,8]{0,1:T(8,128)S(1)} %get-tuple-element.345, ...), kind=kOutput, calls=%fused_computation.10.clone.1.clone | convolution fusion | flops 547356672 | bytes 9708544 | tf_op jit(solution)/shard_map/while/body/eval_jaxpr/qik,kh->qih/dot_general | solution.py:35
  114.6 2.8 fusion.125
  119.6 4.2 %fusion.127 = f32[8,128,8,128]{3,1,2,0:T(8,128)} fusion(f32[8,128,8,128]{3,1,2,0:T(8,128)} %get-tuple-element.398, s32[]{:T(128)} %get-tuple-element.397, f32[128,8,2048]{2,0,1:T(8,128)S(1)} %get-tuple-element.344, f32[128,8]{0,1:T(8,128)S(1)} %fusion.126, f32[128,8]{0,1:T(8,128)S(1)} %get-tuple-element.345, ...), kind=kOutput, calls=%fused_computation.10.clone.1.clone | convolution fusion | flops 547356672 | bytes 9708544 | tf_op jit(solution)/shard_map/while/body/eval_jaxpr/qik,kh->qih/dot_general | solution.py:35
  124.0 2.8 fusion.125
  129.0 4.2 %fusion.127 = f32[8,128,8,128]{3,1,2,0:T(8,128)} fusion(f32[8,128,8,128]{3,1,2,0:T(8,128)} %get-tuple-element.398, s32[]{:T(128)} %get-tuple-element.397, f32[128,8,2048]{2,0,1:T(8,128)S(1)} %get-tuple-element.344, f32[128,8]{0,1:T(8,128)S(1)} %fusion.126, f32[128,8]{0,1:T(8,128)S(1)} %get-tuple-element.345, ...), kind=kOutput, calls=%fused_computation.10.clone.1.clone | convolution fusion | flops 547356672 | bytes 9708544 | tf_op jit(solution)/shard_map/while/body/eval_jaxpr/qik,kh->qih/dot_general | solution.py:35
  133.5 2.8 fusion.125
  138.5 4.2 %fusion.127 = f32[8,128,8,128]{3,1,2,0:T(8,128)} fusion(f32[8,128,8,128]{3,1,2,0:T(8,128)} %get-tuple-element.398, s32[]{:T(128)} %get-tuple-element.397, f32[128,8,2048]{2,0,1:T(8,128)S(1)} %get-tuple-element.344, f32[128,8]{0,1:T(8,128)S(1)} %fusion.126, f32[128,8]{0,1:T(8,128)S(1)} %get-tuple-element.345, ...), kind=kOutput, calls=%fused_computation.10.clone.1.clone | convolution fusion | flops 547356672 | bytes 9708544 | tf_op jit(solution)/shard_map/while/body/eval_jaxpr/qik,kh->qih/dot_general | solution.py:35
  147.9 4.2 %fusion.127 = f32[8,128,8,128]{3,1,2,0:T(8,128)} fusion(f32[8,128,8,128]{3,1,2,0:T(8,128)} %get-tuple-element.398, s32[]{:T(128)} %get-tuple-element.397, f32[128,8,2048]{2,0,1:T(8,128)S(1)} %get-tuple-element.344, f32[128,8]{0,1:T(8,128)S(1)} %fusion.126, f32[128,8]{0,1:T(8,128)S(1)} %get-tuple-element.345, ...), kind=kOutput, calls=%fused_computation.10.clone.1.clone | convolution fusion | flops 547356672 | bytes 9708544 | tf_op jit(solution)/shard_map/while/body/eval_jaxpr/qik,kh->qih/dot_general | solution.py:35
  152.4 2.8 fusion.125
  157.4 4.2 %fusion.127 = f32[8,128,8,128]{3,1,2,0:T(8,128)} fusion(f32[8,128,8,128]{3,1,2,0:T(8,128)} %get-tuple-element.398, s32[]{:T(128)} %get-tuple-element.397, f32[128,8,2048]{2,0,1:T(8,128)S(1)} %get-tuple-element.344, f32[128,8]{0,1:T(8,128)S(1)} %fusion.126, f32[128,8]{0,1:T(8,128)S(1)} %get-tuple-element.345, ...), kind=kOutput, calls=%fused_computation.10.clone.1.clone | convolution fusion | flops 547356672 | bytes 9708544 | tf_op jit(solution)/shard_map/while/body/eval_jaxpr/qik,kh->qih/dot_general | solution.py:35
  161.9 2.8 fusion.125
  166.9 4.2 %fusion.127 = f32[8,128,8,128]{3,1,2,0:T(8,128)} fusion(f32[8,128,8,128]{3,1,2,0:T(8,128)} %get-tuple-element.398, s32[]{:T(128)} %get-tuple-element.397, f32[128,8,2048]{2,0,1:T(8,128)S(1)} %get-tuple-element.344, f32[128,8]{0,1:T(8,128)S(1)} %fusion.126, f32[128,8]{0,1:T(8,128)S(1)} %get-tuple-element.345, ...), kind=kOutput, calls=%fused_computation.10.clone.1.clone | convolution fusion | flops 547356672 | bytes 9708544 | tf_op jit(solution)/shard_map/while/body/eval_jaxpr/qik,kh->qih/dot_general | solution.py:35
  171.1 135.6 %while.31 = (s32[]{:T(128)}, bf16[8,128,8,128]{3,1,2,0:T(8,128)(2,1)}, bf16[8,2048,128]{2,1,0:T(8,128)(2,1)}, bf16[8,2048,128]{2,1,0:T(8,128)(2,1)}, s32[2048]{0...) while((s32[]{:T(128)}, ...), condition=%wide.region_7.8_spmd.clone, body=%wide.region_5.7_spmd.sunk.clone | while | flops 2702443520 | bytes 44361348 | solution.py:126
  171.4 3.7 exponential_divide_fusion.3
  178.8 3.1 fusion.140
  182.0 3.0 fusion.139
  185.0 3.1 fusion.141
  188.4 3.7 exponential_divide_fusion.3
  195.8 3.1 fusion.140
  198.9 3.0 fusion.139
  202.0 3.1 fusion.141
  205.4 3.7 exponential_divide_fusion.3
  212.8 3.1 fusion.140
  215.9 3.0 fusion.139
  218.9 3.1 fusion.141
  222.3 3.7 exponential_divide_fusion.3
  229.8 3.1 fusion.140
  232.9 3.0 fusion.139
  235.9 3.1 fusion.141
  239.2 3.7 exponential_divide_fusion.3
  246.7 3.1 fusion.140
  249.8 3.0 fusion.139
  252.8 3.1 fusion.141
  256.1 3.7 exponential_divide_fusion.3
  263.6 3.1 fusion.140
  266.6 3.0 fusion.139
  269.7 3.1 fusion.141
  273.0 3.7 exponential_divide_fusion.3
  280.5 3.1 fusion.140
  283.6 3.0 fusion.139
  286.6 3.1 fusion.141
  290.0 3.7 exponential_divide_fusion.3
  297.4 3.1 fusion.140
  300.5 3.0 fusion.139
  303.6 3.1 fusion.141
  306.7 4.9 %copy_bitcast_fusion.1 = bf16[2048,1024]{1,0:T(8,128)(2,1)} fusion(bf16[8,2048,128]{2,1,0:T(8,128)(2,1)} %get-tuple-element.127), kind=kLoop, calls=%fused_computation.70 | loop fusion | bytes 8388608 | tf_op jit(solution)/shard_map/reshape | solution.py:110
  314.2 8.1 %pad_maximum_fusion = bf16[2048,2048]{1,0:T(8,128)(2,1)} fusion(bf16[2048,1024]{1,0:T(8,128)(2,1)} %copy_bitcast_fusion.1, bf16[2048,1024]{1,0:T(8,128)(2,1)} %copy_bitcast_fusion.2), kind=kLoop, calls=%fused_computation.68 | loop fusion | flops 16777216 | bytes 16777216 | tf_op jit(solution)/shard_map/concatenate | solution.py:182
  324.0 3.5 copy.35
  327.5 3.9 fusion.49
  331.4 3.9 collective-permute-start
  338.5 3.2 gather_fusion
  341.7 3.6 fusion.51
  345.3 13.0 %collective-permute-done = bf16[128,8192]{1,0:T(8,128)(2,1)} collective-permute-done((bf16[128,8192]{1,0:T(8,128)(2,1)}, bf16[128,8192]{1,0:T(8,128)(2,1)}, u32[]{:S(2)}, u32[]{:S(2)}) %collective-permute-start) | collective-permute-done | bytes 2097184 | tf_op jit(solution)/shard_map/ppermute | solution.py:16
  358.3 47.5 %reduce-scatter.2.cloned.1.call-done = bf16[128,2048]{1,0:T(8,128)(2,1)} async-done(((bf16[2048,2048]{1,0:T(8,128)(2,1)}), bf16[128,2048]{1,0:T(8,128)(2,1)}) %reduce-scatter.2.cloned.1.call-update) | async-done | bytes 524304 | tf_op jit(solution)/shard_map/reduce_scatter | solution.py:183
  409.7 3.1 copy.89
  (123 shorter events, 77.3 us)
Async XLA Ops:
  7.2 4.3 %copy-start = (bf16[1,128,8192]{2,1,0:T(8,128)(2,1)S(1)}, bf16[1,128,8192]{2,1,0:T(8,128)(2,1)}, u32[]{:S(2)}) copy-start(bf16[1,128,8192]{2,1,0:T(8,128)(2,1)} %param.12) | copy-start | bytes 6291460
  7.2 78.5 %all-gather.3.cloned.1.call-start = ((), (), s32[]{:S(2)}) async-start(), calls=%async_computation.1 | async-start | bytes 8912896 | tf_op jit(solution)/shard_map/all_gather | solution.py:169
  8.0 7.0 %copy-start.7 = (pred[128]{0:T(512)(128)(4,1)}, pred[128]{0:T(512)(128)(4,1)S(1)}, u32[]{:S(2)}) copy-start(pred[128]{0:T(512)(128)(4,1)S(1)} %iota_compare_fusion.1) | copy-start | bytes 388
  11.4 394.5 %reduce-scatter.2.cloned.1.call-start = ((), (), s32[]{:S(2)}) async-start(), calls=%async_computation.2 | async-start | bytes 8912896 | tf_op jit(solution)/shard_map/reduce_scatter | solution.py:183
  11.5 3.5 copy-start.4
  11.5 3.5 copy-start.5
  306.7 4.9 %copy-start.3 = (bf16[8,2048,128]{2,1,0:T(8,128)(2,1)S(1)}, bf16[8,2048,128]{2,1,0:T(8,128)(2,1)}, u32[]{:S(2)}) copy-start(bf16[8,2048,128]{2,1,0:T(8,128)(2,1)} %get-tuple-element.126) | copy-start | bytes 12582916
  322.3 0.7 copy-start.6
  323.0 4.5 %copy-start.8 = (pred[128]{0:T(512)(128)(4,1)S(1)}, pred[128]{0:T(512)(128)(4,1)}, u32[]{:S(2)}) copy-start(pred[128]{0:T(512)(128)(4,1)} %copy-done.7) | copy-start | bytes 388
  327.5 7.8 %copy-start.2 = (bf16[8,128,8,128]{3,1,2,0:T(8,128)(2,1)S(1)}, bf16[8,128,8,128]{3,1,2,0:T(8,128)(2,1)}, u32[]{:S(2)}) copy-start(bf16[8,128,8,128]{3,1,2,0:T(8,128)(2,1)} %get-tuple-element.125) | copy-start | bytes 6291460
  331.4 26.9 %collective-permute-start = (bf16[128,8192]{1,0:T(8,128)(2,1)}, bf16[128,8192]{1,0:T(8,128)(2,1)}, u32[]{:S(2)}, u32[]{:S(2)}) collective-permute-start(bf16[128,8192]{1,0:T(8,128)(2,1)} %fusion.49), channel_id=1, source_target_pairs={{0,16},{16,32},{32,48},{48,64},{64,80},{80,96},{96,112},{1,17},{17... | collective-permute-start | bytes 6291464 | tf_op jit(solution)/shard_map/ppermute | solution.py:16
  405.9 6.9 %copy-start.1 = (bf16[1,128,8192]{2,1,0:T(8,128)(2,1)S(1)}, bf16[1,128,8192]{2,1,0:T(8,128)(2,1)}, u32[]{:S(2)}) copy-start(bf16[1,128,8192]{2,1,0:T(8,128)(2,1)} %param.12) | copy-start | bytes 6291460
Sparse Core Ops, SparseCore 0:
  11.5 74.0 all-gather.2
  322.5 83.3 reduce-scatter.1
where the time goes:
time: 422 us; the launch traced here: 420 us
  matrix products  187 us (44%)
  waiting for transfers between devices  99.7 us (24%)
  other arithmetic  46.9 us (11%)
  local copies, waits for them, and re-layouts  46.1 us (11%)
  blocking collectives  20.1 us (5%)
  between operations  15.1 us (4%)
    dot_general x16, matrix products, masked_scores(): jnp.einsum('qih,kh->qik', query_group, key_group, preferred_element_type=...  51.6 us
    reduce_scatter x1, waiting for transfers between devices, body(): lax.psum_scatter(pair_term.astype(jnp.bfloat16), 'ctx', scatter_dimension...  47.5 us
    all_gather x1, waiting for transfers between devices, body(): lax.all_gather(own_pairs, 'ctx', axis=0, tiled=True)  39.1 us
    dot_general x8, matrix products, attend_group(): jnp.einsum('qik,kh->qih', prob_b, value_group, preferred_element_type=jnp...  33.7 us
    dot_general x8, matrix products, both_grads(): jnp.einsum('qik,qih->kh', prob_b, out_grad, preferred_element_type=jnp.fl...  24.8 us
    dot_general x8, matrix products, both_grads(): jnp.einsum('qik,qih->kh', score_grad, query_group, preferred_element_type...  24.8 us
    dot_general x8, matrix products, both_grads(): jnp.einsum('qik,kh->qih', score_grad, key_group, preferred_element_type=j...  24.1 us
    all_gather x1, blocking collectives, body(): lax.all_gather(position, 'ctx', axis=0, tiled=True)  20.1 us
  transfers between devices with their start and end apart: 3, of which 3 were waited for; matrix products, arithmetic and copies ran while one was open for 8% of the time, Pallas kernels for 0%

commit v1 on v0

v1 whole, which is shorter than its diff:
```python
import functools, math
import jax, jax.numpy as jnp
from jax import lax
from jax.experimental import pallas as pl
from jax.experimental.pallas import tpu as pltpu
from jax.sharding import PartitionSpec as P

HEAD = 128
GROUP = 8
ROWS = 128
SLOTS = 32
BLOCKS = 16
CHUNK = 512
TILE = 512
SCALE = HEAD ** -0.5
LOG2E = math.log2(math.e)
BF = jnp.bfloat16
F32 = jnp.float32


def dot(a, b):
    return jnp.dot(a, b, preferred_element_type=F32)


def fold(x, op):
    return op(x.reshape(x.shape[0] // 8, 8, x.shape[1]), axis=0)


def block_pass(q, g, width, k_ref, v_ref, kt_ref, vt_ref, dk_ref, dv_ref, chunks, full, mask_of, scr):
    qs, gs, qt, gt, s_scr, e_scr, m_scr, l_scr, acc, dqa = scr
    cols = width * GROUP
    for h in range(GROUP):
        qh, gh = q[:, h * HEAD:(h + 1) * HEAD], g[:, h * HEAD:(h + 1) * HEAD]
        rows = slice(h * width, (h + 1) * width)
        qs[rows, :] = qh
        gs[rows, :] = gh
    for t in range(cols // 128):
        rows = slice(t * 128, (t + 1) * 128)
        qt[:, rows] = qs[rows, :].T
        gt[:, rows] = gs[rows, :].T
    tile = min(TILE, cols)
    tiles = [slice(t, t + tile) for t in range(0, cols, tile)]
    m_scr[:, :cols] = jnp.full((8, cols), -1e30, F32)
    l_scr[:, :cols] = jnp.zeros((8, cols), F32)
    acc[:, :cols] = jnp.zeros((HEAD, cols), F32)
    dqa[:, :cols] = jnp.zeros((HEAD, cols), F32)

    def at(c):
        return pl.ds(pl.multiple_of(c * CHUNK, CHUNK), CHUNK)

    def score(c, masked):
        k = k_ref[at(c), :]
        for t in tiles:
            s = dot(k, qt[:, t])
            if masked:
                s = jnp.where(mask_of(c), s, -1e30)
            s_scr[at(c), t] = s
            m_scr[:, t] = jnp.maximum(m_scr[:, t], fold(s, jnp.max))

    def loop(fn):
        lax.fori_loop(0, chunks, lambda c, z: (fn(c), z)[1], 0)

    lax.fori_loop(0, full, lambda c, z: (score(c, False), z)[1], 0)
    lax.fori_loop(full, chunks, lambda c, z: (score(c, True), z)[1], 0)
    top = jnp.max(m_scr[:, :cols], axis=0, keepdims=True) * (SCALE * LOG2E)
    m_scr[:, :cols] = jnp.broadcast_to(top, (8, cols))

    def weigh(c):
        for t in tiles:
            e = jnp.exp2(s_scr[at(c), t] * (SCALE * LOG2E) - m_scr[0:1, t])
            l_scr[:, t] += fold(e, jnp.sum)
            eb = e.astype(BF)
            e_scr[at(c), t] = eb
            acc[:, t] += dot(vt_ref[c], eb)

    loop(weigh)
    inv = 1.0 / jnp.sum(l_scr[:, :cols], axis=0, keepdims=True)
    attn_t = acc[:, :cols] * inv
    acc[:, :cols] = attn_t
    delta = jnp.sum(attn_t * gt[:, :cols].astype(F32), axis=0, keepdims=True)
    l_scr[:, :cols] = jnp.broadcast_to(inv, (8, cols))
    m_scr[:, :cols] = jnp.broadcast_to(delta, (8, cols))

    def back(c):
        v = v_ref[at(c), :]
        dk = dk_ref[at(c), :]
        dv = dv_ref[at(c), :]
        for t in tiles:
            dp = dot(v, gt[:, t])
            p = e_scr[at(c), t].astype(F32) * l_scr[0:1, t]
            ds = (p * (dp - m_scr[0:1, t])).astype(BF)
            dv += dot(p.astype(BF), gs[t, :])
            dk += dot(ds, qs[t, :])
            dqa[:, t] += dot(kt_ref[c], ds)
        dk_ref[at(c), :] = dk
        dv_ref[at(c), :] = dv

    loop(back)


def emit(src, width, scale, out, row, col):
    for t in range(width * GROUP // 128):
        x = (src[:, t * 128:(t + 1) * 128] * scale).T.astype(BF)
        per = 128 // width
        for i in range(per):
            h = t * per + i
            out[row:row + width, col + h * HEAD:col + (h + 1) * HEAD] = x[i * width:(i + 1) * width, :]


def scratch(cols):
    return [
        pltpu.VMEM((cols, HEAD), BF), pltpu.VMEM((cols, HEAD), BF),
        pltpu.VMEM((HEAD, cols), BF), pltpu.VMEM((HEAD, cols), BF),
        pltpu.VMEM((BLOCKS * ROWS, cols), F32), pltpu.VMEM((BLOCKS * ROWS, cols), BF),
        pltpu.VMEM((8, cols), F32), pltpu.VMEM((8, cols), F32),
        pltpu.VMEM((HEAD, cols), F32), pltpu.VMEM((HEAD, cols), F32),
    ]


def chooser(sel):
    return (lax.broadcasted_iota(jnp.int32, (ROWS, ROWS), 0) == sel[0:1, :]).astype(F32)


def compact(sel):
    return chooser(sel).T[:SLOTS, :].astype(BF)


HALF = GROUP * HEAD
QG = 2 * HALF
KV = 2 * HEAD
DENSE = BLOCKS * ROWS
FEW = BLOCKS * SLOTS
SENT = ROWS + SLOTS
COUNT = 16
MARKED = SENT + COUNT
VMEM = pl.BlockSpec(memory_space=pltpu.VMEM)
SMEM = pl.BlockSpec(memory_space=pltpu.SMEM)
WHOLE = pltpu.CompilerParams(vmem_limit_bytes=60 << 20)
PARAMS = pltpu.CompilerParams(vmem_limit_bytes=20 << 20)
ANY = pl.BlockSpec(memory_space=pl.ANY)
SEL = pl.BlockSpec((1, ROWS), lambda i, info: (0, 0))


def pack_kernel(wide, info, a, b, a_in, b_in, sel, sel_in, *outs):
    def fill(out, dense, few, few_sel):
        pick = compact(few_sel)
        for side in range(2):
            cols = slice(side * wide, (side + 1) * wide)
            out[:ROWS, cols] = dense[side][...]
            out[ROWS:SENT, cols] = dot(pick, few[side][...]).astype(BF)
        if out.shape[0] > SENT:
            count = jnp.sum((few_sel[0:1, :] >= 0).astype(F32), axis=1, keepdims=True)
            out[SENT:, :] = jnp.broadcast_to(count, (COUNT, 2 * wide)).astype(BF)

    for step, out in enumerate(outs):
        @pl.when(pl.program_id(0) == step)
        def _(out=out):
            @pl.when(info[0] == 1)
            def _():
                fill(out, (a, b), (a_in, b_in), sel_in)

            @pl.when(info[0] == 0)
            def _():
                fill(out, (a_in, b_in), (a, b), sel)


def pack(wide, rows, info, a, b, a_in, b_in, sel, sel_in):
    part = pl.BlockSpec((ROWS, wide), lambda i, info: (0, 2 * lax.rem(info[1] + i, 4) + info[0]))
    return list(pl.pallas_call(
        functools.partial(pack_kernel, wide),
        grid_spec=pltpu.PrefetchScalarGridSpec(
            num_scalar_prefetch=1,
            grid=(4,),
            in_specs=[part] * 4 + [SEL] * 2,
            out_specs=[pl.BlockSpec((rows, 2 * wide), lambda i, info: (0, 0))] * 4,
        ),
        out_shape=[jax.ShapeDtypeStruct((rows, 2 * wide), BF)] * 4,
        compiler_params=WHOLE,
        name="pack",
    )(info, a, b, a_in, b_in, sel, sel_in))


ATTEND = pltpu.CompilerParams(vmem_limit_bytes=32 << 20)
KEYED = [((DENSE, HEAD), BF)] * 2 + [((DENSE // CHUNK, HEAD, CHUNK), BF)] * 2
KEYED += [((FEW, HEAD), BF)] * 2 + [((FEW // CHUNK, HEAD, CHUNK), BF)] * 2 + [((FEW, HEAD), F32)]
SUMS = [((DENSE, HEAD), F32)] * 2 + [((FEW, HEAD), F32)] * 2


def cost(blocks):
    return pl.CostEstimate(flops=blocks * 9 * 10 ** 9, bytes_accessed=6 << 20, transcendentals=0)


def arrange(info, kvs, keyed):
    kd, vd, ktd, vtd, kr, vr, ktr, vtr, flags = keyed
    slot = lax.broadcasted_iota(jnp.int32, (SLOTS, HEAD), 0).astype(F32)
    for ky, kv in enumerate(kvs):
        for kz in range(4):
            b = 4 * lax.rem(info[1] + 4 - kz, 4) + lax.rem(info[2] + 4 - ky, 4)
            big = pl.ds(pl.multiple_of(b * ROWS, ROWS), ROWS)
            small = pl.ds(pl.multiple_of(b * SLOTS, SLOTS), SLOTS)
            kd[big, :] = kv[kz, :ROWS, :HEAD]
            vd[big, :] = kv[kz, :ROWS, HEAD:]
            kr[small, :] = kv[kz, ROWS:SENT, :HEAD]
            vr[small, :] = kv[kz, ROWS:SENT, HEAD:]
            flags[small, :] = (slot < kv[kz, SENT:, :HEAD].astype(F32)[0:1, :]).astype(F32)
    for k, v, kt, vt in ((kd, vd, ktd, vtd), (kr, vr, ktr, vtr)):
        for c in range(kt.shape[0]):
            rows = slice(c * CHUNK, (c + 1) * CHUNK)
            kt[c] = k[rows, :].T
            vt[c] = v[rows, :].T


def attend_block(info, shift, qg, keyed, sums, out, scr):
    kd, vd, ktd, vtd, kr, vr, ktr, vtr, flags = keyed
    per = CHUNK // ROWS
    blk = 4 * lax.rem(info[1] + 4 - shift, 4) + info[2]
    chunks = lax.div(blk + per, per)

    def place(cols):
        shape = (CHUNK, cols)
        return lax.broadcasted_iota(jnp.int32, shape, 0), lax.broadcasted_iota(jnp.int32, shape, 1)

    def causal(c):
        row, col = place(TILE)
        return c * CHUNK + row <= blk * ROWS + lax.rem(col, ROWS)

    def routed(c):
        cols = SLOTS * GROUP
        row, col = place(cols)
        near = c * CHUNK + row <= blk * SLOTS + lax.rem(col, SLOTS)
        held = flags[pl.ds(pl.multiple_of(c * CHUNK, CHUNK), CHUNK), :]
        return near & (jnp.concatenate([held] * (cols // HEAD), axis=1) > 0.5)

    block_pass(qg[:ROWS, :HALF], qg[:ROWS, HALF:], ROWS, kd, vd, ktd, vtd, sums[0], sums[1],
               chunks, chunks - 1, causal, scr)
    emit(scr[8], ROWS, 1.0, out, 0, 0)
    emit(scr[9], ROWS, SCALE, out, 0, HALF)
    block_pass(qg[ROWS:, :HALF], qg[ROWS:, HALF:], SLOTS, kr, vr, ktr, vtr, sums[2], sums[3],
               FEW // CHUNK, 0, routed, scr)
    emit(scr[8], SLOTS, 1.0, out, ROWS, 0)
    emit(scr[9], SLOTS, SCALE, out, ROWS, HALF)


def first_kernel(info, qg, kv0, kv1, kv2, kv3, out, *refs):
    keyed, sums, scr = refs[:9], refs[9:13], refs[13:]
    arrange(info, (kv0, kv1, kv2, kv3), keyed)
    for total in sums:
        total[...] = jnp.zeros_like(total)
    attend_block(info, 0, qg, keyed, sums, out, scr)


def attend_first(info, qg, kvs):
    shapes = [((SENT, QG), BF)] + KEYED + SUMS
    outs = pl.pallas_call(
        first_kernel,
        out_shape=[jax.ShapeDtypeStruct(s, d) for s, d in shapes],
        in_specs=[SMEM] + [VMEM] * 5,
        out_specs=[VMEM] * len(shapes),
        scratch_shapes=scratch(HALF),
        compiler_params=ATTEND,
        cost_estimate=cost(1),
        name="attend_first",
    )(info, qg, *kvs)
    return outs[0], outs[1:10], outs[10:]


def middle_kernel(shifts, info, *refs):
    n = len(shifts)
    qgs, refs = refs[:n], refs[n:]
    keyed, sums_in, refs = refs[:9], refs[9:13], refs[13:]
    outs, sums, scr = refs[:n], refs[n:n + 4], refs[n + 4:]
    for total, come in zip(sums, sums_in):
        total[...] = come[...]
    for shift, qg, out in zip(shifts, qgs, outs):
        attend_block(info, shift, qg, keyed, sums, out, scr)


def attend_middle(shifts, info, qgs, keyed, sums):
    n = len(shifts)
    shapes = [((SENT, QG), BF)] * n + SUMS
    outs = pl.pallas_call(
        functools.partial(middle_kernel, shifts),
        out_shape=[jax.ShapeDtypeStruct(s, d) for s, d in shapes],
        in_specs=[SMEM] + [VMEM] * (n + 13),
        out_specs=[VMEM] * len(shapes),
        scratch_shapes=scratch(HALF),
        input_output_aliases={n + 10 + i: n + i for i in range(4)},
        compiler_params=ATTEND,
        cost_estimate=cost(n),
        name="attend_middle",
    )(info, *qgs, *keyed, *sums)
    return outs[:n], outs[n:]


def last_kernel(shift, info, qg, *refs):
    keyed, sums_in, refs = refs[:9], refs[9:13], refs[13:]
    out, sent, sums, scr = refs[0], refs[1:5], refs[5:9], refs[9:]
    for total, come in zip(sums, sums_in):
        total[...] = come[...]
    attend_block(info, shift, qg, keyed, sums, out, scr)
    for ky in range(4):
        for kz in range(4):
            b = 4 * lax.rem(info[1] + kz, 4) + lax.rem(info[2] + ky, 4)
            big = pl.ds(pl.multiple_of(b * ROWS, ROWS), ROWS)
            small = pl.ds(pl.multiple_of(b * SLOTS, SLOTS), SLOTS)
            sent[ky][kz, :ROWS, :HEAD] = (sums[0][big, :] * SCALE).astype(BF)
            sent[ky][kz, :ROWS, HEAD:] = sums[1][big, :].astype(BF)
            sent[ky][kz, ROWS:, :HEAD] = (sums[2][small, :] * SCALE).astype(BF)
            sent[ky][kz, ROWS:, HEAD:] = sums[3][small, :].astype(BF)


def attend_last(shift, info, qg, keyed, sums):
    shapes = [(SENT, QG)] + [(4, SENT, KV)] * 4
    outs = pl.pallas_call(
        functools.partial(last_kernel, shift),
        out_shape=[jax.ShapeDtypeStruct(s, BF) for s in shapes],
        in_specs=[SMEM] + [VMEM] * 14,
        out_specs=[VMEM] * len(shapes),
        scratch_shapes=[pltpu.VMEM(s, d) for s, d in SUMS] + scratch(HALF),
        compiler_params=ATTEND,
        cost_estimate=cost(1),
        name="attend_last",
    )(info, qg, *keyed, *sums)
    return outs[0], list(outs[1:])


def fold_kernel(a, b, c, d, *outs):
    for i, out in enumerate(outs):
        total = a[i].astype(F32) + b[i].astype(F32) + c[i].astype(F32) + d[i].astype(F32)
        out[...] = total.astype(BF)


def fold_sums(parts):
    return list(pl.pallas_call(
        fold_kernel,
        out_shape=[jax.ShapeDtypeStruct((SENT, KV), BF)] * 4,
        in_specs=[VMEM] * 4,
        out_specs=[VMEM] * 4,
        compiler_params=PARAMS,
        name="fold_sums",
    )(*parts))


def heads_of(info, sel, mine, theirs, put):
    @pl.when(info[0] == 1)
    def _():
        put(0, theirs[0, :ROWS, :].astype(F32))
        put(1, mine[0, :ROWS, :].astype(F32))

    @pl.when(info[0] == 0)
    def _():
        pick = chooser(sel)[:, :SLOTS].astype(BF)
        put(0, dot(pick, mine[0, ROWS:, :]))
        put(1, dot(pick, theirs[0, ROWS:, :]))


def update_kernel(info, seg, mine, theirs, sel, out):
    def put(i, x):
        cols = slice(i * HALF, (i + 1) * HALF)
        out[0, :, cols] = (seg[:, cols].astype(F32) + x).astype(BF)

    heads_of(info, sel, mine, theirs, put)


def turner(shifts):
    def turn(i, info):
        shift = shifts[0]
        for j in range(1, len(shifts)):
            shift = jnp.where(i == j, shifts[j], shift)
        return lax.rem(info[1] + shift, 4)

    return turn


def update(shifts, info, seg, mine, theirs, sel):
    turn = turner(shifts)
    part = pl.BlockSpec((1, SENT, HALF), lambda i, info: (i, 0, 0))
    return pl.pallas_call(
        update_kernel,
        grid_spec=pltpu.PrefetchScalarGridSpec(
            num_scalar_prefetch=1,
            grid=(len(shifts),),
            in_specs=[pl.BlockSpec((ROWS, 2 * HALF), lambda i, info: (0, turn(i, info))), part, part, SEL],
            out_specs=pl.BlockSpec((1, ROWS, 2 * HALF), lambda i, info: (i, 0, 0)),
        ),
        out_shape=jax.ShapeDtypeStruct((len(shifts), ROWS, 2 * HALF), BF),
        compiler_params=PARAMS,
        name="update",
    )(info, seg, mine, theirs, sel)


def finish_kernel(info, near, near_in, far, far_in, sums, sums_in, sel, dq, dk, dv):
    def put_q(i, x):
        dq[:, i * HALF:(i + 1) * HALF] = x.astype(BF)

    def put_kv(i, x):
        x = x.astype(BF)
        dk[:, i * HEAD:(i + 1) * HEAD] = x[:, :HEAD]
        dv[:, i * HEAD:(i + 1) * HEAD] = x[:, HEAD:]

    @pl.when(pl.program_id(0) < 3)
    def _():
        heads_of(info, sel, near, near_in, put_q)

    @pl.when(pl.program_id(0) == 3)
    def _():
        heads_of(info, sel, far, far_in, put_q)

    heads_of(info, sel, sums, sums_in, put_kv)


def finish(info, near, near_in, far, far_in, sums, sums_in, sel):
    turn = turner((0, 1, 3, 2))

    def head(i, info):
        return (0, turn(i, info))

    def back(i, info):
        return (lax.rem(4 - turner((0, 1, 3, 2))(i, (0, 0)), 4), 0, 0)

    one = pl.BlockSpec((1, SENT, HALF), lambda i, info: (jnp.minimum(i, 2), 0, 1))
    two = pl.BlockSpec((1, SENT, HALF), lambda i, info: (0, 0, 1))
    tally = pl.BlockSpec((1, SENT, KV), back)
    return pl.pallas_call(
        finish_kernel,
        grid_spec=pltpu.PrefetchScalarGridSpec(
            num_scalar_prefetch=1,
            grid=(4,),
            in_specs=[one, one, two, two, tally, tally, SEL],
            out_specs=[
                pl.BlockSpec((ROWS, 2 * HALF), head),
                pl.BlockSpec((ROWS, 2 * HEAD), head),
                pl.BlockSpec((ROWS, 2 * HEAD), head),
            ],
        ),
        out_shape=[
            jax.ShapeDtypeStruct((ROWS, 8 * HALF), BF),
            jax.ShapeDtypeStruct((ROWS, 8 * HEAD), BF),
            jax.ShapeDtypeStruct((ROWS, 8 * HEAD), BF),
        ],
        compiler_params=PARAMS,
        name="finish",
    )(info, near, near_in, far, far_in, sums, sums_in, sel)


def join_kernel(info, near, far, out):
    out[...] = jnp.where(pl.program_id(0) == 3, far[0], near[0])


def join(info, near, far):
    def head(i, info):
        shift = jnp.where(i == 3, 2, jnp.where(i == 2, 3, i))
        return (0, lax.rem(info[1] + shift, 4))

    return pl.pallas_call(
        join_kernel,
        grid_spec=pltpu.PrefetchScalarGridSpec(
            num_scalar_prefetch=1,
            grid=(4,),
            in_specs=[
                pl.BlockSpec((1, ROWS, 2 * HALF), lambda i, info: (jnp.minimum(i, 2), 0, 0)),
                pl.BlockSpec((1, ROWS, 2 * HALF), lambda i, info: (0, 0, 0)),
            ],
            out_specs=pl.BlockSpec((ROWS, 2 * HALF), head),
        ),
        out_shape=jax.ShapeDtypeStruct((ROWS, 8 * HALF), BF),
        compiler_params=PARAMS,
        name="join",
    )(info, near, far)


def along_z(x, by):
    return lax.ppermute(x, "ctx", [(4 * z + y, 4 * ((z + by) % 4) + y) for z in range(4) for y in range(4)])


def along_y(x, by):
    return lax.ppermute(x, "ctx", [(4 * z + y, 4 * z + (y + by) % 4) for z in range(4) for y in range(4)])


def swap(x):
    return lax.ppermute(x, "section", [(i, i ^ 1) for i in range(8)])


def onward(x):
    return lax.ppermute(x, "section", [(i, i + 1) for i in range(7)])


def both(*xs):
    return lax.optimization_barrier(xs)


def body(segment_input, queries, keys, values, cotangent, selected, counts):
    section, place = lax.axis_index("section"), lax.axis_index("ctx")
    info = jnp.stack([section % 2, place // 4, place % 4]).astype(jnp.int32)
    seg, q, k, v, g = (x[0] for x in (segment_input, queries, keys, values, cotangent))
    sel = jnp.where(jnp.arange(ROWS, dtype=jnp.int32)[None, :] < counts, selected, -1)

    sel_in = swap(sel)
    kv = pack(HEAD, MARKED, info, k, v, swap(k), swap(v), sel, sel_in)
    for by in (1, 3, 2):
        kv[by] = along_z(kv[by], by)
    column = jnp.stack(kv)
    kvs = [column] + [along_y(column, by) for by in (1, 2, 3)]
    qg = pack(HALF, SENT, info, q, g, swap(q), swap(g), sel, sel_in)
    qg[1], qg[2], qg[3], _ = both(qg[1], qg[2], qg[3], column)
    for by in (1, 3, 2):
        qg[by] = along_z(qg[by], by)

    out = [None] * 4
    out[0], keyed, sums = attend_first(info, qg[0], kvs)
    (out[1], out[3]), sums = attend_middle((1, 3), info, [qg[1], qg[3]], keyed, sums)
    out[2], sent = attend_last(2, info, qg[2], keyed, sums)
    for by in (1, 3):
        out[by] = along_z(out[by], 4 - by)
    out[1], out[3], out[2] = both(out[1], out[3], out[2])
    out[2] = along_z(out[2], 2)
    sums = fold_sums([sent[0]] + [along_y(sent[by], by) for by in (1, 2, 3)])
    out[2], sums[0], sums[1], sums[2], sums[3] = both(out[2], *sums)

    near = jnp.stack([out[0], out[1], out[3]])
    near_in = swap(near)
    first = update((0, 1, 3), info, seg, near, near_in, sel)
    far = out[2][None]
    far_in = swap(far)
    second = update((2,), info, seg, far, far_in, sel)
    next_input = join(info, onward(first), onward(second))

    sums = jnp.stack([sums[0]] + [along_z(sums[by], by) for by in (1, 2, 3)])
    grads = finish(info, near, near_in, far, far_in, sums, swap(sums), sel)
    return (next_input[None],) + tuple(x[None] for x in grads)


def solution(mesh):
    wide, thin = P("section", "ctx", None), P("section", "ctx")
    return jax.shard_map(
        body,
        mesh=mesh,
        in_specs=(wide,) * 5 + (thin,) * 2,
        out_specs=(wide,) * 4,
        check_vma=False,
    )
```

time: 422 us -> 140 us (0.33)
  matrix products: 187 us -> 0 us
  waiting for transfers between devices: 99.7 us -> 38.6 us
  Pallas kernels: 0 us -> 47.2 us
  other arithmetic: 46.9 us -> 2.45 us
  local copies, waits for them, and re-layouts: 46.1 us -> 3.12 us
  starting transfers between devices: 3.99 us -> 46.3 us
  blocking collectives: 20.1 us -> 0 us
  between operations: 15.1 us -> 1.46 us
    dot_general x61 -> x0, matrix products: 187 us -> none  [the longest x16 51.6 us: masked_scores(): jnp.einsum('qih,kh->qik', query_group, key_group, preferred_element_type=...]
    reduce_scatter x1 -> x0, waiting for transfers between devices: 47.5 us -> none  [body(): lax.psum_scatter(pair_term.astype(jnp.bfloat16), 'ctx', scatter_dimension...]
    pallas_call x0 -> x10, Pallas kernels: none -> 47.2 us  [the longest x1 16.9 us: attend_middle(): pl.pallas_call(functools.partial(middle_kernel, shifts), out_shape=[jax.S...]
    ppermute x1 -> x28, starting transfers between devices: 3.91 us -> 46.3 us  [the longest x12 15.3 us: along_z(): lax.ppermute(x, 'ctx', [(4 * z + y, 4 * ((z + by) % 4) + y) for z in rang...]
    all_gather x1 -> x0, waiting for transfers between devices: 39.1 us -> none  [body(): lax.all_gather(own_pairs, 'ctx', axis=0, tiled=True)]
    reduce_sum x16 -> x0, other arithmetic: 28.1 us -> none  [the longest x8 17.6 us: attend_group(): totals = jnp.sum(weights, axis=-1, keepdims=True)]
    ppermute x1 -> x28, waiting for transfers between devices: 13 us -> 38.6 us  [the longest x6 22.1 us: along_y(): lax.ppermute(x, 'ctx', [(4 * z + y, 4 * z + (y + by) % 4) for z in range(...]
    all_gather x1 -> x0, blocking collectives: 20.1 us -> none  [body(): lax.all_gather(position, 'ctx', axis=0, tiled=True)]
  transfers between devices with their start and end apart: 3 -> 28, of which waited for: 3 -> 13; matrix products, arithmetic and copies ran while one was open for 8% -> 2% of each run, Pallas kernels for 0% -> 32%
where the time goes in v1:
time: 140 us; the launch traced here: 139 us
  Pallas kernels  47.2 us (34%)
  starting transfers between devices  46.3 us (33%)
  waiting for transfers between devices  38.6 us (28%)
  local copies, waits for them, and re-layouts  3.12 us (2%)
  other arithmetic  2.45 us (2%)
  between operations  1.46 us (1%)
    ppermute x6, waiting for transfers between devices, along_y(): lax.ppermute(x, 'ctx', [(4 * z + y, 4 * z + (y + by) % 4) for z in range(...  22.1 us
    pallas_call x1, Pallas kernels, attend_middle(): pl.pallas_call(functools.partial(middle_kernel, shifts), out_shape=[jax.S...  16.9 us
    ppermute x12, starting transfers between devices, along_z(): lax.ppermute(x, 'ctx', [(4 * z + y, 4 * ((z + by) % 4) + y) for z in rang...  15.3 us
    ppermute x8, starting transfers between devices, swap(): return lax.ppermute(x, 'section', [(i, i ^ 1) for i in range(8)])  14.6 us
    ppermute x8, waiting for transfers between devices, swap(): return lax.ppermute(x, 'section', [(i, i ^ 1) for i in range(8)])  9.46 us
    pallas_call x2, Pallas kernels, pack(): pl.pallas_call(functools.partial(pack_kernel, wide), grid_spec=pltpu.Pref...  9.17 us
    pallas_call x1, Pallas kernels, attend_last(): pl.pallas_call(functools.partial(last_kernel, shift), out_shape=[jax.Shap...  8.87 us
    ppermute x2, starting transfers between devices, onward(): return lax.ppermute(x, 'section', [(i, i + 1) for i in range(7)])  8.37 us
  transfers between devices with their start and end apart: 28, of which 13 were waited for; matrix products, arithmetic and copies ran while one was open for 2% of the time, Pallas kernels for 32%

profile of v1, /device:TPU:1, one launch (start us, length us, event | category | flops | bytes accessed | tf_op | source)
XLA Modules:
  0.0 139.2 jit_solution(2135033888584377921)
XLA Ops:
  0.6 1.5 %collective-permute-start = (bf16[128,8192]{1,0:T(8,128)(2,1)}, bf16[128,8192]{1,0:T(8,128)(2,1)S(1)}, u32[]{:S(2)}, u32[]{:S(2)}) collective-permute-start(bf16[128,8192]{1,0:T(8,128)(2,1)} %bitcast.33), channel_id=1, source_target_pairs={{0,16},{16,0},{32,48},{48,32},{64,80},{80,64},{96,112},{112,96},{1... | collective-permute-start | bytes 6291464 | tf_op jit(solution)/shard_map/ppermute | solution.py:481
  2.1 0.1 collective-permute-start.1
  2.2 0.4 collective-permute-start.3
  2.6 0.1 collective-permute-start.4
  3.4 0.7 compare_select_fusion.sel
  4.1 0.4 collective-permute-start.2
  4.5 0.6 pad_add_fusion.info
  5.1 2.9 %collective-permute-done.2.sel_in = s32[1,128]{1,0:T(1,128)S(1)} collective-permute-done((s32[1,128]{1,0:T(1,128)S(1)}, s32[1,128]{1,0:T(1,128)S(1)}, u32[]{:S(2)}, u32[]{:S(2)}) %collective-permute-start.2) | collective-permute-done | bytes 544 | tf_op jit(solution)/shard_map/ppermute | solution.py:481
  8.0 1.0 collective-permute-done.3.a_in
  8.9 0.7 collective-permute-done.4.b_in
  9.7 0.7 copy-done.7
  10.4 3.6 %pack.3 = (bf16[176,256]{1,0:T(8,128)(2,1)}, bf16[176,256]{1,0:T(8,128)(2,1)}, bf16[176,256]{1,0:T(8,128)(2,1)}, bf16[176,256]{1,0:T(8,128)(2,1)}) custom-call(s32[3]{0:T(128)} %pad_add_fusion.info, bf16[128,1024]{1,0:T(8,128)(2,1)} %bitcast.41, bf16[128,1024]{1,0:T(8,128)(2,1)} %bitcast.43, bf16[128,1024]{1,0:T(8,128)(2,1)} %copy-done.6, ...), custom_call_target="tpu_custom_call" | custom-call | tf_op jit(solution)/shard_map/pack/pallas_call | solution.py:169
  14.0 1.7 %collective-permute-start.5 = (bf16[176,256]{1,0:T(8,128)(2,1)}, bf16[176,256]{1,0:T(8,128)(2,1)S(1)}, u32[]{:S(2)}, u32[]{:S(2)}) collective-permute-start(bf16[176,256]{1,0:T(8,128)(2,1)} %get-tuple-element.57), channel_id=1, source_target_pairs={{0,4},{1,5},{2,6},{3,7},{4,8},{5,9},{6,10},{7,11},{8,12},{9,13},{1... | collective-permute-start | bytes 270344 | tf_op jit(solution)/shard_map/ppermute | solution.py:473
  15.8 3.3 %collective-permute-start.6 = (bf16[176,256]{1,0:T(8,128)(2,1)}, bf16[176,256]{1,0:T(8,128)(2,1)S(1)}, u32[]{:S(2)}, u32[]{:S(2)}) collective-permute-start(bf16[176,256]{1,0:T(8,128)(2,1)} %get-tuple-element.58), channel_id=1, source_target_pairs={{0,8},{1,9},{2,10},{3,11},{4,12},{5,13},{6,14},{7,15},{8,0},{9,1},... | collective-permute-start | bytes 270344 | tf_op jit(solution)/shard_map/ppermute | solution.py:473
  19.1 0.7 collective-permute-start.7
  19.8 1.0 collective-permute-done.5
  20.8 2.8 %collective-permute-done.6 = bf16[176,256]{1,0:T(8,128)(2,1)S(1)} collective-permute-done((bf16[176,256]{1,0:T(8,128)(2,1)}, bf16[176,256]{1,0:T(8,128)(2,1)S(1)}, u32[]{:S(2)}, u32[]{:S(2)}) %collective-permute-start.6) | collective-permute-done | bytes 90144 | tf_op jit(solution)/shard_map/ppermute | solution.py:473
  23.6 0.9 pad_maximum_fusion.1.kv0
  24.5 2.8 %collective-permute-start.10 = (bf16[4,176,256]{2,1,0:T(8,128)(2,1)S(1)}, bf16[4,176,256]{2,1,0:T(8,128)(2,1)S(1)}, u32[]{:S(2)}, u32[]{:S(2)}) collective-permute-start(bf16[4,176,256]{2,1,0:T(8,128)(2,1)S(1)} %pad_maximum_fusion.1.kv0), channel_id=1, source_target_pairs={{0,3},{1,0},{2,1},{3,2},{4,7},{5,4},{6,5},{7,6},{8,11},{9,8},{10,9... | collective-permute-start | bytes 1081352 | tf_op jit(solution)/shard_map/ppermute | solution.py:477
  27.3 0.3 collective-permute-start.9
  27.7 0.7 collective-permute-start.8
  28.4 0.0 collective-permute-done.a_in
  28.4 0.0 collective-permute-done.1.b_in
  28.4 1.3 copy-done.5
  29.7 5.5 %pack.2 = (bf16[160,2048]{1,0:T(8,128)(2,1)}, bf16[160,2048]{1,0:T(8,128)(2,1)}, bf16[160,2048]{1,0:T(8,128)(2,1)}, bf16[160,2048]{1,0:T(8,128)(2,1)}) custom-call(s32[3]{0:T(128)} %pad_add_fusion.info, bf16[128,8192]{1,0:T(8,128)(2,1)} %bitcast.34, bf16[128,8192]{1,0:T(8,128)(2,1)} %bitcast.36, bf16[128,8192]{1,0:T(8,128)(2,1)} %copy-done.5, ...), custom_call_target="tpu_custom_call" | custom-call | tf_op jit(solution)/shard_map/pack/pallas_call | solution.py:169
  35.2 1.3 collective-permute-start.11
  36.5 1.4 collective-permute-start.12
  37.9 0.5 collective-permute-start.15
  38.4 0.0 collective-permute-done.9.kv2
  38.4 8.5 %collective-permute-done.8.kv1 = bf16[4,176,256]{2,1,0:T(8,128)(2,1)S(1)} collective-permute-done((bf16[4,176,256]{2,1,0:T(8,128)(2,1)S(1)}, bf16[4,176,256]{2,1,0:T(8,128)(2,1)S(1)}, u32[]{:S(2)}, u32[]{:S(2)}) %collective-permute-start.8) | collective-permute-done | bytes 360480 | tf_op jit(solution)/shard_map/ppermute | solution.py:477
  46.9 1.1 copy-done.4
  48.0 4.8 %attend_first.1 = (bf16[160,2048]{1,0:T(8,128)(2,1)S(1)}, bf16[2048,128]{1,0:T(8,128)(2,1)S(1)}, bf16[2048,128]{1,0:T(8,128)(2,1)S(1)}, bf16[4,128,512]{2,1,0:T(...) custom-call(s32[3]{0:T(128)S(1)} %copy-done.1, ...), custom_call_target="tpu_custom_call" | custom-call | flops 8999999488 | bytes 6291456 | tf_op jit(solution)/shard_map/attend_first/pallas_call | solution.py:254
  52.8 0.0 collective-permute-done.11.refs_0_
  52.8 0.0 collective-permute-done.12.refs_1_
  52.8 16.9 %attend_middle.1 = (bf16[160,2048]{1,0:T(8,128)(2,1)S(1)}, bf16[160,2048]{1,0:T(8,128)(2,1)S(1)}, f32[2048,128]{1,0:T(8,128)S(1)}, f32[2048,128]{1,0:T(8,128)S(1...) custom-call(s32[3]{0:T(128)S(1)} %copy-done.1, ...), custom_call_target="tpu_custom_call", output_to_operand_aliasing={{2}: (12, {}), {3}: (13, {}), {4}: (14, {}), {5}: (15, {})} | custom-call | flops 17999998976 | bytes 6291456 | tf_op jit(solution)/shard_map/attend_middle/pallas_call | solution.py:281
  69.7 3.7 %collective-permute-start.13 = (bf16[160,2048]{1,0:T(8,128)(2,1)S(1)}, bf16[160,2048]{1,0:T(8,128)(2,1)S(1)}, u32[]{:S(2)}, u32[]{:S(2)}) collective-permute-start(bf16[160,2048]{1,0:T(8,128)(2,1)S(1)} %get-tuple-element.79), channel_id=1, source_target_pairs={{0,12},{1,13},{2,14},{3,15},{4,0},{5,1},{6,2},{7,3},{8,4},{9,5},{1... | collective-permute-start | bytes 1966088 | tf_op jit(solution)/shard_map/ppermute | solution.py:473
  73.4 0.0 collective-permute-start.14
  73.4 0.0 collective-permute-done.15.qg
  73.4 8.9 %attend_last.1 = (bf16[160,2048]{1,0:T(8,128)(2,1)S(1)}, bf16[4,160,256]{2,1,0:T(8,128)(2,1)S(1)}, bf16[4,160,256]{2,1,0:T(8,128)(2,1)S(1)}, bf16[4,160,256]{2,1,0:T(8,128)(2,1)S(1)}, bf16[4,160,256]{2,1,0:T(8,128)(2,1)S(1)}) custom-call(s32[3]{0:T(128)S(1)} %copy-done.1, bf16[160,2048]{1,0:T(8,128)(2,1)S(1)} %collective-permute-done.15.qg, ...), custom_call_target="tpu_custom_call" | custom-call | flops 8999999488 | bytes 6291456 | tf_op jit(solution)/shard_map/attend_last/pallas_call | solution.py:314
  82.3 1.8 %collective-permute-done.14 = bf16[160,2048]{1,0:T(8,128)(2,1)S(1)} collective-permute-done((bf16[160,2048]{1,0:T(8,128)(2,1)S(1)}, bf16[160,2048]{1,0:T(8,128)(2,1)S(1)}, u32[]{:S(2)}, u32[]{:S(2)}) %collective-permute-start.14) | collective-permute-done | bytes 655392 | tf_op jit(solution)/shard_map/ppermute | solution.py:473
  84.1 0.2 pad_maximum_fusion.mine.near
  84.3 11.1 %collective-permute-start.16 = (bf16[3,160,2048]{2,1,0:T(8,128)(2,1)S(1)}, bf16[3,160,2048]{2,1,0:T(8,128)(2,1)S(1)}, u32[]{:S(2)}, u32[]{:S(2)}) collective-permute-start(bf16[3,160,2048]{2,1,0:T(8,128)(2,1)S(1)} %pad_maximum_fusion.mine.near), channel_id=1, source_target_pairs={{0,16},{16,0},{32,48},{48,32},{64,80},{80,64},{96,112},{112,96},{1... | collective-permute-start | bytes 5898248 | tf_op jit(solution)/shard_map/ppermute | solution.py:481
  95.4 3.6 %collective-permute-done.16.theirs.near_in = bf16[3,160,2048]{2,1,0:T(8,128)(2,1)S(1)} collective-permute-done((bf16[3,160,2048]{2,1,0:T(8,128)(2,1)S(1)}, bf16[3,160,2048]{2,1,0:T(8,128)(2,1)S(1)}, u32[]{:S(2)}, u32[]{:S(2)}) %collective-permute-start.16) | collective-permute-done | bytes 1966112 | tf_op jit(solution)/shard_map/ppermute | solution.py:481
  99.0 1.3 update.2
  100.4 3.8 %collective-permute-start.17 = (bf16[3,128,2048]{2,1,0:T(8,128)(2,1)S(1)}, bf16[3,128,2048]{2,1,0:T(8,128)(2,1)S(1)}, u32[]{:S(2)}, u32[]{:S(2)}) collective-permute-start(bf16[3,128,2048]{2,1,0:T(8,128)(2,1)S(1)} %update.2), channel_id=1, source_target_pairs={{0,16},{16,32},{32,48},{48,64},{64,80},{80,96},{96,112},{1,17},{17... | collective-permute-start | bytes 4718600 | tf_op jit(solution)/shard_map/ppermute | solution.py:485
  104.2 1.7 %collective-permute-start.19 = (bf16[4,160,256]{2,1,0:T(8,128)(2,1)S(1)}, bf16[4,160,256]{2,1,0:T(8,128)(2,1)S(1)}, u32[]{:S(2)}, u32[]{:S(2)}) collective-permute-start(bf16[4,160,256]{2,1,0:T(8,128)(2,1)S(1)} %get-tuple-element.91), channel_id=1, source_target_pairs={{0,1},{1,2},{2,3},{3,0},{4,5},{5,6},{6,7},{7,4},{8,9},{9,10},{10,1... | collective-permute-start | bytes 983048 | tf_op jit(solution)/shard_map/ppermute | solution.py:477
  105.9 1.6 %collective-permute-start.20 = (bf16[4,160,256]{2,1,0:T(8,128)(2,1)S(1)}, bf16[4,160,256]{2,1,0:T(8,128)(2,1)S(1)}, u32[]{:S(2)}, u32[]{:S(2)}) collective-permute-start(bf16[4,160,256]{2,1,0:T(8,128)(2,1)S(1)} %get-tuple-element.92), channel_id=1, source_target_pairs={{0,2},{1,3},{2,0},{3,1},{4,6},{5,7},{6,4},{7,5},{8,10},{9,11},{10,... | collective-permute-start | bytes 983048 | tf_op jit(solution)/shard_map/ppermute | solution.py:477
  107.4 0.9 collective-permute-start.21
  108.4 6.3 %collective-permute-done.19.b = bf16[4,160,256]{2,1,0:T(8,128)(2,1)S(1)} collective-permute-done((bf16[4,160,256]{2,1,0:T(8,128)(2,1)S(1)}, bf16[4,160,256]{2,1,0:T(8,128)(2,1)S(1)}, u32[]{:S(2)}, u32[]{:S(2)}) %collective-permute-start.19) | collective-permute-done | bytes 327712 | tf_op jit(solution)/shard_map/ppermute | solution.py:477
  114.7 6.9 %collective-permute-done.20.c = bf16[4,160,256]{2,1,0:T(8,128)(2,1)S(1)} collective-permute-done((bf16[4,160,256]{2,1,0:T(8,128)(2,1)S(1)}, bf16[4,160,256]{2,1,0:T(8,128)(2,1)S(1)}, u32[]{:S(2)}, u32[]{:S(2)}) %collective-permute-start.20) | collective-permute-done | bytes 327712 | tf_op jit(solution)/shard_map/ppermute | solution.py:477
  121.6 0.4 collective-permute-done.21.d
  122.0 0.2 fold_sums.1
  122.2 0.0 collective-permute-done.18
  122.2 0.5 collective-permute-start.22
  122.7 0.9 collective-permute-start.25
  123.6 1.8 %collective-permute-start.26 = (bf16[160,256]{1,0:T(8,128)(2,1)S(1)}, bf16[160,256]{1,0:T(8,128)(2,1)S(1)}, u32[]{:S(2)}, u32[]{:S(2)}) collective-permute-start(bf16[160,256]{1,0:T(8,128)(2,1)S(1)} %get-tuple-element.102), channel_id=1, source_target_pairs={{0,12},{1,13},{2,14},{3,15},{4,0},{5,1},{6,2},{7,3},{8,4},{9,5},{1... | collective-permute-start | bytes 245768 | tf_op jit(solution)/shard_map/ppermute | solution.py:473
  125.3 0.7 update.3
  126.1 4.6 %collective-permute-start.23 = (bf16[1,128,2048]{2,1,0:T(8,128)(2,1)S(1)}, bf16[1,128,2048]{2,1,0:T(8,128)(2,1)S(1)}, u32[]{:S(2)}, u32[]{:S(2)}) collective-permute-start(bf16[1,128,2048]{2,1,0:T(8,128)(2,1)S(1)} %update.3), channel_id=1, source_target_pairs={{0,16},{16,32},{32,48},{48,64},{64,80},{80,96},{96,112},{1,17},{17... | collective-permute-start | bytes 1572872 | tf_op jit(solution)/shard_map/ppermute | solution.py:485
  130.6 0.0 collective-permute-done.24
  130.7 0.5 collective-permute-start.27
  131.2 1.3 collective-permute-done.27.sums_in
  132.4 2.8 %finish.1 = (bf16[128,8192]{1,0:T(8,128)(2,1)}, bf16[128,1024]{1,0:T(8,128)(2,1)}, bf16[128,1024]{1,0:T(8,128)(2,1)}) custom-call(s32[3]{0:T(128)S(1)} %copy-done.1, bf16[3,160,2048]{2,1,0:T(8,128)(2,1)S(1)} %pad_maximum_fusion.mine.near, bf16[3,160,2048]{2,1,0:T(8,128)(2,1)S(1)} %collective-permute-done.16.theirs.near_in, ...), custom_call_target="tpu_custom_call" | custom-call | tf_op jit(solution)/shard_map/finish/pallas_call | solution.py:424
  135.3 1.5 %collective-permute-done.23.far = bf16[1,128,2048]{2,1,0:T(8,128)(2,1)S(1)} collective-permute-done((bf16[1,128,2048]{2,1,0:T(8,128)(2,1)S(1)}, bf16[1,128,2048]{2,1,0:T(8,128)(2,1)S(1)}, u32[]{:S(2)}, u32[]{:S(2)}) %collective-permute-start.23) | collective-permute-done | bytes 524320 | tf_op jit(solution)/shard_map/ppermute | solution.py:485
  136.8 2.4 %join.1 = bf16[128,8192]{1,0:T(8,128)(2,1)} custom-call(s32[3]{0:T(128)S(1)} %copy-done.1, bf16[3,128,2048]{2,1,0:T(8,128)(2,1)S(1)} %collective-permute-done.17.near, bf16[1,128,2048]{2,1,0:T(8,128)(2,1)S(1)} %collective-permute-done.23.far), custom_call_target="tpu_custom_call" | custom-call | tf_op jit(solution)/shard_map/join/pallas_call | solution.py:455
  (25 shorter events, 0.1 us)
Async XLA Ops:
  0.6 27.7 %collective-permute-start = (bf16[128,8192]{1,0:T(8,128)(2,1)}, bf16[128,8192]{1,0:T(8,128)(2,1)S(1)}, u32[]{:S(2)}, u32[]{:S(2)}) collective-permute-start(bf16[128,8192]{1,0:T(8,128)(2,1)} %bitcast.33), channel_id=1, source_target_pairs={{0,16},{16,0},{32,48},{48,32},{64,80},{80,64},{96,112},{112,96},{1... | collective-permute-start | bytes 6291464 | tf_op jit(solution)/shard_map/ppermute | solution.py:481
  2.1 26.3 %collective-permute-start.1 = (bf16[128,8192]{1,0:T(8,128)(2,1)}, bf16[128,8192]{1,0:T(8,128)(2,1)}, u32[]{:S(2)}, u32[]{:S(2)}) collective-permute-start(bf16[128,8192]{1,0:T(8,128)(2,1)} %bitcast.35), channel_id=1, source_target_pairs={{0,16},{16,0},{32,48},{48,32},{64,80},{80,64},{96,112},{112,96},{1... | collective-permute-start | bytes 6291464 | tf_op jit(solution)/shard_map/ppermute | solution.py:481
  2.2 6.7 %collective-permute-start.3 = (bf16[128,1024]{1,0:T(8,128)(2,1)}, bf16[128,1024]{1,0:T(8,128)(2,1)S(1)}, u32[]{:S(2)}, u32[]{:S(2)}) collective-permute-start(bf16[128,1024]{1,0:T(8,128)(2,1)} %bitcast.40), channel_id=1, source_target_pairs={{0,16},{16,0},{32,48},{48,32},{64,80},{80,64},{96,112},{112,96},{1... | collective-permute-start | bytes 786440 | tf_op jit(solution)/shard_map/ppermute | solution.py:481
  2.6 7.0 %collective-permute-start.4 = (bf16[128,1024]{1,0:T(8,128)(2,1)}, bf16[128,1024]{1,0:T(8,128)(2,1)S(1)}, u32[]{:S(2)}, u32[]{:S(2)}) collective-permute-start(bf16[128,1024]{1,0:T(8,128)(2,1)} %bitcast.42), channel_id=1, source_target_pairs={{0,16},{16,0},{32,48},{48,32},{64,80},{80,64},{96,112},{112,96},{1... | collective-permute-start | bytes 786440 | tf_op jit(solution)/shard_map/ppermute | solution.py:481
  4.1 5.6 %copy-start.2 = (s32[1,128]{1,0:T(1,128)}, s32[1,128]{1,0:T(1,128)S(1)}, u32[]{:S(2)}) copy-start(s32[1,128]{1,0:T(1,128)S(1)} %compare_select_fusion.sel) | copy-start | bytes 1540
  4.1 3.9 %collective-permute-start.2 = (s32[1,128]{1,0:T(1,128)S(1)}, s32[1,128]{1,0:T(1,128)S(1)}, u32[]{:S(2)}, u32[]{:S(2)}) collective-permute-start(s32[1,128]{1,0:T(1,128)S(1)} %compare_select_fusion.sel), channel_id=1, source_target_pairs={{0,16},{16,0},{32,48},{48,32},{64,80},{80,64},{96,112},{112,96},{1... | collective-permute-start | bytes 1544 | tf_op jit(solution)/shard_map/ppermute | solution.py:481
  8.0 1.7 %copy-start.8 = (s32[1,128]{1,0:T(1,128)}, s32[1,128]{1,0:T(1,128)S(1)}, u32[]{:S(2)}) copy-start(s32[1,128]{1,0:T(1,128)S(1)} %collective-permute-done.2.sel_in) | copy-start | bytes 1540
  8.9 0.8 copy-start.6
  9.7 0.7 copy-start.7
  14.0 6.8 %collective-permute-start.5 = (bf16[176,256]{1,0:T(8,128)(2,1)}, bf16[176,256]{1,0:T(8,128)(2,1)S(1)}, u32[]{:S(2)}, u32[]{:S(2)}) collective-permute-start(bf16[176,256]{1,0:T(8,128)(2,1)} %get-tuple-element.57), channel_id=1, source_target_pairs={{0,4},{1,5},{2,6},{3,7},{4,8},{5,9},{6,10},{7,11},{8,12},{9,13},{1... | collective-permute-start | bytes 270344 | tf_op jit(solution)/shard_map/ppermute | solution.py:473
  15.8 7.8 %collective-permute-start.6 = (bf16[176,256]{1,0:T(8,128)(2,1)}, bf16[176,256]{1,0:T(8,128)(2,1)S(1)}, u32[]{:S(2)}, u32[]{:S(2)}) collective-permute-start(bf16[176,256]{1,0:T(8,128)(2,1)} %get-tuple-element.58), channel_id=1, source_target_pairs={{0,8},{1,9},{2,10},{3,11},{4,12},{5,13},{6,14},{7,15},{8,0},{9,1},... | collective-permute-start | bytes 270344 | tf_op jit(solution)/shard_map/ppermute | solution.py:473
  19.1 4.5 %collective-permute-start.7 = (bf16[176,256]{1,0:T(8,128)(2,1)}, bf16[176,256]{1,0:T(8,128)(2,1)S(1)}, u32[]{:S(2)}, u32[]{:S(2)}) collective-permute-start(bf16[176,256]{1,0:T(8,128)(2,1)} %get-tuple-element.59), channel_id=1, source_target_pairs={{0,12},{1,13},{2,14},{3,15},{4,0},{5,1},{6,2},{7,3},{8,4},{9,5},{1... | collective-permute-start | bytes 270344 | tf_op jit(solution)/shard_map/ppermute | solution.py:473
  24.5 22.4 %copy-start.1 = (s32[3]{0:T(128)S(1)}, s32[3]{0:T(128)}, u32[]{:S(2)}) copy-start(s32[3]{0:T(128)} %pad_add_fusion.info) | copy-start | bytes 40
  24.5 13.4 %collective-permute-start.10 = (bf16[4,176,256]{2,1,0:T(8,128)(2,1)S(1)}, bf16[4,176,256]{2,1,0:T(8,128)(2,1)S(1)}, u32[]{:S(2)}, u32[]{:S(2)}) collective-permute-start(bf16[4,176,256]{2,1,0:T(8,128)(2,1)S(1)} %pad_maximum_fusion.1.kv0), channel_id=1, source_target_pairs={{0,3},{1,0},{2,1},{3,2},{4,7},{5,4},{6,5},{7,6},{8,11},{9,8},{10,9... | collective-permute-start | bytes 1081352 | tf_op jit(solution)/shard_map/ppermute | solution.py:477
  27.3 11.1 %collective-permute-start.9 = (bf16[4,176,256]{2,1,0:T(8,128)(2,1)S(1)}, bf16[4,176,256]{2,1,0:T(8,128)(2,1)S(1)}, u32[]{:S(2)}, u32[]{:S(2)}) collective-permute-start(bf16[4,176,256]{2,1,0:T(8,128)(2,1)S(1)} %pad_maximum_fusion.1.kv0), channel_id=1, source_target_pairs={{0,2},{1,3},{2,0},{3,1},{4,6},{5,7},{6,4},{7,5},{8,10},{9,11},{10,... | collective-permute-start | bytes 1081352 | tf_op jit(solution)/shard_map/ppermute | solution.py:477
  27.7 19.2 %collective-permute-start.8 = (bf16[4,176,256]{2,1,0:T(8,128)(2,1)S(1)}, bf16[4,176,256]{2,1,0:T(8,128)(2,1)S(1)}, u32[]{:S(2)}, u32[]{:S(2)}) collective-permute-start(bf16[4,176,256]{2,1,0:T(8,128)(2,1)S(1)} %pad_maximum_fusion.1.kv0), channel_id=1, source_target_pairs={{0,1},{1,2},{2,3},{3,0},{4,5},{5,6},{6,7},{7,4},{8,9},{9,10},{10,1... | collective-permute-start | bytes 1081352 | tf_op jit(solution)/shard_map/ppermute | solution.py:477
  28.4 1.3 copy-start.5
  35.2 17.6 %collective-permute-start.11 = (bf16[160,2048]{1,0:T(8,128)(2,1)}, bf16[160,2048]{1,0:T(8,128)(2,1)S(1)}, u32[]{:S(2)}, u32[]{:S(2)}) collective-permute-start(bf16[160,2048]{1,0:T(8,128)(2,1)} %get-tuple-element.64), channel_id=1, source_target_pairs={{0,4},{1,5},{2,6},{3,7},{4,8},{5,9},{6,10},{7,11},{8,12},{9,13},{1... | collective-permute-start | bytes 1966088 | tf_op jit(solution)/shard_map/ppermute | solution.py:473
  36.5 16.3 %collective-permute-start.12 = (bf16[160,2048]{1,0:T(8,128)(2,1)}, bf16[160,2048]{1,0:T(8,128)(2,1)S(1)}, u32[]{:S(2)}, u32[]{:S(2)}) collective-permute-start(bf16[160,2048]{1,0:T(8,128)(2,1)} %get-tuple-element.65), channel_id=1, source_target_pairs={{0,12},{1,13},{2,14},{3,15},{4,0},{5,1},{6,2},{7,3},{8,4},{9,5},{1... | collective-permute-start | bytes 1966088 | tf_op jit(solution)/shard_map/ppermute | solution.py:473
  37.9 35.5 %collective-permute-start.15 = (bf16[160,2048]{1,0:T(8,128)(2,1)}, bf16[160,2048]{1,0:T(8,128)(2,1)S(1)}, u32[]{:S(2)}, u32[]{:S(2)}) collective-permute-start(bf16[160,2048]{1,0:T(8,128)(2,1)} %get-tuple-element.81), channel_id=1, source_target_pairs={{0,8},{1,9},{2,10},{3,11},{4,12},{5,13},{6,14},{7,15},{8,0},{9,1},... | collective-permute-start | bytes 1966088 | tf_op jit(solution)/shard_map/ppermute | solution.py:473
  46.9 1.1 copy-start.4
  69.7 12.6 %collective-permute-start.13 = (bf16[160,2048]{1,0:T(8,128)(2,1)S(1)}, bf16[160,2048]{1,0:T(8,128)(2,1)S(1)}, u32[]{:S(2)}, u32[]{:S(2)}) collective-permute-start(bf16[160,2048]{1,0:T(8,128)(2,1)S(1)} %get-tuple-element.79), channel_id=1, source_target_pairs={{0,12},{1,13},{2,14},{3,15},{4,0},{5,1},{6,2},{7,3},{8,4},{9,5},{1... | collective-permute-start | bytes 1966088 | tf_op jit(solution)/shard_map/ppermute | solution.py:473
  73.4 10.6 %collective-permute-start.14 = (bf16[160,2048]{1,0:T(8,128)(2,1)S(1)}, bf16[160,2048]{1,0:T(8,128)(2,1)S(1)}, u32[]{:S(2)}, u32[]{:S(2)}) collective-permute-start(bf16[160,2048]{1,0:T(8,128)(2,1)S(1)} %get-tuple-element.80), channel_id=1, source_target_pairs={{0,4},{1,5},{2,6},{3,7},{4,8},{5,9},{6,10},{7,11},{8,12},{9,13},{1... | collective-permute-start | bytes 1966088 | tf_op jit(solution)/shard_map/ppermute | solution.py:473
  84.1 15.0 %copy-start = (bf16[1,128,8192]{2,1,0:T(8,128)(2,1)S(1)}, bf16[1,128,8192]{2,1,0:T(8,128)(2,1)}, u32[]{:S(2)}) copy-start(bf16[1,128,8192]{2,1,0:T(8,128)(2,1)} %param.7) | copy-start | bytes 6291460
  84.1 15.0 %copy-start.3 = (s32[1,128]{1,0:T(1,128)S(1)}, s32[1,128]{1,0:T(1,128)}, u32[]{:S(2)}) copy-start(s32[1,128]{1,0:T(1,128)} %copy-done.2) | copy-start | bytes 1540
  84.3 14.7 %collective-permute-start.16 = (bf16[3,160,2048]{2,1,0:T(8,128)(2,1)S(1)}, bf16[3,160,2048]{2,1,0:T(8,128)(2,1)S(1)}, u32[]{:S(2)}, u32[]{:S(2)}) collective-permute-start(bf16[3,160,2048]{2,1,0:T(8,128)(2,1)S(1)} %pad_maximum_fusion.mine.near), channel_id=1, source_target_pairs={{0,16},{16,0},{32,48},{48,32},{64,80},{80,64},{96,112},{112,96},{1... | collective-permute-start | bytes 5898248 | tf_op jit(solution)/shard_map/ppermute | solution.py:481
  95.4 26.7 %collective-permute-start.18 = (bf16[160,2048]{1,0:T(8,128)(2,1)S(1)}, bf16[160,2048]{1,0:T(8,128)(2,1)S(1)}, u32[]{:S(2)}, u32[]{:S(2)}) collective-permute-start(bf16[160,2048]{1,0:T(8,128)(2,1)S(1)} %get-tuple-element.89), channel_id=1, source_target_pairs={{0,8},{1,9},{2,10},{3,11},{4,12},{5,13},{6,14},{7,15},{8,0},{9,1},... | collective-permute-start | bytes 1966088 | tf_op jit(solution)/shard_map/ppermute | solution.py:473
  100.4 36.4 %collective-permute-start.17 = (bf16[3,128,2048]{2,1,0:T(8,128)(2,1)S(1)}, bf16[3,128,2048]{2,1,0:T(8,128)(2,1)S(1)}, u32[]{:S(2)}, u32[]{:S(2)}) collective-permute-start(bf16[3,128,2048]{2,1,0:T(8,128)(2,1)S(1)} %update.2), channel_id=1, source_target_pairs={{0,16},{16,32},{32,48},{48,64},{64,80},{80,96},{96,112},{1,17},{17... | collective-permute-start | bytes 4718600 | tf_op jit(solution)/shard_map/ppermute | solution.py:485
  104.2 10.5 %collective-permute-start.19 = (bf16[4,160,256]{2,1,0:T(8,128)(2,1)S(1)}, bf16[4,160,256]{2,1,0:T(8,128)(2,1)S(1)}, u32[]{:S(2)}, u32[]{:S(2)}) collective-permute-start(bf16[4,160,256]{2,1,0:T(8,128)(2,1)S(1)} %get-tuple-element.91), channel_id=1, source_target_pairs={{0,1},{1,2},{2,3},{3,0},{4,5},{5,6},{6,7},{7,4},{8,9},{9,10},{10,1... | collective-permute-start | bytes 983048 | tf_op jit(solution)/shard_map/ppermute | solution.py:477
  105.9 15.7 %collective-permute-start.20 = (bf16[4,160,256]{2,1,0:T(8,128)(2,1)S(1)}, bf16[4,160,256]{2,1,0:T(8,128)(2,1)S(1)}, u32[]{:S(2)}, u32[]{:S(2)}) collective-permute-start(bf16[4,160,256]{2,1,0:T(8,128)(2,1)S(1)} %get-tuple-element.92), channel_id=1, source_target_pairs={{0,2},{1,3},{2,0},{3,1},{4,6},{5,7},{6,4},{7,5},{8,10},{9,11},{10,... | collective-permute-start | bytes 983048 | tf_op jit(solution)/shard_map/ppermute | solution.py:477
  107.4 14.6 %collective-permute-start.21 = (bf16[4,160,256]{2,1,0:T(8,128)(2,1)S(1)}, bf16[4,160,256]{2,1,0:T(8,128)(2,1)S(1)}, u32[]{:S(2)}, u32[]{:S(2)}) collective-permute-start(bf16[4,160,256]{2,1,0:T(8,128)(2,1)S(1)} %get-tuple-element.93), channel_id=1, source_target_pairs={{0,3},{1,0},{2,1},{3,2},{4,7},{5,4},{6,5},{7,6},{8,11},{9,8},{10,9... | collective-permute-start | bytes 983048 | tf_op jit(solution)/shard_map/ppermute | solution.py:477
  122.2 3.2 %collective-permute-start.22 = (bf16[1,160,2048]{2,1,0:T(8,128)(2,1)S(1)}, bf16[1,160,2048]{2,1,0:T(8,128)(2,1)S(1)}, u32[]{:S(2)}, u32[]{:S(2)}) collective-permute-start(bf16[1,160,2048]{2,1,0:T(8,128)(2,1)S(1)} %bitcast.28), channel_id=1, source_target_pairs={{0,16},{16,0},{32,48},{48,32},{64,80},{80,64},{96,112},{112,96},{1... | collective-permute-start | bytes 1966088 | tf_op jit(solution)/shard_map/ppermute | solution.py:481
  122.7 8.0 %collective-permute-start.24 = (bf16[160,256]{1,0:T(8,128)(2,1)S(1)}, bf16[160,256]{1,0:T(8,128)(2,1)S(1)}, u32[]{:S(2)}, u32[]{:S(2)}) collective-permute-start(bf16[160,256]{1,0:T(8,128)(2,1)S(1)} %get-tuple-element.100), channel_id=1, source_target_pairs={{0,4},{1,5},{2,6},{3,7},{4,8},{5,9},{6,10},{7,11},{8,12},{9,13},{1... | collective-permute-start | bytes 245768 | tf_op jit(solution)/shard_map/ppermute | solution.py:473
  122.7 8.0 %collective-permute-start.25 = (bf16[160,256]{1,0:T(8,128)(2,1)S(1)}, bf16[160,256]{1,0:T(8,128)(2,1)S(1)}, u32[]{:S(2)}, u32[]{:S(2)}) collective-permute-start(bf16[160,256]{1,0:T(8,128)(2,1)S(1)} %get-tuple-element.101), channel_id=1, source_target_pairs={{0,8},{1,9},{2,10},{3,11},{4,12},{5,13},{6,14},{7,15},{8,0},{9,1},... | collective-permute-start | bytes 245768 | tf_op jit(solution)/shard_map/ppermute | solution.py:473
  123.6 7.1 %collective-permute-start.26 = (bf16[160,256]{1,0:T(8,128)(2,1)S(1)}, bf16[160,256]{1,0:T(8,128)(2,1)S(1)}, u32[]{:S(2)}, u32[]{:S(2)}) collective-permute-start(bf16[160,256]{1,0:T(8,128)(2,1)S(1)} %get-tuple-element.102), channel_id=1, source_target_pairs={{0,12},{1,13},{2,14},{3,15},{4,0},{5,1},{6,2},{7,3},{8,4},{9,5},{1... | collective-permute-start | bytes 245768 | tf_op jit(solution)/shard_map/ppermute | solution.py:473
  126.1 10.7 %collective-permute-start.23 = (bf16[1,128,2048]{2,1,0:T(8,128)(2,1)S(1)}, bf16[1,128,2048]{2,1,0:T(8,128)(2,1)S(1)}, u32[]{:S(2)}, u32[]{:S(2)}) collective-permute-start(bf16[1,128,2048]{2,1,0:T(8,128)(2,1)S(1)} %update.3), channel_id=1, source_target_pairs={{0,16},{16,32},{32,48},{48,64},{64,80},{80,96},{96,112},{1,17},{17... | collective-permute-start | bytes 1572872 | tf_op jit(solution)/shard_map/ppermute | solution.py:485
  130.7 1.7 %collective-permute-start.27 = (bf16[4,160,256]{2,1,0:T(8,128)(2,1)S(1)}, bf16[4,160,256]{2,1,0:T(8,128)(2,1)S(1)}, u32[]{:S(2)}, u32[]{:S(2)}) collective-permute-start(bf16[4,160,256]{2,1,0:T(8,128)(2,1)S(1)} %pad_maximum_fusion.2.sums), channel_id=1, source_target_pairs={{0,16},{16,0},{32,48},{48,32},{64,80},{80,64},{96,112},{112,96},{1... | collective-permute-start | bytes 983048 | tf_op jit(solution)/shard_map/ppermute | solution.py:481

commit v2 on v1

v2 whole, which is shorter than its diff:
```python
import functools, math
import jax, jax.numpy as jnp
from jax import lax
from jax.experimental import pallas as pl
from jax.experimental.pallas import tpu as pltpu
from jax.sharding import PartitionSpec as P

HEAD = 128
GROUP = 8
ROWS = 128
SLOTS = 32
BLOCKS = 16
CHUNK = 512
TILE = 512
SCALE = HEAD ** -0.5
LOG2E = math.log2(math.e)
BF = jnp.bfloat16
F32 = jnp.float32


def dot(a, b):
    return jnp.dot(a, b, preferred_element_type=F32)


def fold(x, op):
    return op(x.reshape(x.shape[0] // 8, 8, x.shape[1]), axis=0)


def turned(x, width, rows, out):
    cols = width * GROUP
    for h in range(GROUP):
        rows[h * width:(h + 1) * width, :] = x[:, h * HEAD:(h + 1) * HEAD]
    for t in range(0, cols, HEAD):
        out[:, t:t + HEAD] = rows[t:t + HEAD, :].T


def tiles_of(cols):
    tile = min(TILE, cols)
    return [slice(t, t + tile) for t in range(0, cols, tile)]


def at(c):
    return pl.ds(pl.multiple_of(c * CHUNK, CHUNK), CHUNK)


def loop(first, end, fn):
    lax.fori_loop(first, end, lambda c, z: (fn(c), z)[1], 0)


def forward_pass(q, width, k_ref, vt_ref, e_ref, stat, acc, chunks, full, mask_of, scr):
    rows, qt, s_scr, m_scr, l_scr = scr
    cols = width * GROUP
    turned(q, width, rows, qt)
    tiles = tiles_of(cols)
    m_scr[:, :cols] = jnp.full((8, cols), -1e30, F32)
    l_scr[:, :cols] = jnp.zeros((8, cols), F32)
    acc[...] = jnp.zeros((HEAD, cols), F32)

    def score(c, masked):
        k = k_ref[at(c), :]
        for t in tiles:
            s = dot(k, qt[:, t])
            if masked:
                s = jnp.where(mask_of(c), s, -1e30)
            s_scr[at(c), t] = s
            m_scr[:, t] = jnp.maximum(m_scr[:, t], fold(s, jnp.max))

    loop(0, full, lambda c: score(c, False))
    loop(full, chunks, lambda c: score(c, True))
    top = jnp.max(m_scr[:, :cols], axis=0, keepdims=True) * (SCALE * LOG2E)
    m_scr[:, :cols] = jnp.broadcast_to(top, (8, cols))

    def weigh(c):
        for t in tiles:
            e = jnp.exp2(s_scr[at(c), t] * (SCALE * LOG2E) - m_scr[0:1, t])
            l_scr[:, t] += fold(e, jnp.sum)
            eb = e.astype(BF)
            e_ref[at(c), t] = eb
            acc[:, t] += dot(vt_ref[c], eb)

    loop(0, chunks, weigh)
    inv = 1.0 / jnp.sum(l_scr[:, :cols], axis=0, keepdims=True)
    acc[:, :cols] = acc[:, :cols] * inv
    stat[...] = jnp.broadcast_to(inv, (8, cols))


def backward_pass(q, g, width, v_ref, kt_ref, e_ref, stat, attn_t, dk_ref, dv_ref, chunks, scr):
    qs, gs, gt, acc, d_scr = scr
    cols = width * GROUP
    for h in range(GROUP):
        qs[h * width:(h + 1) * width, :] = q[:, h * HEAD:(h + 1) * HEAD]
    turned(g, width, gs, gt)
    tiles = tiles_of(cols)
    acc[:, :cols] = jnp.zeros((HEAD, cols), F32)
    delta = jnp.sum(attn_t[...] * gt[:, :cols].astype(F32), axis=0, keepdims=True)
    d_scr[:, :cols] = jnp.broadcast_to(delta, (8, cols))

    def back(c):
        v = v_ref[at(c), :]
        dk = dk_ref[at(c), :]
        dv = dv_ref[at(c), :]
        for t in tiles:
            dp = dot(v, gt[:, t])
            p = e_ref[at(c), t].astype(F32) * stat[0:1, t]
            ds = (p * (dp - d_scr[0:1, t])).astype(BF)
            dv += dot(p.astype(BF), gs[t, :])
            dk += dot(ds, qs[t, :])
            acc[:, t] += dot(kt_ref[c], ds)
        dk_ref[at(c), :] = dk
        dv_ref[at(c), :] = dv

    loop(0, chunks, back)


def emit(src, width, scale, out, row, col):
    for t in range(width * GROUP // 128):
        x = (src[:, t * 128:(t + 1) * 128] * scale).T.astype(BF)
        per = 128 // width
        for i in range(per):
            h = t * per + i
            out[row:row + width, col + h * HEAD:col + (h + 1) * HEAD] = x[i * width:(i + 1) * width, :]


def chooser(sel):
    return (lax.broadcasted_iota(jnp.int32, (ROWS, ROWS), 0) == sel[0:1, :]).astype(F32)


def compact(sel):
    return chooser(sel).T[:SLOTS, :].astype(BF)


HALF = GROUP * HEAD
QG = 2 * HALF
KV = 2 * HEAD
DENSE = BLOCKS * ROWS
FEW = BLOCKS * SLOTS
SENT = ROWS + SLOTS
COUNT = 16
MARKED = SENT + COUNT
VMEM = pl.BlockSpec(memory_space=pltpu.VMEM)
SMEM = pl.BlockSpec(memory_space=pltpu.SMEM)
WHOLE = pltpu.CompilerParams(vmem_limit_bytes=60 << 20)
PARAMS = pltpu.CompilerParams(vmem_limit_bytes=16 << 20)
ANY = pl.BlockSpec(memory_space=pl.ANY)
SEL = pl.BlockSpec((1, ROWS), lambda i, info: (0, 0))


def own_head(shift):
    core, z = lax.rem(lax.axis_index("section"), 2), lax.div(lax.axis_index("ctx"), 4)
    return 2 * lax.rem(z + shift, 4) + core, core


def pack_kv_kernel(k, v, k_in, v_in, sel, sel_in, *outs):
    def fill(dense, few, few_sel):
        pick = compact(few_sel)
        count = jnp.sum((few_sel[0:1, :] >= 0).astype(F32), axis=1, keepdims=True)
        for step, out in enumerate(outs):
            here = pl.ds(pl.multiple_of(own_head(step)[0] * HEAD, HEAD), HEAD)
            for side in range(2):
                cols = slice(side * HEAD, (side + 1) * HEAD)
                out[:ROWS, cols] = dense[side][:, here]
                out[ROWS:SENT, cols] = dot(pick, few[side][:, here]).astype(BF)
            out[SENT:, :] = jnp.broadcast_to(count, (COUNT, KV)).astype(BF)

    @pl.when(own_head(0)[1] == 1)
    def _():
        fill((k, v), (k_in, v_in), sel_in)

    @pl.when(own_head(0)[1] == 0)
    def _():
        fill((k_in, v_in), (k, v), sel)


def pack_kv(k, v, k_in, v_in, sel, sel_in):
    return list(pl.pallas_call(
        pack_kv_kernel,
        out_shape=[jax.ShapeDtypeStruct((MARKED, KV), BF)] * 4,
        in_specs=[VMEM] * 6,
        out_specs=[VMEM] * 4,
        compiler_params=PARAMS,
        name="pack_kv",
    )(k, v, k_in, v_in, sel, sel_in))


def pack_kernel(own, come, sel, sel_in, o0, o1, o2, o3, held, sems):
    core = own_head(0)[1]
    outs, copies = (o0, o1, o2, o3), []
    for step in range(4):
        here = pl.ds(pl.multiple_of(own_head(step)[0] * HALF, HALF), HALF)
        for i, ref in enumerate((own, come)):
            copies.append(pltpu.make_async_copy(ref.at[:, here], held.at[step, i], sems.at[2 * step + i]))
            copies[-1].start()
    pick = compact(jnp.where(core == 1, sel_in[...], sel[...]))
    for step, out in enumerate(outs):
        copies[2 * step].wait()
        copies[2 * step + 1].wait()

        @pl.when(core == 1)
        def _(step=step, out=out):
            out[:ROWS, :] = held[step, 0]
            out[ROWS:, :] = dot(pick, held[step, 1]).astype(BF)

        @pl.when(core == 0)
        def _(step=step, out=out):
            out[:ROWS, :] = held[step, 1]
            out[ROWS:, :] = dot(pick, held[step, 0]).astype(BF)


def pack(own, come, sel, sel_in):
    return list(pl.pallas_call(
        pack_kernel,
        out_shape=[jax.ShapeDtypeStruct((SENT, HALF), BF)] * 4,
        in_specs=[ANY] * 2 + [VMEM] * 2,
        out_specs=[VMEM] * 4,
        scratch_shapes=[pltpu.VMEM((4, 2, ROWS, HALF), BF), pltpu.SemaphoreType.DMA((8,))],
        compiler_params=WHOLE,
        name="pack",
    )(own, come, sel, sel_in))


FORTH = pltpu.CompilerParams(vmem_limit_bytes=12 << 20)
BACK = pltpu.CompilerParams(vmem_limit_bytes=8 << 20)
SUMS = [((DENSE, HEAD), F32)] * 2 + [((FEW, HEAD), F32)] * 2
FEWER = SLOTS * GROUP
LEFT = [((SENT, HALF), BF), ((DENSE, HALF), BF), ((8, HALF), F32), ((HEAD, HALF), F32),
        ((FEW, FEWER), BF), ((8, FEWER), F32), ((HEAD, FEWER), F32)]
KEYS = [((DENSE, HEAD), BF), ((DENSE // CHUNK, HEAD, CHUNK), BF), ((FEW, HEAD), BF), ((FEW // CHUNK, HEAD, CHUNK), BF)]
KEYED = KEYS + KEYS + [((FEW, HEAD), F32)]


def shaped(shapes):
    return [jax.ShapeDtypeStruct(s, d) for s, d in shapes]


def held(shapes):
    return [pltpu.VMEM(s, d) for s, d in shapes]


FORWARD = held([((HALF, HEAD), BF), ((HEAD, HALF), BF), ((DENSE, HALF), F32), ((8, HALF), F32), ((8, HALF), F32)])
BACKWARD = held([((HALF, HEAD), BF), ((HALF, HEAD), BF), ((HEAD, HALF), BF), ((HEAD, HALF), F32), ((8, HALF), F32)])


def cost(flops):
    return pl.CostEstimate(flops=int(flops), bytes_accessed=4 << 20, transcendentals=0)


def turn_blocks(x, xt):
    for c in range(xt.shape[0]):
        xt[c] = x[c * CHUNK:(c + 1) * CHUNK, :].T


def arrange(info, kvs, keyed):
    kd, ktd, kr, ktr, vd, vtd, vr, vtr, flags = keyed
    slot = lax.broadcasted_iota(jnp.int32, (SLOTS, HEAD), 0).astype(F32)
    for ky, kv in enumerate(kvs):
        for kz in range(4):
            b = 4 * lax.rem(info[1] + 4 - kz, 4) + lax.rem(info[2] + 4 - ky, 4)
            big = pl.ds(pl.multiple_of(b * ROWS, ROWS), ROWS)
            small = pl.ds(pl.multiple_of(b * SLOTS, SLOTS), SLOTS)
            kd[big, :] = kv[kz, :ROWS, :HEAD]
            vd[big, :] = kv[kz, :ROWS, HEAD:]
            kr[small, :] = kv[kz, ROWS:SENT, :HEAD]
            vr[small, :] = kv[kz, ROWS:SENT, HEAD:]
            flags[small, :] = (slot < kv[kz, SENT:, :HEAD].astype(F32)[0:1, :]).astype(F32)
    for x, xt in ((kd, ktd), (kr, ktr), (vd, vtd), (vr, vtr)):
        turn_blocks(x, xt)


def reach(info, shift):
    blk = 4 * lax.rem(info[1] + 4 - shift, 4) + info[2]
    per = CHUNK // ROWS
    return blk, lax.div(blk + per, per)


def forward_block(info, shift, q, keyed, left, scr):
    kd, _, kr, _, _, vtd, _, vtr, flags = keyed
    attn, e_dense, inv_dense, t_dense, e_few, inv_few, t_few = left
    blk, chunks = reach(info, shift)

    def place(cols):
        shape = (CHUNK, cols)
        return lax.broadcasted_iota(jnp.int32, shape, 0), lax.broadcasted_iota(jnp.int32, shape, 1)

    def causal(c):
        row, col = place(TILE)
        return c * CHUNK + row <= blk * ROWS + lax.rem(col, ROWS)

    def routed(c):
        row, col = place(FEWER)
        near = c * CHUNK + row <= blk * SLOTS + lax.rem(col, SLOTS)
        return near & (jnp.concatenate([flags[at(c), :]] * (FEWER // HEAD), axis=1) > 0.5)

    forward_pass(q[:ROWS, :], ROWS, kd, vtd, e_dense, inv_dense, t_dense, chunks, chunks - 1, causal, scr)
    emit(t_dense, ROWS, 1.0, attn, 0, 0)
    forward_pass(q[ROWS:, :], SLOTS, kr, vtr, e_few, inv_few, t_few, FEW // CHUNK, 0, routed, scr)
    emit(t_few, SLOTS, 1.0, attn, ROWS, 0)


def forward_kernel(shifts, first, info, *refs):
    n, m = len(shifts), len(LEFT)
    qs, refs = refs[:n], refs[n:]
    if first:
        kvs, refs = refs[:4], refs[4:]
    else:
        keyed, refs = refs[:9], refs[9:]
    lefts, refs = refs[:m * n], refs[m * n:]
    if first:
        keyed, refs = refs[:9], refs[9:]
        arrange(info, kvs, keyed)
    for i, shift in enumerate(shifts):
        forward_block(info, shift, qs[i], keyed, lefts[m * i:m * (i + 1)], refs)


def forward(shifts, info, qs, kvs=None, keyed=None):
    n, m, first = len(shifts), len(LEFT), kvs is not None
    shapes = LEFT * n + (KEYED if first else [])
    others = list(kvs if first else keyed)
    outs = pl.pallas_call(
        functools.partial(forward_kernel, shifts, first),
        out_shape=shaped(shapes),
        in_specs=[SMEM] + [VMEM] * (n + len(others)),
        out_specs=[VMEM] * len(shapes),
        scratch_shapes=FORWARD,
        compiler_params=FORTH,
        cost_estimate=cost(n * 4e9),
        name="forward",
    )(info, *qs, *others)
    lefts = [list(outs[m * i:m * (i + 1)]) for i in range(n)]
    return (lefts, outs[m * n:]) if first else lefts


def backward_block(info, shift, q, g, keyed, left, sums, dq, scr):
    _, ktd, _, ktr, vd, _, vr, _, _ = keyed
    _, chunks = reach(info, shift)
    backward_pass(q[:ROWS, :], g[:ROWS, :], ROWS, vd, ktd, *left[:3], *sums[:2], chunks, scr)
    emit(scr[3], ROWS, SCALE, dq, 0, 0)
    backward_pass(q[ROWS:, :], g[ROWS:, :], SLOTS, vr, ktr, *left[3:], *sums[2:], FEW // CHUNK, scr)
    emit(scr[3], SLOTS, SCALE, dq, ROWS, 0)


def backward_kernel(shifts, first, info, *refs):
    n, m = len(shifts), len(LEFT) - 1
    qs, gs, refs = refs[:n], refs[n:2 * n], refs[2 * n:]
    lefts, keyed, refs = refs[:m * n], refs[m * n:m * n + 9], refs[m * n + 9:]
    if first:
        dqs, sums, scr = refs[:n], refs[n:n + 4], refs[n + 4:]
    else:
        came, dqs, sent, sums, scr = refs[:4], refs[4:n + 4], refs[n + 4:n + 8], refs[n + 8:n + 12], refs[n + 12:]
    for i, total in enumerate(sums):
        total[...] = jnp.zeros_like(total) if first else came[i][...]
    for i, shift in enumerate(shifts):
        backward_block(info, shift, qs[i], gs[i], keyed, lefts[m * i:m * (i + 1)], sums, dqs[i], scr)
    for ky in range(0 if first else 4):
        for kz in range(4):
            b = 4 * lax.rem(info[1] + kz, 4) + lax.rem(info[2] + ky, 4)
            big = pl.ds(pl.multiple_of(b * ROWS, ROWS), ROWS)
            small = pl.ds(pl.multiple_of(b * SLOTS, SLOTS), SLOTS)
            sent[ky][kz, :ROWS, :HEAD] = (sums[0][big, :] * SCALE).astype(BF)
            sent[ky][kz, :ROWS, HEAD:] = sums[1][big, :].astype(BF)
            sent[ky][kz, ROWS:, :HEAD] = (sums[2][small, :] * SCALE).astype(BF)
            sent[ky][kz, ROWS:, HEAD:] = sums[3][small, :].astype(BF)


def backward(shifts, info, qs, gs, lefts, keyed, sums=()):
    n, first = len(shifts), not sums
    shapes = [((SENT, HALF), BF)] * n + (SUMS if first else [((4, SENT, KV), BF)] * 4)
    args = [qs[i] for i in shifts] + [gs[i] for i in shifts] + [x for i in shifts for x in lefts[i][1:]]
    args += list(keyed) + list(sums)
    outs = pl.pallas_call(
        functools.partial(backward_kernel, shifts, first),
        out_shape=shaped(shapes),
        in_specs=[SMEM] + [VMEM] * len(args),
        out_specs=[VMEM] * len(shapes),
        scratch_shapes=([] if first else held(SUMS)) + BACKWARD,
        compiler_params=BACK,
        cost_estimate=cost(n * 6e9),
        name="backward",
    )(info, *args)
    return list(outs[:n]), list(outs[n:])


def fold_kernel(a, b, c, d, *outs):
    for i, out in enumerate(outs):
        total = a[i].astype(F32) + b[i].astype(F32) + c[i].astype(F32) + d[i].astype(F32)
        out[...] = total.astype(BF)


def fold_sums(parts):
    return list(pl.pallas_call(
        fold_kernel,
        out_shape=[jax.ShapeDtypeStruct((SENT, KV), BF)] * 4,
        in_specs=[VMEM] * 4,
        out_specs=[VMEM] * 4,
        compiler_params=PARAMS,
        name="fold_sums",
    )(*parts))


def heads_of(info, sel, mine, theirs, put):
    @pl.when(info[0] == 1)
    def _():
        put(0, theirs[0, :ROWS, :].astype(F32))
        put(1, mine[0, :ROWS, :].astype(F32))

    @pl.when(info[0] == 0)
    def _():
        pick = chooser(sel)[:, :SLOTS].astype(BF)
        put(0, dot(pick, mine[0, ROWS:, :]))
        put(1, dot(pick, theirs[0, ROWS:, :]))


def update_kernel(info, seg, mine, theirs, sel, out):
    def put(i, x):
        cols = slice(i * HALF, (i + 1) * HALF)
        out[:, cols] = (seg[:, cols].astype(F32) + x).astype(BF)

    heads_of(info, sel, mine, theirs, put)


def finish_q_kernel(info, mine, theirs, sel, out):
    def put(i, x):
        out[:, i * HALF:(i + 1) * HALF] = x.astype(BF)

    heads_of(info, sel, mine, theirs, put)


def by_head(kernel, name, info, seg, mine, theirs, sel):
    part = pl.BlockSpec((1, SENT, HALF), lambda i, info: (i, 0, 0))
    whole = pl.BlockSpec((ROWS, 2 * HALF), lambda i, info: (0, lax.rem(info[1] + i, 4)))
    segs = [] if seg is None else [seg]
    return pl.pallas_call(
        kernel,
        grid_spec=pltpu.PrefetchScalarGridSpec(
            num_scalar_prefetch=1,
            grid=(4,),
            in_specs=[whole] * len(segs) + [part, part, SEL],
            out_specs=whole,
        ),
        out_shape=jax.ShapeDtypeStruct((ROWS, 8 * HALF), BF),
        compiler_params=PARAMS,
        name=name,
    )(info, *segs, mine, theirs, sel)


def settle_kernel(x, out):
    out[...] = x[...]


def settle(x):
    part = pl.BlockSpec((ROWS, 2 * HALF), lambda i: (0, i))
    return pl.pallas_call(
        settle_kernel,
        grid=(4,),
        in_specs=[part],
        out_specs=part,
        out_shape=jax.ShapeDtypeStruct(x.shape, x.dtype),
        compiler_params=PARAMS,
        name="settle",
    )(x)


def finish_kv_kernel(info, sums, sums_in, sel, dk, dv):
    def fill(even, odd, rows):
        for shift in range(4):
            for i, ref in enumerate((even, odd)):
                head = 2 * lax.rem(info[1] + 4 - shift, 4) + i
                at = pl.ds(pl.multiple_of(head * HEAD, HEAD), HEAD)
                x = rows(ref[shift])
                dk[:, at] = x[:, :HEAD]
                dv[:, at] = x[:, HEAD:]

    @pl.when(info[0] == 1)
    def _():
        fill(sums_in, sums, lambda x: x[:ROWS, :])

    @pl.when(info[0] == 0)
    def _():
        pick = chooser(sel)[:, :SLOTS].astype(BF)
        fill(sums, sums_in, lambda x: dot(pick, x[ROWS:, :]).astype(BF))


def finish_kv(info, sums, sums_in, sel):
    return pl.pallas_call(
        finish_kv_kernel,
        out_shape=[jax.ShapeDtypeStruct((ROWS, 8 * HEAD), BF)] * 2,
        in_specs=[SMEM] + [VMEM] * 3,
        out_specs=[VMEM] * 2,
        compiler_params=PARAMS,
        name="finish_kv",
    )(info, sums, sums_in, sel)


def along_z(x, by):
    return lax.ppermute(x, "ctx", [(4 * z + y, 4 * ((z + by) % 4) + y) for z in range(4) for y in range(4)])


def along_y(x, by):
    return lax.ppermute(x, "ctx", [(4 * z + y, 4 * z + (y + by) % 4) for z in range(4) for y in range(4)])


def swap(x):
    return lax.ppermute(x, "section", [(i, i ^ 1) for i in range(8)])


def onward(x):
    return lax.ppermute(x, "section", [(i, i + 1) for i in range(7)])


def both(*xs):
    return lax.optimization_barrier(xs)


def body(segment_input, queries, keys, values, cotangent, selected, counts):
    section, place = lax.axis_index("section"), lax.axis_index("ctx")
    info = jnp.stack([section % 2, place // 4, place % 4]).astype(jnp.int32)
    seg, q, k, v, g = (x[0] for x in (segment_input, queries, keys, values, cotangent))
    sel = jnp.where(jnp.arange(ROWS, dtype=jnp.int32)[None, :] < counts, selected, -1)

    k_in, v_in, sel_in = swap(k), swap(v), swap(sel)
    kv = pack_kv(k, v, k_in, v_in, sel, sel_in)
    q, g, *_ = both(q, g, k_in, v_in, sel_in)
    q_in, g_in = swap(q), swap(g)
    qs = pack(q, q_in, sel, sel_in)
    for by in (1, 3, 2):
        kv[by] = along_z(kv[by], by)
    kv[1], kv[2], kv[3], qs[1], qs[2], qs[3], g_in = both(kv[1], kv[2], kv[3], qs[1], qs[2], qs[3], g_in)
    column = jnp.stack(kv)
    kvs = [column] + [along_y(column, by) for by in (1, 2, 3)]
    qs[1], qs[2], qs[3], g_in, _ = both(qs[1], qs[2], qs[3], g_in, column)
    for by in (1, 3, 2):
        qs[by] = along_z(qs[by], by)
    gs = pack(g, g_in, sel, sel_in)

    (own,), keyed = forward((0,), info, [qs[0]], kvs=kvs)
    for by in (1, 3, 2):
        gs[by] = along_z(gs[by], by)
    one, three, two = forward((1, 3, 2), info, [qs[1], qs[3], qs[2]], keyed=keyed)
    lefts = [own, one, two, three]
    attn = [along_z(lefts[by][0], 4 - by) if by else lefts[by][0] for by in range(4)]
    dq = [None] * 4
    (dq[1], dq[3]), sums = backward((1, 3), info, qs, gs, lefts, keyed)
    (dq[0], dq[2]), sent = backward((0, 2), info, qs, gs, lefts, keyed, sums)
    dq = [along_z(dq[by], 4 - by) if by else dq[by] for by in range(4)]
    attn[1], attn[2], attn[3], dq[1], dq[3], sent[0] = both(attn[1], attn[2], attn[3], dq[1], dq[3], sent[0])
    attn = jnp.stack(attn)
    updated = by_head(update_kernel, "update", info, seg, attn, swap(attn), sel)
    next_input = onward(updated)
    sums = fold_sums([sent[0]] + [along_y(sent[by], by) for by in (1, 2, 3)])
    dq[2], sums[0] = both(dq[2], sums[0])
    dq = jnp.stack(dq)
    query_grad = by_head(finish_q_kernel, "finish_q", info, None, dq, swap(dq), sel)
    sums = [sums[0]] + [along_z(sums[by], by) for by in (1, 2, 3)]
    next_input, query_grad, *sums = both(settle(next_input), query_grad, *sums)
    sums = jnp.stack(sums)
    key_grad, value_grad = finish_kv(info, sums, swap(sums), sel)
    return next_input[None], query_grad[None], key_grad[None], value_grad[None]


def solution(mesh):
    wide, thin = P("section", "ctx", None), P("section", "ctx")
    return jax.shard_map(
        body,
        mesh=mesh,
        in_specs=(wide,) * 5 + (thin,) * 2,
        out_specs=(wide,) * 4,
        check_vma=False,
    )
```

time: 140 us -> 127 us (0.907)
  waiting for transfers between devices: 38.6 us -> 32.4 us
  starting transfers between devices: 46.3 us -> 41.3 us
    ppermute x12 -> x18, starting transfers between devices: 15.3 us -> 25.5 us  [along_z(): lax.ppermute(x, 'ctx', [(4 * z + y, 4 * ((z + by) % 4) + y) for z in rang...]
    ppermute x8, starting transfers between devices: 14.6 us -> 5.31 us  [swap(): return lax.ppermute(x, 'section', [(i, i ^ 1) for i in range(8)])]
    ppermute x8, waiting for transfers between devices: 9.46 us -> 4.75 us  [swap(): return lax.ppermute(x, 'section', [(i, i ^ 1) for i in range(8)])]
    ppermute x2 -> x1, starting transfers between devices: 8.37 us -> 3.96 us  [onward(): return lax.ppermute(x, 'section', [(i, i + 1) for i in range(7)])]
    ppermute x2 -> x1, waiting for transfers between devices: 1.5 us -> 0.01 us  [onward(): return lax.ppermute(x, 'section', [(i, i + 1) for i in range(7)])]
    ppermute x6, starting transfers between devices: 8.01 us -> 6.58 us  [along_y(): lax.ppermute(x, 'ctx', [(4 * z + y, 4 * z + (y + by) % 4) for z in range(...]
    pallas_call x9 -> x11, Pallas kernels: 47.1 us -> 46.6 us  [the longest x2 16.8 us: backward(): pl.pallas_call(functools.partial(backward_kernel, shifts, first), out_sha...]
    ppermute x12 -> x18, waiting for transfers between devices: 5.55 us -> 5.25 us  [along_z(): lax.ppermute(x, 'ctx', [(4 * z + y, 4 * ((z + by) % 4) + y) for z in rang...]
  transfers between devices with their start and end apart: 28 -> 33, of which waited for: 13 -> 11; matrix products, arithmetic and copies ran while one was open for 2% -> 1% of each run, Pallas kernels for 32% -> 35%
where the time goes in v2:
time: 127 us; the launch traced here: 126 us
  Pallas kernels  46.7 us (37%)
  starting transfers between devices  41.3 us (33%)
  waiting for transfers between devices  32.4 us (26%)
  local copies, waits for them, and re-layouts  3.25 us (3%)
  between operations  1.5 us (1%)
    ppermute x18, starting transfers between devices, along_z(): lax.ppermute(x, 'ctx', [(4 * z + y, 4 * ((z + by) % 4) + y) for z in rang...  25.5 us
    ppermute x6, waiting for transfers between devices, along_y(): lax.ppermute(x, 'ctx', [(4 * z + y, 4 * z + (y + by) % 4) for z in range(...  22.3 us
    pallas_call x2, Pallas kernels, backward(): pl.pallas_call(functools.partial(backward_kernel, shifts, first), out_sha...  16.8 us
    pallas_call x2, Pallas kernels, forward(): pl.pallas_call(functools.partial(forward_kernel, shifts, first), out_shap...  15 us
    pallas_call x2, Pallas kernels, pack(): pl.pallas_call(pack_kernel, out_shape=[jax.ShapeDtypeStruct((SENT, HALF),...  7.12 us
    ppermute x6, starting transfers between devices, along_y(): lax.ppermute(x, 'ctx', [(4 * z + y, 4 * z + (y + by) % 4) for z in range(...  6.58 us
    ppermute x8, starting transfers between devices, swap(): return lax.ppermute(x, 'section', [(i, i ^ 1) for i in range(8)])  5.31 us
    ppermute x18, waiting for transfers between devices, along_z(): lax.ppermute(x, 'ctx', [(4 * z + y, 4 * ((z + by) % 4) + y) for z in rang...  5.25 us
  transfers between devices with their start and end apart: 33, of which 11 were waited for; matrix products, arithmetic and copies ran while one was open for 1% of the time, Pallas kernels for 35%

profile of v2, /device:TPU:1, one launch (start us, length us, event | category | flops | bytes accessed | tf_op | source)
XLA Modules:
  0.0 126.3 jit_solution(10187475068482573118)
XLA Ops:
  0.6 1.5 %collective-permute-start = (bf16[128,1024]{1,0:T(8,128)(2,1)}, bf16[128,1024]{1,0:T(8,128)(2,1)S(1)}, u32[]{:S(2)}, u32[]{:S(2)}) collective-permute-start(bf16[128,1024]{1,0:T(8,128)(2,1)} %bitcast.33), channel_id=1, source_target_pairs={{0,16},{16,0},{32,48},{48,32},{64,80},{80,64},{96,112},{112,96},{1... | collective-permute-start | bytes 786440 | tf_op jit(solution)/shard_map/ppermute | solution.py:502
  2.1 0.1 collective-permute-start.1
  2.9 0.7 compare_select_fusion.sel
  3.5 0.4 collective-permute-start.2
  4.0 0.8 collective-permute-done.2.sel_in
  4.8 0.0 collective-permute-done.k_in
  4.8 0.4 collective-permute-start.3
  5.2 0.2 collective-permute-start.7
  5.4 0.9 copy-done.1
  6.3 0.9 copy-done.2
  7.3 0.3 pack_kv.1
  7.5 1.8 %collective-permute-start.4 = (bf16[176,256]{1,0:T(8,128)(2,1)S(1)}, bf16[176,256]{1,0:T(8,128)(2,1)S(1)}, u32[]{:S(2)}, u32[]{:S(2)}) collective-permute-start(bf16[176,256]{1,0:T(8,128)(2,1)S(1)} %get-tuple-element.101), channel_id=1, source_target_pairs={{0,4},{1,5},{2,6},{3,7},{4,8},{5,9},{6,10},{7,11},{8,12},{9,13},{1... | collective-permute-start | bytes 270344 | tf_op jit(solution)/shard_map/ppermute | solution.py:494
  9.3 3.3 %collective-permute-start.5 = (bf16[176,256]{1,0:T(8,128)(2,1)S(1)}, bf16[176,256]{1,0:T(8,128)(2,1)S(1)}, u32[]{:S(2)}, u32[]{:S(2)}) collective-permute-start(bf16[176,256]{1,0:T(8,128)(2,1)S(1)} %get-tuple-element.102), channel_id=1, source_target_pairs={{0,8},{1,9},{2,10},{3,11},{4,12},{5,13},{6,14},{7,15},{8,0},{9,1},... | collective-permute-start | bytes 270344 | tf_op jit(solution)/shard_map/ppermute | solution.py:494
  12.6 0.7 collective-permute-start.6
  13.4 3.5 %pack.2 = (bf16[160,1024]{1,0:T(8,128)(2,1)}, bf16[160,1024]{1,0:T(8,128)(2,1)}, bf16[160,1024]{1,0:T(8,128)(2,1)}, bf16[160,1024]{1,0:T(8,128)(2,1)}) custom-call(bf16[128,8192]{1,0:T(8,128)(2,1)} %bitcast.40, bf16[128,8192]{1,0:T(8,128)(2,1)} %collective-permute-done.3.come, s32[1,128]{1,0:T(1,128)} %copy-done.3, s32[1,128]{1,0:T(1,128)} %copy-done.5), custom_call_target="tpu_custom_call" | custom-call | tf_op jit(solution)/shard_map/pack/pallas_call | solution.py:210
  16.9 0.1 collective-permute-done.5
  17.0 1.3 %copy-done.8 = bf16[128,8192]{1,0:T(8,128)(2,1)} copy-done((bf16[128,8192]{1,0:T(8,128)(2,1)}, bf16[128,8192]{1,0:T(8,128)(2,1)S(1)}, u32[]{:S(2)}) %copy-start.8) | copy-done | bytes 2097176
  18.4 2.8 %collective-permute-start.10 = (bf16[4,176,256]{2,1,0:T(8,128)(2,1)S(1)}, bf16[4,176,256]{2,1,0:T(8,128)(2,1)S(1)}, u32[]{:S(2)}, u32[]{:S(2)}) collective-permute-start(bf16[4,176,256]{2,1,0:T(8,128)(2,1)S(1)} %pad_maximum_fusion.2.refs_1_), channel_id=1, source_target_pairs={{0,3},{1,0},{2,1},{3,2},{4,7},{5,4},{6,5},{7,6},{8,11},{9,8},{10,9... | collective-permute-start | bytes 1081352 | tf_op jit(solution)/shard_map/ppermute | solution.py:498
  21.2 0.3 collective-permute-start.9
  21.5 0.7 collective-permute-start.8
  22.2 0.1 pad_add_fusion.info
  22.3 1.2 collective-permute-start.11
  23.5 1.5 %collective-permute-start.12 = (bf16[160,1024]{1,0:T(8,128)(2,1)}, bf16[160,1024]{1,0:T(8,128)(2,1)S(1)}, u32[]{:S(2)}, u32[]{:S(2)}) collective-permute-start(bf16[160,1024]{1,0:T(8,128)(2,1)} %get-tuple-element.117), channel_id=1, source_target_pairs={{0,12},{1,13},{2,14},{3,15},{4,0},{5,1},{6,2},{7,3},{8,4},{9,5},{1... | collective-permute-start | bytes 983048 | tf_op jit(solution)/shard_map/ppermute | solution.py:494
  25.0 3.6 %pack.3 = (bf16[160,1024]{1,0:T(8,128)(2,1)}, bf16[160,1024]{1,0:T(8,128)(2,1)}, bf16[160,1024]{1,0:T(8,128)(2,1)}, bf16[160,1024]{1,0:T(8,128)(2,1)}) custom-call(bf16[128,8192]{1,0:T(8,128)(2,1)} %bitcast.42, bf16[128,8192]{1,0:T(8,128)(2,1)} %copy-done.8, s32[1,128]{1,0:T(1,128)} %copy-done.3, s32[1,128]{1,0:T(1,128)} %copy-done.5), custom_call_target="tpu_custom_call" | custom-call | tf_op jit(solution)/shard_map/pack/pallas_call | solution.py:210
  28.6 0.2 collective-permute-done.10.refs_4_
  28.8 1.3 %collective-permute-start.13 = (bf16[160,1024]{1,0:T(8,128)(2,1)S(1)}, bf16[160,1024]{1,0:T(8,128)(2,1)S(1)}, u32[]{:S(2)}, u32[]{:S(2)}) collective-permute-start(bf16[160,1024]{1,0:T(8,128)(2,1)S(1)} %copy-done.9), channel_id=1, source_target_pairs={{0,8},{1,9},{2,10},{3,11},{4,12},{5,13},{6,14},{7,15},{8,0},{9,1},... | collective-permute-start | bytes 983048 | tf_op jit(solution)/shard_map/ppermute | solution.py:494
  30.1 1.2 collective-permute-done.9.refs_3_
  31.2 1.5 %collective-permute-start.17 = (bf16[160,1024]{1,0:T(8,128)(2,1)}, bf16[160,1024]{1,0:T(8,128)(2,1)S(1)}, u32[]{:S(2)}, u32[]{:S(2)}) collective-permute-start(bf16[160,1024]{1,0:T(8,128)(2,1)} %get-tuple-element.132), channel_id=1, source_target_pairs={{0,4},{1,5},{2,6},{3,7},{4,8},{5,9},{6,10},{7,11},{8,12},{9,13},{1... | collective-permute-start | bytes 983048 | tf_op jit(solution)/shard_map/ppermute | solution.py:494
  32.7 8.0 %collective-permute-done.8.refs_2_ = bf16[4,176,256]{2,1,0:T(8,128)(2,1)S(1)} collective-permute-done((bf16[4,176,256]{2,1,0:T(8,128)(2,1)S(1)}, bf16[4,176,256]{2,1,0:T(8,128)(2,1)S(1)}, u32[]{:S(2)}, u32[]{:S(2)}) %collective-permute-start.8) | collective-permute-done | bytes 360480 | tf_op jit(solution)/shard_map/ppermute | solution.py:498
  40.7 1.4 %collective-permute-start.18 = (bf16[160,1024]{1,0:T(8,128)(2,1)}, bf16[160,1024]{1,0:T(8,128)(2,1)S(1)}, u32[]{:S(2)}, u32[]{:S(2)}) collective-permute-start(bf16[160,1024]{1,0:T(8,128)(2,1)} %get-tuple-element.133), channel_id=1, source_target_pairs={{0,12},{1,13},{2,14},{3,15},{4,0},{5,1},{6,2},{7,3},{8,4},{9,5},{1... | collective-permute-start | bytes 983048 | tf_op jit(solution)/shard_map/ppermute | solution.py:494
  42.1 2.9 %forward.2 = (bf16[160,1024]{1,0:T(8,128)(2,1)S(1)}, bf16[2048,1024]{1,0:T(8,128)(2,1)S(1)}, f32[8,1024]{1,0:T(8,128)S(1)}, f32[128,1024]{1,0:T(8,128)S(1)}, bf1...) custom-call(s32[3]{0:T(128)S(1)} %pad_add_fusion.info, ...), custom_call_target="tpu_custom_call" | custom-call | flops 4000000000 | bytes 4194304 | tf_op jit(solution)/shard_map/forward/pallas_call | solution.py:318
  45.0 3.7 %collective-permute-start.21 = (bf16[160,1024]{1,0:T(8,128)(2,1)S(1)}, bf16[160,1024]{1,0:T(8,128)(2,1)S(1)}, u32[]{:S(2)}, u32[]{:S(2)}) collective-permute-start(bf16[160,1024]{1,0:T(8,128)(2,1)S(1)} %copy-done.10), channel_id=1, source_target_pairs={{0,8},{1,9},{2,10},{3,11},{4,12},{5,13},{6,14},{7,15},{8,0},{9,1},... | collective-permute-start | bytes 983048 | tf_op jit(solution)/shard_map/ppermute | solution.py:494
  48.8 12.1 %forward.3 = (bf16[160,1024]{1,0:T(8,128)(2,1)S(1)}, bf16[2048,1024]{1,0:T(8,128)(2,1)S(1)}, f32[8,1024]{1,0:T(8,128)S(1)}, f32[128,1024]{1,0:T(8,128)S(1)}, bf1...) custom-call(s32[3]{0:T(128)S(1)} %pad_add_fusion.info, ...), custom_call_target="tpu_custom_call" | custom-call | flops 12000000000 | bytes 4194304 | tf_op jit(solution)/shard_map/forward/pallas_call | solution.py:318
  60.9 0.1 collective-permute-start.14
  61.0 1.2 collective-permute-start.15
  62.2 0.2 collective-permute-start.16
  62.4 9.6 %backward.2 = (bf16[160,1024]{1,0:T(8,128)(2,1)S(1)}, bf16[160,1024]{1,0:T(8,128)(2,1)S(1)}, f32[2048,128]{1,0:T(8,128)S(1)}, f32[2048,128]{1,0:T(8,128)S(1)}, f...) custom-call(s32[3]{0:T(128)S(1)} %pad_add_fusion.info, bf16[160,1024]{1,0:T(8,128)(2,1)S(1)} %collective-permute-done.11.refs_0_, ...), custom_call_target="tpu_custom_call" | custom-call | flops 12000000000 | bytes 4194304 | tf_op jit(solution)/shard_map/backward/pallas_call | solution.py:369
  72.0 0.1 collective-permute-start.19
  72.1 1.4 %collective-permute-start.20 = (bf16[160,1024]{1,0:T(8,128)(2,1)S(1)}, bf16[160,1024]{1,0:T(8,128)(2,1)S(1)}, u32[]{:S(2)}, u32[]{:S(2)}) collective-permute-start(bf16[160,1024]{1,0:T(8,128)(2,1)S(1)} %get-tuple-element.147), channel_id=1, source_target_pairs={{0,4},{1,5},{2,6},{3,7},{4,8},{5,9},{6,10},{7,11},{8,12},{9,13},{1... | collective-permute-start | bytes 983048 | tf_op jit(solution)/shard_map/ppermute | solution.py:494
  73.6 7.3 %backward.3 = (bf16[160,1024]{1,0:T(8,128)(2,1)S(1)}, bf16[160,1024]{1,0:T(8,128)(2,1)S(1)}, bf16[4,160,256]{2,1,0:T(8,128)(2,1)S(1)}, bf16[4,160,256]{2,1,0:T(8...) custom-call(s32[3]{0:T(128)S(1)} %pad_add_fusion.info, ...), custom_call_target="tpu_custom_call" | custom-call | flops 12000000000 | bytes 4194304 | tf_op jit(solution)/shard_map/backward/pallas_call | solution.py:369
  80.9 2.8 %collective-permute-done.19 = bf16[160,1024]{1,0:T(8,128)(2,1)S(1)} collective-permute-done((bf16[160,1024]{1,0:T(8,128)(2,1)S(1)}, bf16[160,1024]{1,0:T(8,128)(2,1)S(1)}, u32[]{:S(2)}, u32[]{:S(2)}) %collective-permute-start.19) | collective-permute-done | bytes 327712 | tf_op jit(solution)/shard_map/ppermute | solution.py:494
  83.6 2.4 %collective-permute-done.20 = bf16[160,1024]{1,0:T(8,128)(2,1)S(1)} collective-permute-done((bf16[160,1024]{1,0:T(8,128)(2,1)S(1)}, bf16[160,1024]{1,0:T(8,128)(2,1)S(1)}, u32[]{:S(2)}, u32[]{:S(2)}) %collective-permute-start.20) | collective-permute-done | bytes 327712 | tf_op jit(solution)/shard_map/ppermute | solution.py:494
  86.0 0.2 pad_maximum_fusion.mine
  86.2 1.0 collective-permute-start.22
  87.2 2.7 %collective-permute-done.22.theirs = bf16[4,160,1024]{2,1,0:T(8,128)(2,1)S(1)} collective-permute-done((bf16[4,160,1024]{2,1,0:T(8,128)(2,1)S(1)}, bf16[4,160,1024]{2,1,0:T(8,128)(2,1)S(1)}, u32[]{:S(2)}, u32[]{:S(2)}) %collective-permute-start.22) | collective-permute-done | bytes 1310752 | tf_op jit(solution)/shard_map/ppermute | solution.py:502
  89.9 1.5 %update.1 = bf16[128,8192]{1,0:T(8,128)(2,1)S(1)} custom-call(s32[3]{0:T(128)S(1)} %pad_add_fusion.info, bf16[128,8192]{1,0:T(8,128)(2,1)S(1)} %bitcast.30, bf16[4,160,1024]{2,1,0:T(8,128)(2,1)S(1)} %pad_maximum_fusion.mine, bf16[4,160,1024]{2,1,0:T(8,128)(2,1)S(1)} %collective-permute-done.22.theirs, s32[1,128]{1,0:T(1,128)S(1)} %copy-done.4), custom_call_target="tpu_custom_call" | custom-call | tf_op jit(solution)/shard_map/update/pallas_call | solution.py:431
  91.4 4.0 %collective-permute-start.23 = (bf16[128,8192]{1,0:T(8,128)(2,1)S(1)}, bf16[128,8192]{1,0:T(8,128)(2,1)S(1)}, u32[]{:S(2)}, u32[]{:S(2)}) collective-permute-start(bf16[128,8192]{1,0:T(8,128)(2,1)S(1)} %update.1), channel_id=1, source_target_pairs={{0,16},{16,32},{32,48},{48,64},{64,80},{80,96},{96,112},{1,17},{17... | collective-permute-start | bytes 6291464 | tf_op jit(solution)/shard_map/ppermute | solution.py:506
  95.4 0.1 collective-permute-start.25
  95.5 1.5 %collective-permute-start.26 = (bf16[4,160,256]{2,1,0:T(8,128)(2,1)S(1)}, bf16[4,160,256]{2,1,0:T(8,128)(2,1)S(1)}, u32[]{:S(2)}, u32[]{:S(2)}) collective-permute-start(bf16[4,160,256]{2,1,0:T(8,128)(2,1)S(1)} %get-tuple-element.175), channel_id=1, source_target_pairs={{0,2},{1,3},{2,0},{3,1},{4,6},{5,7},{6,4},{7,5},{8,10},{9,11},{10,... | collective-permute-start | bytes 983048 | tf_op jit(solution)/shard_map/ppermute | solution.py:498
  96.9 1.2 collective-permute-start.27
  98.1 2.0 %collective-permute-start.24 = (bf16[160,1024]{1,0:T(8,128)(2,1)S(1)}, bf16[160,1024]{1,0:T(8,128)(2,1)S(1)}, u32[]{:S(2)}, u32[]{:S(2)}) collective-permute-start(bf16[160,1024]{1,0:T(8,128)(2,1)S(1)} %get-tuple-element.172), channel_id=1, source_target_pairs={{0,8},{1,9},{2,10},{3,11},{4,12},{5,13},{6,14},{7,15},{8,0},{9,1},... | collective-permute-start | bytes 983048 | tf_op jit(solution)/shard_map/ppermute | solution.py:494
  100.1 12.0 %collective-permute-done.25.b = bf16[4,160,256]{2,1,0:T(8,128)(2,1)S(1)} collective-permute-done((bf16[4,160,256]{2,1,0:T(8,128)(2,1)S(1)}, bf16[4,160,256]{2,1,0:T(8,128)(2,1)S(1)}, u32[]{:S(2)}, u32[]{:S(2)}) %collective-permute-start.25) | collective-permute-done | bytes 327712 | tf_op jit(solution)/shard_map/ppermute | solution.py:498
  112.2 0.9 collective-permute-done.27.d
  113.1 0.2 fold_sums.1
  113.2 0.2 pad_maximum_fusion.1.mine
  113.4 0.1 collective-permute-start.28
  113.6 1.6 %collective-permute-start.29 = (bf16[160,256]{1,0:T(8,128)(2,1)S(1)}, bf16[160,256]{1,0:T(8,128)(2,1)S(1)}, u32[]{:S(2)}, u32[]{:S(2)}) collective-permute-start(bf16[160,256]{1,0:T(8,128)(2,1)S(1)} %get-tuple-element.181), channel_id=1, source_target_pairs={{0,4},{1,5},{2,6},{3,7},{4,8},{5,9},{6,10},{7,11},{8,12},{9,13},{1... | collective-permute-start | bytes 245768 | tf_op jit(solution)/shard_map/ppermute | solution.py:494
  115.2 1.7 %collective-permute-start.30 = (bf16[160,256]{1,0:T(8,128)(2,1)S(1)}, bf16[160,256]{1,0:T(8,128)(2,1)S(1)}, u32[]{:S(2)}, u32[]{:S(2)}) collective-permute-start(bf16[160,256]{1,0:T(8,128)(2,1)S(1)} %get-tuple-element.182), channel_id=1, source_target_pairs={{0,8},{1,9},{2,10},{3,11},{4,12},{5,13},{6,14},{7,15},{8,0},{9,1},... | collective-permute-start | bytes 245768 | tf_op jit(solution)/shard_map/ppermute | solution.py:494
  116.9 0.7 collective-permute-start.31
  117.6 2.4 %finish_q.1 = bf16[128,8192]{1,0:T(8,128)(2,1)} custom-call(s32[3]{0:T(128)S(1)} %pad_add_fusion.info, bf16[4,160,1024]{2,1,0:T(8,128)(2,1)S(1)} %pad_maximum_fusion.1.mine, bf16[4,160,1024]{2,1,0:T(8,128)(2,1)S(1)} %collective-permute-done.28.theirs, s32[1,128]{1,0:T(1,128)S(1)} %copy-done.4), custom_call_target="tpu_custom_call" | custom-call | tf_op jit(solution)/shard_map/finish_q/pallas_call | solution.py:431
  120.1 1.9 %settle.1 = bf16[128,8192]{1,0:T(8,128)(2,1)} custom-call(bf16[128,8192]{1,0:T(8,128)(2,1)S(1)} %collective-permute-done.23.x), custom_call_target="tpu_custom_call" | custom-call | tf_op jit(solution)/shard_map/settle/pallas_call | solution.py:451
  122.1 1.6 %collective-permute-start.32 = (bf16[4,160,256]{2,1,0:T(8,128)(2,1)S(1)}, bf16[4,160,256]{2,1,0:T(8,128)(2,1)S(1)}, u32[]{:S(2)}, u32[]{:S(2)}) collective-permute-start(bf16[4,160,256]{2,1,0:T(8,128)(2,1)S(1)} %pad_maximum_fusion.3.sums), channel_id=1, source_target_pairs={{0,16},{16,0},{32,48},{48,32},{64,80},{80,64},{96,112},{112,96},{1... | collective-permute-start | bytes 983048 | tf_op jit(solution)/shard_map/ppermute | solution.py:502
  123.6 1.3 collective-permute-done.32.sums_in
  124.9 1.4 %finish_kv.1 = (bf16[128,1024]{1,0:T(8,128)(2,1)}, bf16[128,1024]{1,0:T(8,128)(2,1)}) custom-call(s32[3]{0:T(128)S(1)} %pad_add_fusion.info, bf16[4,160,256]{2,1,0:T(8,128)(2,1)S(1)} %pad_maximum_fusion.3.sums, bf16[4,160,256]{2,1,0:T(8,128)(2,1)S(1)} %collective-permute-done.32.sums_in, s32[1,128]{1,0:T(1,128)S(1)} %copy-done.4), custom_call_target="tpu_custom_call" | custom-call | tf_op jit(solution)/shard_map/finish_kv/pallas_call | solution.py:483
  (42 shorter events, 0.2 us)
Async XLA Ops:
  0.6 4.2 %collective-permute-start = (bf16[128,1024]{1,0:T(8,128)(2,1)}, bf16[128,1024]{1,0:T(8,128)(2,1)S(1)}, u32[]{:S(2)}, u32[]{:S(2)}) collective-permute-start(bf16[128,1024]{1,0:T(8,128)(2,1)} %bitcast.33), channel_id=1, source_target_pairs={{0,16},{16,0},{32,48},{48,32},{64,80},{80,64},{96,112},{112,96},{1... | collective-permute-start | bytes 786440 | tf_op jit(solution)/shard_map/ppermute | solution.py:502
  2.1 2.7 %collective-permute-start.1 = (bf16[128,1024]{1,0:T(8,128)(2,1)}, bf16[128,1024]{1,0:T(8,128)(2,1)S(1)}, u32[]{:S(2)}, u32[]{:S(2)}) collective-permute-start(bf16[128,1024]{1,0:T(8,128)(2,1)} %bitcast.35), channel_id=1, source_target_pairs={{0,16},{16,0},{32,48},{48,32},{64,80},{80,64},{96,112},{112,96},{1... | collective-permute-start | bytes 786440 | tf_op jit(solution)/shard_map/ppermute | solution.py:502
  3.5 9.8 %copy-start.3 = (s32[1,128]{1,0:T(1,128)}, s32[1,128]{1,0:T(1,128)S(1)}, u32[]{:S(2)}) copy-start(s32[1,128]{1,0:T(1,128)S(1)} %compare_select_fusion.sel) | copy-start | bytes 1540
  3.5 1.2 collective-permute-start.2
  4.8 8.6 %copy-start.5 = (s32[1,128]{1,0:T(1,128)}, s32[1,128]{1,0:T(1,128)S(1)}, u32[]{:S(2)}) copy-start(s32[1,128]{1,0:T(1,128)S(1)} %collective-permute-done.2.sel_in) | copy-start | bytes 1540
  4.8 8.6 %collective-permute-start.3 = (bf16[128,8192]{1,0:T(8,128)(2,1)}, bf16[128,8192]{1,0:T(8,128)(2,1)}, u32[]{:S(2)}, u32[]{:S(2)}) collective-permute-start(bf16[128,8192]{1,0:T(8,128)(2,1)} %bitcast.39), channel_id=1, source_target_pairs={{0,16},{16,0},{32,48},{48,32},{64,80},{80,64},{96,112},{112,96},{1... | collective-permute-start | bytes 6291464 | tf_op jit(solution)/shard_map/ppermute | solution.py:502
  5.2 11.8 %collective-permute-start.7 = (bf16[128,8192]{1,0:T(8,128)(2,1)}, bf16[128,8192]{1,0:T(8,128)(2,1)S(1)}, u32[]{:S(2)}, u32[]{:S(2)}) collective-permute-start(bf16[128,8192]{1,0:T(8,128)(2,1)} %bitcast.41), channel_id=1, source_target_pairs={{0,16},{16,0},{32,48},{48,32},{64,80},{80,64},{96,112},{112,96},{1... | collective-permute-start | bytes 6291464 | tf_op jit(solution)/shard_map/ppermute | solution.py:502
  5.4 0.9 copy-start.1
  6.3 0.9 copy-start.2
  7.5 9.4 %collective-permute-start.4 = (bf16[176,256]{1,0:T(8,128)(2,1)S(1)}, bf16[176,256]{1,0:T(8,128)(2,1)S(1)}, u32[]{:S(2)}, u32[]{:S(2)}) collective-permute-start(bf16[176,256]{1,0:T(8,128)(2,1)S(1)} %get-tuple-element.101), channel_id=1, source_target_pairs={{0,4},{1,5},{2,6},{3,7},{4,8},{5,9},{6,10},{7,11},{8,12},{9,13},{1... | collective-permute-start | bytes 270344 | tf_op jit(solution)/shard_map/ppermute | solution.py:494
  9.3 7.7 %collective-permute-start.5 = (bf16[176,256]{1,0:T(8,128)(2,1)S(1)}, bf16[176,256]{1,0:T(8,128)(2,1)S(1)}, u32[]{:S(2)}, u32[]{:S(2)}) collective-permute-start(bf16[176,256]{1,0:T(8,128)(2,1)S(1)} %get-tuple-element.102), channel_id=1, source_target_pairs={{0,8},{1,9},{2,10},{3,11},{4,12},{5,13},{6,14},{7,15},{8,0},{9,1},... | collective-permute-start | bytes 270344 | tf_op jit(solution)/shard_map/ppermute | solution.py:494
  12.6 4.4 %collective-permute-start.6 = (bf16[176,256]{1,0:T(8,128)(2,1)S(1)}, bf16[176,256]{1,0:T(8,128)(2,1)S(1)}, u32[]{:S(2)}, u32[]{:S(2)}) collective-permute-start(bf16[176,256]{1,0:T(8,128)(2,1)S(1)} %get-tuple-element.103), channel_id=1, source_target_pairs={{0,12},{1,13},{2,14},{3,15},{4,0},{5,1},{6,2},{7,3},{8,4},{9,5},{1... | collective-permute-start | bytes 270344 | tf_op jit(solution)/shard_map/ppermute | solution.py:494
  17.0 1.3 %copy-start.8 = (bf16[128,8192]{1,0:T(8,128)(2,1)}, bf16[128,8192]{1,0:T(8,128)(2,1)S(1)}, u32[]{:S(2)}) copy-start(bf16[128,8192]{1,0:T(8,128)(2,1)S(1)} %collective-permute-done.7.come) | copy-start | bytes 6291460
  18.4 10.4 %collective-permute-start.10 = (bf16[4,176,256]{2,1,0:T(8,128)(2,1)S(1)}, bf16[4,176,256]{2,1,0:T(8,128)(2,1)S(1)}, u32[]{:S(2)}, u32[]{:S(2)}) collective-permute-start(bf16[4,176,256]{2,1,0:T(8,128)(2,1)S(1)} %pad_maximum_fusion.2.refs_1_), channel_id=1, source_target_pairs={{0,3},{1,0},{2,1},{3,2},{4,7},{5,4},{6,5},{7,6},{8,11},{9,8},{10,9... | collective-permute-start | bytes 1081352 | tf_op jit(solution)/shard_map/ppermute | solution.py:498
  21.2 10.1 %collective-permute-start.9 = (bf16[4,176,256]{2,1,0:T(8,128)(2,1)S(1)}, bf16[4,176,256]{2,1,0:T(8,128)(2,1)S(1)}, u32[]{:S(2)}, u32[]{:S(2)}) collective-permute-start(bf16[4,176,256]{2,1,0:T(8,128)(2,1)S(1)} %pad_maximum_fusion.2.refs_1_), channel_id=1, source_target_pairs={{0,2},{1,3},{2,0},{3,1},{4,6},{5,7},{6,4},{7,5},{8,10},{9,11},{10,... | collective-permute-start | bytes 1081352 | tf_op jit(solution)/shard_map/ppermute | solution.py:498
  21.5 19.2 %collective-permute-start.8 = (bf16[4,176,256]{2,1,0:T(8,128)(2,1)S(1)}, bf16[4,176,256]{2,1,0:T(8,128)(2,1)S(1)}, u32[]{:S(2)}, u32[]{:S(2)}) collective-permute-start(bf16[4,176,256]{2,1,0:T(8,128)(2,1)S(1)} %pad_maximum_fusion.2.refs_1_), channel_id=1, source_target_pairs={{0,1},{1,2},{2,3},{3,0},{4,5},{5,6},{6,7},{7,4},{8,9},{9,10},{10,1... | collective-permute-start | bytes 1081352 | tf_op jit(solution)/shard_map/ppermute | solution.py:498
  22.3 6.5 %copy-start.9 = (bf16[160,1024]{1,0:T(8,128)(2,1)S(1)}, bf16[160,1024]{1,0:T(8,128)(2,1)}, u32[]{:S(2)}) copy-start(bf16[160,1024]{1,0:T(8,128)(2,1)} %get-tuple-element.118) | copy-start | bytes 983044
  22.3 19.8 %copy-start.6 = (bf16[160,1024]{1,0:T(8,128)(2,1)S(1)}, bf16[160,1024]{1,0:T(8,128)(2,1)}, u32[]{:S(2)}) copy-start(bf16[160,1024]{1,0:T(8,128)(2,1)} %get-tuple-element.99.refs_0_) | copy-start | bytes 983044
  22.3 22.7 %collective-permute-start.11 = (bf16[160,1024]{1,0:T(8,128)(2,1)}, bf16[160,1024]{1,0:T(8,128)(2,1)S(1)}, u32[]{:S(2)}, u32[]{:S(2)}) collective-permute-start(bf16[160,1024]{1,0:T(8,128)(2,1)} %get-tuple-element.116), channel_id=1, source_target_pairs={{0,4},{1,5},{2,6},{3,7},{4,8},{5,9},{6,10},{7,11},{8,12},{9,13},{1... | collective-permute-start | bytes 983048 | tf_op jit(solution)/shard_map/ppermute | solution.py:494
  23.5 25.2 %collective-permute-start.12 = (bf16[160,1024]{1,0:T(8,128)(2,1)}, bf16[160,1024]{1,0:T(8,128)(2,1)S(1)}, u32[]{:S(2)}, u32[]{:S(2)}) collective-permute-start(bf16[160,1024]{1,0:T(8,128)(2,1)} %get-tuple-element.117), channel_id=1, source_target_pairs={{0,12},{1,13},{2,14},{3,15},{4,0},{5,1},{6,2},{7,3},{8,4},{9,5},{1... | collective-permute-start | bytes 983048 | tf_op jit(solution)/shard_map/ppermute | solution.py:494
  28.8 20.0 %collective-permute-start.13 = (bf16[160,1024]{1,0:T(8,128)(2,1)S(1)}, bf16[160,1024]{1,0:T(8,128)(2,1)S(1)}, u32[]{:S(2)}, u32[]{:S(2)}) collective-permute-start(bf16[160,1024]{1,0:T(8,128)(2,1)S(1)} %copy-done.9), channel_id=1, source_target_pairs={{0,8},{1,9},{2,10},{3,11},{4,12},{5,13},{6,14},{7,15},{8,0},{9,1},... | collective-permute-start | bytes 983048 | tf_op jit(solution)/shard_map/ppermute | solution.py:494
  31.2 31.0 %collective-permute-start.17 = (bf16[160,1024]{1,0:T(8,128)(2,1)}, bf16[160,1024]{1,0:T(8,128)(2,1)S(1)}, u32[]{:S(2)}, u32[]{:S(2)}) collective-permute-start(bf16[160,1024]{1,0:T(8,128)(2,1)} %get-tuple-element.132), channel_id=1, source_target_pairs={{0,4},{1,5},{2,6},{3,7},{4,8},{5,9},{6,10},{7,11},{8,12},{9,13},{1... | collective-permute-start | bytes 983048 | tf_op jit(solution)/shard_map/ppermute | solution.py:494
  40.7 21.7 %collective-permute-start.18 = (bf16[160,1024]{1,0:T(8,128)(2,1)}, bf16[160,1024]{1,0:T(8,128)(2,1)S(1)}, u32[]{:S(2)}, u32[]{:S(2)}) collective-permute-start(bf16[160,1024]{1,0:T(8,128)(2,1)} %get-tuple-element.133), channel_id=1, source_target_pairs={{0,12},{1,13},{2,14},{3,15},{4,0},{5,1},{6,2},{7,3},{8,4},{9,5},{1... | collective-permute-start | bytes 983048 | tf_op jit(solution)/shard_map/ppermute | solution.py:494
  42.1 2.9 %copy-start.10 = (bf16[160,1024]{1,0:T(8,128)(2,1)S(1)}, bf16[160,1024]{1,0:T(8,128)(2,1)}, u32[]{:S(2)}) copy-start(bf16[160,1024]{1,0:T(8,128)(2,1)} %get-tuple-element.149) | copy-start | bytes 983044
  45.0 27.1 %collective-permute-start.21 = (bf16[160,1024]{1,0:T(8,128)(2,1)S(1)}, bf16[160,1024]{1,0:T(8,128)(2,1)S(1)}, u32[]{:S(2)}, u32[]{:S(2)}) collective-permute-start(bf16[160,1024]{1,0:T(8,128)(2,1)S(1)} %copy-done.10), channel_id=1, source_target_pairs={{0,8},{1,9},{2,10},{3,11},{4,12},{5,13},{6,14},{7,15},{8,0},{9,1},... | collective-permute-start | bytes 983048 | tf_op jit(solution)/shard_map/ppermute | solution.py:494
  60.9 19.9 %collective-permute-start.14 = (bf16[160,1024]{1,0:T(8,128)(2,1)S(1)}, bf16[160,1024]{1,0:T(8,128)(2,1)S(1)}, u32[]{:S(2)}, u32[]{:S(2)}) collective-permute-start(bf16[160,1024]{1,0:T(8,128)(2,1)S(1)} %get-tuple-element.128), channel_id=1, source_target_pairs={{0,12},{1,13},{2,14},{3,15},{4,0},{5,1},{6,2},{7,3},{8,4},{9,5},{1... | collective-permute-start | bytes 983048 | tf_op jit(solution)/shard_map/ppermute | solution.py:494
  61.0 19.9 %collective-permute-start.15 = (bf16[160,1024]{1,0:T(8,128)(2,1)S(1)}, bf16[160,1024]{1,0:T(8,128)(2,1)S(1)}, u32[]{:S(2)}, u32[]{:S(2)}) collective-permute-start(bf16[160,1024]{1,0:T(8,128)(2,1)S(1)} %get-tuple-element.129), channel_id=1, source_target_pairs={{0,8},{1,9},{2,10},{3,11},{4,12},{5,13},{6,14},{7,15},{8,0},{9,1},... | collective-permute-start | bytes 983048 | tf_op jit(solution)/shard_map/ppermute | solution.py:494
  62.2 18.6 %collective-permute-start.16 = (bf16[160,1024]{1,0:T(8,128)(2,1)S(1)}, bf16[160,1024]{1,0:T(8,128)(2,1)S(1)}, u32[]{:S(2)}, u32[]{:S(2)}) collective-permute-start(bf16[160,1024]{1,0:T(8,128)(2,1)S(1)} %get-tuple-element.130), channel_id=1, source_target_pairs={{0,4},{1,5},{2,6},{3,7},{4,8},{5,9},{6,10},{7,11},{8,12},{9,13},{1... | collective-permute-start | bytes 983048 | tf_op jit(solution)/shard_map/ppermute | solution.py:494
  62.4 11.1 %copy-start.7 = (bf16[160,1024]{1,0:T(8,128)(2,1)S(1)}, bf16[160,1024]{1,0:T(8,128)(2,1)}, u32[]{:S(2)}) copy-start(bf16[160,1024]{1,0:T(8,128)(2,1)} %get-tuple-element.148.refs_2_) | copy-start | bytes 983044
  72.0 11.6 %collective-permute-start.19 = (bf16[160,1024]{1,0:T(8,128)(2,1)S(1)}, bf16[160,1024]{1,0:T(8,128)(2,1)S(1)}, u32[]{:S(2)}, u32[]{:S(2)}) collective-permute-start(bf16[160,1024]{1,0:T(8,128)(2,1)S(1)} %get-tuple-element.146), channel_id=1, source_target_pairs={{0,12},{1,13},{2,14},{3,15},{4,0},{5,1},{6,2},{7,3},{8,4},{9,5},{1... | collective-permute-start | bytes 983048 | tf_op jit(solution)/shard_map/ppermute | solution.py:494
  72.1 13.9 %collective-permute-start.20 = (bf16[160,1024]{1,0:T(8,128)(2,1)S(1)}, bf16[160,1024]{1,0:T(8,128)(2,1)S(1)}, u32[]{:S(2)}, u32[]{:S(2)}) collective-permute-start(bf16[160,1024]{1,0:T(8,128)(2,1)S(1)} %get-tuple-element.147), channel_id=1, source_target_pairs={{0,4},{1,5},{2,6},{3,7},{4,8},{5,9},{6,10},{7,11},{8,12},{9,13},{1... | collective-permute-start | bytes 983048 | tf_op jit(solution)/shard_map/ppermute | solution.py:494
  86.0 3.9 %copy-start = (bf16[1,128,8192]{2,1,0:T(8,128)(2,1)S(1)}, bf16[1,128,8192]{2,1,0:T(8,128)(2,1)}, u32[]{:S(2)}) copy-start(bf16[1,128,8192]{2,1,0:T(8,128)(2,1)} %param.7) | copy-start | bytes 6291460
  86.0 3.9 %copy-start.4 = (s32[1,128]{1,0:T(1,128)S(1)}, s32[1,128]{1,0:T(1,128)}, u32[]{:S(2)}) copy-start(s32[1,128]{1,0:T(1,128)} %copy-done.3) | copy-start | bytes 1540
  86.2 3.7 %collective-permute-start.22 = (bf16[4,160,1024]{2,1,0:T(8,128)(2,1)S(1)}, bf16[4,160,1024]{2,1,0:T(8,128)(2,1)S(1)}, u32[]{:S(2)}, u32[]{:S(2)}) collective-permute-start(bf16[4,160,1024]{2,1,0:T(8,128)(2,1)S(1)} %pad_maximum_fusion.mine), channel_id=1, source_target_pairs={{0,16},{16,0},{32,48},{48,32},{64,80},{80,64},{96,112},{112,96},{1... | collective-permute-start | bytes 3932168 | tf_op jit(solution)/shard_map/ppermute | solution.py:502
  91.4 28.7 %collective-permute-start.23 = (bf16[128,8192]{1,0:T(8,128)(2,1)S(1)}, bf16[128,8192]{1,0:T(8,128)(2,1)S(1)}, u32[]{:S(2)}, u32[]{:S(2)}) collective-permute-start(bf16[128,8192]{1,0:T(8,128)(2,1)S(1)} %update.1), channel_id=1, source_target_pairs={{0,16},{16,32},{32,48},{48,64},{64,80},{80,96},{96,112},{1,17},{17... | collective-permute-start | bytes 6291464 | tf_op jit(solution)/shard_map/ppermute | solution.py:506
  95.4 16.8 %collective-permute-start.25 = (bf16[4,160,256]{2,1,0:T(8,128)(2,1)S(1)}, bf16[4,160,256]{2,1,0:T(8,128)(2,1)S(1)}, u32[]{:S(2)}, u32[]{:S(2)}) collective-permute-start(bf16[4,160,256]{2,1,0:T(8,128)(2,1)S(1)} %get-tuple-element.174), channel_id=1, source_target_pairs={{0,1},{1,2},{2,3},{3,0},{4,5},{5,6},{6,7},{7,4},{8,9},{9,10},{10,1... | collective-permute-start | bytes 983048 | tf_op jit(solution)/shard_map/ppermute | solution.py:498
  95.5 16.7 %collective-permute-start.26 = (bf16[4,160,256]{2,1,0:T(8,128)(2,1)S(1)}, bf16[4,160,256]{2,1,0:T(8,128)(2,1)S(1)}, u32[]{:S(2)}, u32[]{:S(2)}) collective-permute-start(bf16[4,160,256]{2,1,0:T(8,128)(2,1)S(1)} %get-tuple-element.175), channel_id=1, source_target_pairs={{0,2},{1,3},{2,0},{3,1},{4,6},{5,7},{6,4},{7,5},{8,10},{9,11},{10,... | collective-permute-start | bytes 983048 | tf_op jit(solution)/shard_map/ppermute | solution.py:498
  96.9 16.1 %collective-permute-start.27 = (bf16[4,160,256]{2,1,0:T(8,128)(2,1)S(1)}, bf16[4,160,256]{2,1,0:T(8,128)(2,1)S(1)}, u32[]{:S(2)}, u32[]{:S(2)}) collective-permute-start(bf16[4,160,256]{2,1,0:T(8,128)(2,1)S(1)} %get-tuple-element.176), channel_id=1, source_target_pairs={{0,3},{1,0},{2,1},{3,2},{4,7},{5,4},{6,5},{7,6},{8,11},{9,8},{10,9... | collective-permute-start | bytes 983048 | tf_op jit(solution)/shard_map/ppermute | solution.py:498
  98.1 15.1 %collective-permute-start.24 = (bf16[160,1024]{1,0:T(8,128)(2,1)S(1)}, bf16[160,1024]{1,0:T(8,128)(2,1)S(1)}, u32[]{:S(2)}, u32[]{:S(2)}) collective-permute-start(bf16[160,1024]{1,0:T(8,128)(2,1)S(1)} %get-tuple-element.172), channel_id=1, source_target_pairs={{0,8},{1,9},{2,10},{3,11},{4,12},{5,13},{6,14},{7,15},{8,0},{9,1},... | collective-permute-start | bytes 983048 | tf_op jit(solution)/shard_map/ppermute | solution.py:494
  113.4 4.2 %collective-permute-start.28 = (bf16[4,160,1024]{2,1,0:T(8,128)(2,1)S(1)}, bf16[4,160,1024]{2,1,0:T(8,128)(2,1)S(1)}, u32[]{:S(2)}, u32[]{:S(2)}) collective-permute-start(bf16[4,160,1024]{2,1,0:T(8,128)(2,1)S(1)} %pad_maximum_fusion.1.mine), channel_id=1, source_target_pairs={{0,16},{16,0},{32,48},{48,32},{64,80},{80,64},{96,112},{112,96},{1... | collective-permute-start | bytes 3932168 | tf_op jit(solution)/shard_map/ppermute | solution.py:502
  113.6 8.5 %collective-permute-start.29 = (bf16[160,256]{1,0:T(8,128)(2,1)S(1)}, bf16[160,256]{1,0:T(8,128)(2,1)S(1)}, u32[]{:S(2)}, u32[]{:S(2)}) collective-permute-start(bf16[160,256]{1,0:T(8,128)(2,1)S(1)} %get-tuple-element.181), channel_id=1, source_target_pairs={{0,4},{1,5},{2,6},{3,7},{4,8},{5,9},{6,10},{7,11},{8,12},{9,13},{1... | collective-permute-start | bytes 245768 | tf_op jit(solution)/shard_map/ppermute | solution.py:494
  115.2 6.9 %collective-permute-start.30 = (bf16[160,256]{1,0:T(8,128)(2,1)S(1)}, bf16[160,256]{1,0:T(8,128)(2,1)S(1)}, u32[]{:S(2)}, u32[]{:S(2)}) collective-permute-start(bf16[160,256]{1,0:T(8,128)(2,1)S(1)} %get-tuple-element.182), channel_id=1, source_target_pairs={{0,8},{1,9},{2,10},{3,11},{4,12},{5,13},{6,14},{7,15},{8,0},{9,1},... | collective-permute-start | bytes 245768 | tf_op jit(solution)/shard_map/ppermute | solution.py:494
  116.9 5.1 %collective-permute-start.31 = (bf16[160,256]{1,0:T(8,128)(2,1)S(1)}, bf16[160,256]{1,0:T(8,128)(2,1)S(1)}, u32[]{:S(2)}, u32[]{:S(2)}) collective-permute-start(bf16[160,256]{1,0:T(8,128)(2,1)S(1)} %get-tuple-element.183), channel_id=1, source_target_pairs={{0,12},{1,13},{2,14},{3,15},{4,0},{5,1},{6,2},{7,3},{8,4},{9,5},{1... | collective-permute-start | bytes 245768 | tf_op jit(solution)/shard_map/ppermute | solution.py:494
  122.1 2.8 %collective-permute-start.32 = (bf16[4,160,256]{2,1,0:T(8,128)(2,1)S(1)}, bf16[4,160,256]{2,1,0:T(8,128)(2,1)S(1)}, u32[]{:S(2)}, u32[]{:S(2)}) collective-permute-start(bf16[4,160,256]{2,1,0:T(8,128)(2,1)S(1)} %pad_maximum_fusion.3.sums), channel_id=1, source_target_pairs={{0,16},{16,0},{32,48},{48,32},{64,80},{80,64},{96,112},{112,96},{1... | collective-permute-start | bytes 983048 | tf_op jit(solution)/shard_map/ppermute | solution.py:502

commit v3 on v2

--- a/solution.py
+++ b/solution.py
@@ -34,8 +34,8 @@
         out[:, t:t + HEAD] = rows[t:t + HEAD, :].T
 
 
-def tiles_of(cols):
-    tile = min(TILE, cols)
+def tiles_of(cols, tile):
+    tile = min(tile, cols)
     return [slice(t, t + tile) for t in range(0, cols, tile)]
 
 
@@ -51,7 +51,7 @@
     rows, qt, s_scr, m_scr, l_scr = scr
     cols = width * GROUP
     turned(q, width, rows, qt)
-    tiles = tiles_of(cols)
+    tiles = tiles_of(cols, TILE)
     m_scr[:, :cols] = jnp.full((8, cols), -1e30, F32)
     l_scr[:, :cols] = jnp.zeros((8, cols), F32)
     acc[...] = jnp.zeros((HEAD, cols), F32)
@@ -90,7 +90,11 @@
     for h in range(GROUP):
         qs[h * width:(h + 1) * width, :] = q[:, h * HEAD:(h + 1) * HEAD]
     turned(g, width, gs, gt)
-    tiles = tiles_of(cols)
+    for t in range(0, cols, HEAD):
+        part = (gt[:, t:t + HEAD].astype(F32) * stat[0:1, t:t + HEAD]).astype(BF)
+        gt[:, t:t + HEAD] = part
+        gs[t:t + HEAD, :] = part.T
+    tiles = tiles_of(cols, HALF)
     acc[:, :cols] = jnp.zeros((HEAD, cols), F32)
     delta = jnp.sum(attn_t[...] * gt[:, :cols].astype(F32), axis=0, keepdims=True)
     d_scr[:, :cols] = jnp.broadcast_to(delta, (8, cols))
@@ -100,10 +104,9 @@
         dk = dk_ref[at(c), :]
         dv = dv_ref[at(c), :]
         for t in tiles:
-            dp = dot(v, gt[:, t])
-            p = e_ref[at(c), t].astype(F32) * stat[0:1, t]
-            ds = (p * (dp - d_scr[0:1, t])).astype(BF)
-            dv += dot(p.astype(BF), gs[t, :])
+            e = e_ref[at(c), t]
+            ds = (e.astype(F32) * (dot(v, gt[:, t]) - d_scr[0:1, t])).astype(BF)
+            dv += dot(e, gs[t, :])
             dk += dot(ds, qs[t, :])
             acc[:, t] += dot(kt_ref[c], ds)
         dk_ref[at(c), :] = dk
@@ -135,8 +138,7 @@
 DENSE = BLOCKS * ROWS
 FEW = BLOCKS * SLOTS
 SENT = ROWS + SLOTS
-COUNT = 16
-MARKED = SENT + COUNT
+INVALID = 128.0
 VMEM = pl.BlockSpec(memory_space=pltpu.VMEM)
 SMEM = pl.BlockSpec(memory_space=pltpu.SMEM)
 WHOLE = pltpu.CompilerParams(vmem_limit_bytes=60 << 20)
@@ -153,14 +155,14 @@
 def pack_kv_kernel(k, v, k_in, v_in, sel, sel_in, *outs):
     def fill(dense, few, few_sel):
         pick = compact(few_sel)
-        count = jnp.sum((few_sel[0:1, :] >= 0).astype(F32), axis=1, keepdims=True)
+        mark = INVALID * (1.0 - jnp.sum(pick.astype(F32), axis=1, keepdims=True))
         for step, out in enumerate(outs):
             here = pl.ds(pl.multiple_of(own_head(step)[0] * HEAD, HEAD), HEAD)
             for side in range(2):
                 cols = slice(side * HEAD, (side + 1) * HEAD)
                 out[:ROWS, cols] = dense[side][:, here]
-                out[ROWS:SENT, cols] = dot(pick, few[side][:, here]).astype(BF)
-            out[SENT:, :] = jnp.broadcast_to(count, (COUNT, KV)).astype(BF)
+                rows = dot(pick, few[side][:, here])
+                out[ROWS:, cols] = (rows if side else rows + mark).astype(BF)
 
     @pl.when(own_head(0)[1] == 1)
     def _():
@@ -174,7 +176,7 @@
 def pack_kv(k, v, k_in, v_in, sel, sel_in):
     return list(pl.pallas_call(
         pack_kv_kernel,
-        out_shape=[jax.ShapeDtypeStruct((MARKED, KV), BF)] * 4,
+        out_shape=[jax.ShapeDtypeStruct((SENT, KV), BF)] * 4,
         in_specs=[VMEM] * 6,
         out_specs=[VMEM] * 4,
         compiler_params=PARAMS,
@@ -219,7 +221,7 @@
 
 
 FORTH = pltpu.CompilerParams(vmem_limit_bytes=12 << 20)
-BACK = pltpu.CompilerParams(vmem_limit_bytes=8 << 20)
+BACK = pltpu.CompilerParams(vmem_limit_bytes=24 << 20)
 SUMS = [((DENSE, HEAD), F32)] * 2 + [((FEW, HEAD), F32)] * 2
 FEWER = SLOTS * GROUP
 LEFT = [((SENT, HALF), BF), ((DENSE, HALF), BF), ((8, HALF), F32), ((HEAD, HALF), F32),
@@ -251,7 +253,6 @@
 
 def arrange(info, kvs, keyed):
     kd, ktd, kr, ktr, vd, vtd, vr, vtr, flags = keyed
-    slot = lax.broadcasted_iota(jnp.int32, (SLOTS, HEAD), 0).astype(F32)
     for ky, kv in enumerate(kvs):
         for kz in range(4):
             b = 4 * lax.rem(info[1] + 4 - kz, 4) + lax.rem(info[2] + 4 - ky, 4)
@@ -259,9 +260,9 @@
             small = pl.ds(pl.multiple_of(b * SLOTS, SLOTS), SLOTS)
             kd[big, :] = kv[kz, :ROWS, :HEAD]
             vd[big, :] = kv[kz, :ROWS, HEAD:]
-            kr[small, :] = kv[kz, ROWS:SENT, :HEAD]
-            vr[small, :] = kv[kz, ROWS:SENT, HEAD:]
-            flags[small, :] = (slot < kv[kz, SENT:, :HEAD].astype(F32)[0:1, :]).astype(F32)
+            kr[small, :] = kv[kz, ROWS:, :HEAD]
+            vr[small, :] = kv[kz, ROWS:, HEAD:]
+            flags[small, :] = (kv[kz, ROWS:, :HEAD].astype(F32) < INVALID / 2).astype(F32)
     for x, xt in ((kd, ktd), (kr, ktr), (vd, vtd), (vr, vtr)):
         turn_blocks(x, xt)
 
@@ -338,19 +339,16 @@
     emit(scr[3], SLOTS, SCALE, dq, ROWS, 0)
 
 
-def backward_kernel(shifts, first, info, *refs):
+def backward_kernel(shifts, info, *refs):
     n, m = len(shifts), len(LEFT) - 1
     qs, gs, refs = refs[:n], refs[n:2 * n], refs[2 * n:]
     lefts, keyed, refs = refs[:m * n], refs[m * n:m * n + 9], refs[m * n + 9:]
-    if first:
-        dqs, sums, scr = refs[:n], refs[n:n + 4], refs[n + 4:]
-    else:
-        came, dqs, sent, sums, scr = refs[:4], refs[4:n + 4], refs[n + 4:n + 8], refs[n + 8:n + 12], refs[n + 12:]
-    for i, total in enumerate(sums):
-        total[...] = jnp.zeros_like(total) if first else came[i][...]
+    dqs, sent, sums, scr = refs[:n], refs[n:n + 4], refs[n + 4:n + 8], refs[n + 8:]
+    for total in sums:
+        total[...] = jnp.zeros_like(total)
     for i, shift in enumerate(shifts):
         backward_block(info, shift, qs[i], gs[i], keyed, lefts[m * i:m * (i + 1)], sums, dqs[i], scr)
-    for ky in range(0 if first else 4):
+    for ky in range(4):
         for kz in range(4):
             b = 4 * lax.rem(info[1] + kz, 4) + lax.rem(info[2] + ky, 4)
             big = pl.ds(pl.multiple_of(b * ROWS, ROWS), ROWS)
@@ -361,17 +359,16 @@
             sent[ky][kz, ROWS:, HEAD:] = sums[3][small, :].astype(BF)
 
 
-def backward(shifts, info, qs, gs, lefts, keyed, sums=()):
-    n, first = len(shifts), not sums
-    shapes = [((SENT, HALF), BF)] * n + (SUMS if first else [((4, SENT, KV), BF)] * 4)
-    args = [qs[i] for i in shifts] + [gs[i] for i in shifts] + [x for i in shifts for x in lefts[i][1:]]
-    args += list(keyed) + list(sums)
+def backward(shifts, info, qs, gs, lefts, keyed):
+    n = len(shifts)
+    shapes = [((SENT, HALF), BF)] * n + [((4, SENT, KV), BF)] * 4
+    args = [qs[i] for i in shifts] + [gs[i] for i in shifts] + [x for i in shifts for x in lefts[i][1:]] + list(keyed)
     outs = pl.pallas_call(
-        functools.partial(backward_kernel, shifts, first),
+        functools.partial(backward_kernel, shifts),
         out_shape=shaped(shapes),
         in_specs=[SMEM] + [VMEM] * len(args),
         out_specs=[VMEM] * len(shapes),
-        scratch_shapes=([] if first else held(SUMS)) + BACKWARD,
+        scratch_shapes=held(SUMS) + BACKWARD,
         compiler_params=BACK,
         cost_estimate=cost(n * 6e9),
         name="backward",
@@ -531,17 +528,18 @@
         qs[by] = along_z(qs[by], by)
     gs = pack(g, g_in, sel, sel_in)
 
+    qs[0], qs[1], qs[3] = both(qs[0], qs[1], qs[3])
     (own,), keyed = forward((0,), info, [qs[0]], kvs=kvs)
     for by in (1, 3, 2):
         gs[by] = along_z(gs[by], by)
     one, three, two = forward((1, 3, 2), info, [qs[1], qs[3], qs[2]], keyed=keyed)
     lefts = [own, one, two, three]
     attn = [along_z(lefts[by][0], 4 - by) if by else lefts[by][0] for by in range(4)]
-    dq = [None] * 4
-    (dq[1], dq[3]), sums = backward((1, 3), info, qs, gs, lefts, keyed)
-    (dq[0], dq[2]), sent = backward((0, 2), info, qs, gs, lefts, keyed, sums)
+    dq, sent = backward((1, 3, 0, 2), info, qs, gs, lefts, keyed)
+    dq = [dq[2], dq[0], dq[3], dq[1]]
     dq = [along_z(dq[by], 4 - by) if by else dq[by] for by in range(4)]
-    attn[1], attn[2], attn[3], dq[1], dq[3], sent[0] = both(attn[1], attn[2], attn[3], dq[1], dq[3], sent[0])
+    attn[1], attn[2], attn[3], sent[0] = both(attn[1], attn[2], attn[3], sent[0])
+    dq[1], dq[3], sent[1] = both(dq[1], dq[3], sent[1])
     attn = jnp.stack(attn)
     updated = by_head(update_kernel, "update", info, seg, attn, swap(attn), sel)
     next_input = onward(updated)

time: 127 us -> 116 us (0.913)
  waiting for transfers between devices: 32.4 us -> 24.4 us
  starting transfers between devices: 41.3 us -> 39.8 us
  Pallas kernels: 46.7 us -> 45.4 us
    ppermute x6, waiting for transfers between devices: 22.3 us -> 18.1 us  [along_y(): lax.ppermute(x, 'ctx', [(4 * z + y, 4 * z + (y + by) % 4) for z in range(...]
    ppermute x18, starting transfers between devices: 25.5 us -> 21.8 us  [along_z(): lax.ppermute(x, 'ctx', [(4 * z + y, 4 * ((z + by) % 4) + y) for z in rang...]
    ppermute x8, starting transfers between devices: 5.31 us -> 7.85 us  [swap(): return lax.ppermute(x, 'section', [(i, i ^ 1) for i in range(8)])]
    ppermute x18, waiting for transfers between devices: 5.25 us -> 3.21 us  [along_z(): lax.ppermute(x, 'ctx', [(4 * z + y, 4 * ((z + by) % 4) + y) for z in rang...]
    ppermute x8, waiting for transfers between devices: 4.75 us -> 3.1 us  [swap(): return lax.ppermute(x, 'section', [(i, i ^ 1) for i in range(8)])]
    pallas_call x3 -> x2, Pallas kernels: 17.1 us -> 15.6 us  [the longest x1 15.4 us: backward(): pl.pallas_call(functools.partial(backward_kernel, shifts), out_shape=shap...]
    unnamed x22 -> x20, local copies, waits for them, and re-layouts: 3.25 us -> 3.24 us
  transfers between devices with their start and end apart: 33 -> 33, of which waited for: 11 -> 10; matrix products, arithmetic and copies ran while one was open for 1% -> 1% of each run, Pallas kernels for 35% -> 38%
where the time goes in v3:
time: 116 us
  Pallas kernels  45.4 us (39%)
  starting transfers between devices  39.8 us (34%)
  waiting for transfers between devices  24.4 us (21%)
  local copies, waits for them, and re-layouts  3.24 us (3%)
  between operations  1.5 us (1%)
  other arithmetic  1.16 us (1%)
    ppermute x18, starting transfers between devices, along_z(): lax.ppermute(x, 'ctx', [(4 * z + y, 4 * ((z + by) % 4) + y) for z in rang...  21.8 us
    ppermute x6, waiting for transfers between devices, along_y(): lax.ppermute(x, 'ctx', [(4 * z + y, 4 * z + (y + by) % 4) for z in range(...  18.1 us
    pallas_call x1, Pallas kernels, backward(): pl.pallas_call(functools.partial(backward_kernel, shifts), out_shape=shap...  15.4 us
    pallas_call x2, Pallas kernels, forward(): pl.pallas_call(functools.partial(forward_kernel, shifts, first), out_shap...  15.1 us
    ppermute x8, starting transfers between devices, swap(): return lax.ppermute(x, 'section', [(i, i ^ 1) for i in range(8)])  7.85 us
    pallas_call x2, Pallas kernels, pack(): pl.pallas_call(pack_kernel, out_shape=[jax.ShapeDtypeStruct((SENT, HALF),...  7.23 us
    ppermute x6, starting transfers between devices, along_y(): lax.ppermute(x, 'ctx', [(4 * z + y, 4 * z + (y + by) % 4) for z in range(...  6.23 us
    ppermute x1, starting transfers between devices, onward(): return lax.ppermute(x, 'section', [(i, i + 1) for i in range(7)])  3.96 us
  transfers between devices with their start and end apart: 33, of which 10 were waited for; matrix products, arithmetic and copies ran while one was open for 1% of the time, Pallas kernels for 38%

profile of v3, /device:TPU:1, one launch (start us, length us, event | category | flops | bytes accessed | tf_op | source)
XLA Modules:
  0.0 115.6 jit_solution(9083132053548581105)
XLA Ops:
  0.6 1.5 %collective-permute-start = (bf16[128,1024]{1,0:T(8,128)(2,1)}, bf16[128,1024]{1,0:T(8,128)(2,1)S(1)}, u32[]{:S(2)}, u32[]{:S(2)}) collective-permute-start(bf16[128,1024]{1,0:T(8,128)(2,1)} %bitcast.33), channel_id=1, source_target_pairs={{0,16},{16,0},{32,48},{48,32},{64,80},{80,64},{96,112},{112,96},{1... | collective-permute-start | bytes 786440 | tf_op jit(solution)/shard_map/ppermute | solution.py:499
  2.1 0.1 collective-permute-start.1
  2.9 0.7 compare_select_fusion.sel
  3.5 0.4 collective-permute-start.2
  4.0 0.8 collective-permute-done.2.sel_in
  4.8 0.4 collective-permute-start.3
  5.2 0.2 collective-permute-start.7
  5.4 0.9 copy-done.1
  6.3 0.9 copy-done.2
  7.3 0.3 pack_kv.1
  7.5 1.8 %collective-permute-start.4 = (bf16[160,256]{1,0:T(8,128)(2,1)S(1)}, bf16[160,256]{1,0:T(8,128)(2,1)S(1)}, u32[]{:S(2)}, u32[]{:S(2)}) collective-permute-start(bf16[160,256]{1,0:T(8,128)(2,1)S(1)} %get-tuple-element.100), channel_id=1, source_target_pairs={{0,4},{1,5},{2,6},{3,7},{4,8},{5,9},{6,10},{7,11},{8,12},{9,13},{1... | collective-permute-start | bytes 245768 | tf_op jit(solution)/shard_map/ppermute | solution.py:491
  9.3 3.3 %collective-permute-start.5 = (bf16[160,256]{1,0:T(8,128)(2,1)S(1)}, bf16[160,256]{1,0:T(8,128)(2,1)S(1)}, u32[]{:S(2)}, u32[]{:S(2)}) collective-permute-start(bf16[160,256]{1,0:T(8,128)(2,1)S(1)} %get-tuple-element.101), channel_id=1, source_target_pairs={{0,8},{1,9},{2,10},{3,11},{4,12},{5,13},{6,14},{7,15},{8,0},{9,1},... | collective-permute-start | bytes 245768 | tf_op jit(solution)/shard_map/ppermute | solution.py:491
  12.6 0.7 collective-permute-start.6
  13.4 0.0 collective-permute-done.3.come
  13.4 3.6 %pack.2 = (bf16[160,1024]{1,0:T(8,128)(2,1)}, bf16[160,1024]{1,0:T(8,128)(2,1)}, bf16[160,1024]{1,0:T(8,128)(2,1)}, bf16[160,1024]{1,0:T(8,128)(2,1)}) custom-call(bf16[128,8192]{1,0:T(8,128)(2,1)} %bitcast.40, bf16[128,8192]{1,0:T(8,128)(2,1)} %collective-permute-done.3.come, s32[1,128]{1,0:T(1,128)} %copy-done.3, s32[1,128]{1,0:T(1,128)} %copy-done.5), custom_call_target="tpu_custom_call" | custom-call | tf_op jit(solution)/shard_map/pack/pallas_call | solution.py:212
  16.9 0.0 collective-permute-done.4
  17.0 0.0 collective-permute-done.6
  17.0 0.0 collective-permute-done.7.come
  17.0 0.0 copy-start.8
  17.0 1.3 %copy-done.8 = bf16[128,8192]{1,0:T(8,128)(2,1)} copy-done((bf16[128,8192]{1,0:T(8,128)(2,1)}, bf16[128,8192]{1,0:T(8,128)(2,1)S(1)}, u32[]{:S(2)}) %copy-start.8) | copy-done | bytes 2097176
  18.4 1.0 collective-permute-start.8
  19.3 1.8 %collective-permute-start.9 = (bf16[160,1024]{1,0:T(8,128)(2,1)}, bf16[160,1024]{1,0:T(8,128)(2,1)S(1)}, u32[]{:S(2)}, u32[]{:S(2)}) collective-permute-start(bf16[160,1024]{1,0:T(8,128)(2,1)} %get-tuple-element.116), channel_id=1, source_target_pairs={{0,12},{1,13},{2,14},{3,15},{4,0},{5,1},{6,2},{7,3},{8,4},{9,5},{1... | collective-permute-start | bytes 983048 | tf_op jit(solution)/shard_map/ppermute | solution.py:491
  21.1 1.3 %collective-permute-start.10 = (bf16[4,160,256]{2,1,0:T(8,128)(2,1)S(1)}, bf16[4,160,256]{2,1,0:T(8,128)(2,1)S(1)}, u32[]{:S(2)}, u32[]{:S(2)}) collective-permute-start(bf16[4,160,256]{2,1,0:T(8,128)(2,1)S(1)} %pad_maximum_fusion.2.refs_1_), channel_id=1, source_target_pairs={{0,1},{1,2},{2,3},{3,0},{4,5},{5,6},{6,7},{7,4},{8,9},{9,10},{10,1... | collective-permute-start | bytes 983048 | tf_op jit(solution)/shard_map/ppermute | solution.py:495
  22.4 2.6 %collective-permute-start.11 = (bf16[4,160,256]{2,1,0:T(8,128)(2,1)S(1)}, bf16[4,160,256]{2,1,0:T(8,128)(2,1)S(1)}, u32[]{:S(2)}, u32[]{:S(2)}) collective-permute-start(bf16[4,160,256]{2,1,0:T(8,128)(2,1)S(1)} %pad_maximum_fusion.2.refs_1_), channel_id=1, source_target_pairs={{0,2},{1,3},{2,0},{3,1},{4,6},{5,7},{6,4},{7,5},{8,10},{9,11},{10,... | collective-permute-start | bytes 983048 | tf_op jit(solution)/shard_map/ppermute | solution.py:495
  25.0 1.1 collective-permute-start.12
  26.1 0.1 pad_add_fusion.info
  26.2 3.7 %pack.3 = (bf16[160,1024]{1,0:T(8,128)(2,1)}, bf16[160,1024]{1,0:T(8,128)(2,1)}, bf16[160,1024]{1,0:T(8,128)(2,1)}, bf16[160,1024]{1,0:T(8,128)(2,1)}) custom-call(bf16[128,8192]{1,0:T(8,128)(2,1)} %bitcast.42, bf16[128,8192]{1,0:T(8,128)(2,1)} %copy-done.8, s32[1,128]{1,0:T(1,128)} %copy-done.3, s32[1,128]{1,0:T(1,128)} %copy-done.5), custom_call_target="tpu_custom_call" | custom-call | tf_op jit(solution)/shard_map/pack/pallas_call | solution.py:212
  29.8 0.0 collective-permute-done.8.refs_0_
  29.9 0.2 collective-permute-start.13
  30.0 0.5 collective-permute-start.17
  30.5 2.2 %collective-permute-start.18 = (bf16[160,1024]{1,0:T(8,128)(2,1)}, bf16[160,1024]{1,0:T(8,128)(2,1)S(1)}, u32[]{:S(2)}, u32[]{:S(2)}) collective-permute-start(bf16[160,1024]{1,0:T(8,128)(2,1)} %get-tuple-element.136), channel_id=1, source_target_pairs={{0,12},{1,13},{2,14},{3,15},{4,0},{5,1},{6,2},{7,3},{8,4},{9,5},{1... | collective-permute-start | bytes 983048 | tf_op jit(solution)/shard_map/ppermute | solution.py:491
  32.7 5.4 %collective-permute-done.11.refs_3_ = bf16[4,160,256]{2,1,0:T(8,128)(2,1)S(1)} collective-permute-done((bf16[4,160,256]{2,1,0:T(8,128)(2,1)S(1)}, bf16[4,160,256]{2,1,0:T(8,128)(2,1)S(1)}, u32[]{:S(2)}, u32[]{:S(2)}) %collective-permute-start.11) | collective-permute-done | bytes 327712 | tf_op jit(solution)/shard_map/ppermute | solution.py:495
  38.1 0.5 collective-permute-done.12.refs_4_
  38.6 2.9 %forward.2 = (bf16[160,1024]{1,0:T(8,128)(2,1)S(1)}, bf16[2048,1024]{1,0:T(8,128)(2,1)S(1)}, f32[8,1024]{1,0:T(8,128)S(1)}, f32[128,1024]{1,0:T(8,128)S(1)}, bf1...) custom-call(s32[3]{0:T(128)S(1)} %pad_add_fusion.info, ...), custom_call_target="tpu_custom_call" | custom-call | flops 4000000000 | bytes 4194304 | tf_op jit(solution)/shard_map/forward/pallas_call | solution.py:319
  41.5 12.2 %forward.3 = (bf16[160,1024]{1,0:T(8,128)(2,1)S(1)}, bf16[2048,1024]{1,0:T(8,128)(2,1)S(1)}, f32[8,1024]{1,0:T(8,128)S(1)}, f32[128,1024]{1,0:T(8,128)S(1)}, bf1...) custom-call(s32[3]{0:T(128)S(1)} %pad_add_fusion.info, ...), custom_call_target="tpu_custom_call" | custom-call | flops 12000000000 | bytes 4194304 | tf_op jit(solution)/shard_map/forward/pallas_call | solution.py:319
  53.7 1.8 %collective-permute-start.14 = (bf16[160,1024]{1,0:T(8,128)(2,1)S(1)}, bf16[160,1024]{1,0:T(8,128)(2,1)S(1)}, u32[]{:S(2)}, u32[]{:S(2)}) collective-permute-start(bf16[160,1024]{1,0:T(8,128)(2,1)S(1)} %get-tuple-element.131), channel_id=1, source_target_pairs={{0,12},{1,13},{2,14},{3,15},{4,0},{5,1},{6,2},{7,3},{8,4},{9,5},{1... | collective-permute-start | bytes 983048 | tf_op jit(solution)/shard_map/ppermute | solution.py:491
  55.4 0.9 collective-permute-start.15
  56.3 0.8 collective-permute-start.16
  57.1 15.4 %backward.1 = (bf16[160,1024]{1,0:T(8,128)(2,1)S(1)}, bf16[160,1024]{1,0:T(8,128)(2,1)S(1)}, bf16[160,1024]{1,0:T(8,128)(2,1)S(1)}, bf16[160,1024]{1,0:T(8,128)(...) custom-call(s32[3]{0:T(128)S(1)} %pad_add_fusion.info, ...), custom_call_target="tpu_custom_call" | custom-call | flops 24000000000 | bytes 4194304 | tf_op jit(solution)/shard_map/backward/pallas_call | solution.py:366
  72.5 0.8 collective-permute-done.16
  73.3 0.2 pad_maximum_fusion.mine
  73.4 3.1 %collective-permute-start.20 = (bf16[4,160,1024]{2,1,0:T(8,128)(2,1)S(1)}, bf16[4,160,1024]{2,1,0:T(8,128)(2,1)S(1)}, u32[]{:S(2)}, u32[]{:S(2)}) collective-permute-start(bf16[4,160,1024]{2,1,0:T(8,128)(2,1)S(1)} %pad_maximum_fusion.mine), channel_id=1, source_target_pairs={{0,16},{16,0},{32,48},{48,32},{64,80},{80,64},{96,112},{112,96},{1... | collective-permute-start | bytes 3932168 | tf_op jit(solution)/shard_map/ppermute | solution.py:499
  76.5 1.6 %collective-permute-start.22 = (bf16[160,1024]{1,0:T(8,128)(2,1)S(1)}, bf16[160,1024]{1,0:T(8,128)(2,1)S(1)}, u32[]{:S(2)}, u32[]{:S(2)}) collective-permute-start(bf16[160,1024]{1,0:T(8,128)(2,1)S(1)} %get-tuple-element.168), channel_id=1, source_target_pairs={{0,12},{1,13},{2,14},{3,15},{4,0},{5,1},{6,2},{7,3},{8,4},{9,5},{1... | collective-permute-start | bytes 983048 | tf_op jit(solution)/shard_map/ppermute | solution.py:491
  78.2 0.0 collective-permute-start.23
  78.2 1.0 collective-permute-done.20.theirs
  79.2 1.5 %update.1 = bf16[128,8192]{1,0:T(8,128)(2,1)S(1)} custom-call(s32[3]{0:T(128)S(1)} %pad_add_fusion.info, bf16[128,8192]{1,0:T(8,128)(2,1)S(1)} %bitcast.30, bf16[4,160,1024]{2,1,0:T(8,128)(2,1)S(1)} %pad_maximum_fusion.mine, bf16[4,160,1024]{2,1,0:T(8,128)(2,1)S(1)} %collective-permute-done.20.theirs, s32[1,128]{1,0:T(1,128)S(1)} %copy-done.4), custom_call_target="tpu_custom_call" | custom-call | tf_op jit(solution)/shard_map/update/pallas_call | solution.py:428
  80.7 4.0 %collective-permute-start.21 = (bf16[128,8192]{1,0:T(8,128)(2,1)S(1)}, bf16[128,8192]{1,0:T(8,128)(2,1)S(1)}, u32[]{:S(2)}, u32[]{:S(2)}) collective-permute-start(bf16[128,8192]{1,0:T(8,128)(2,1)S(1)} %update.1), channel_id=1, source_target_pairs={{0,16},{16,32},{32,48},{48,64},{64,80},{80,96},{96,112},{1,17},{17... | collective-permute-start | bytes 6291464 | tf_op jit(solution)/shard_map/ppermute | solution.py:503
  84.7 1.2 %collective-permute-start.26 = (bf16[4,160,256]{2,1,0:T(8,128)(2,1)S(1)}, bf16[4,160,256]{2,1,0:T(8,128)(2,1)S(1)}, u32[]{:S(2)}, u32[]{:S(2)}) collective-permute-start(bf16[4,160,256]{2,1,0:T(8,128)(2,1)S(1)} %get-tuple-element.175), channel_id=1, source_target_pairs={{0,2},{1,3},{2,0},{3,1},{4,6},{5,7},{6,4},{7,5},{8,10},{9,11},{10,... | collective-permute-start | bytes 983048 | tf_op jit(solution)/shard_map/ppermute | solution.py:495
  85.9 2.4 %collective-permute-done.23 = bf16[160,1024]{1,0:T(8,128)(2,1)S(1)} collective-permute-done((bf16[160,1024]{1,0:T(8,128)(2,1)S(1)}, bf16[160,1024]{1,0:T(8,128)(2,1)S(1)}, u32[]{:S(2)}, u32[]{:S(2)}) %collective-permute-start.23) | collective-permute-done | bytes 327712 | tf_op jit(solution)/shard_map/ppermute | solution.py:491
  88.3 1.4 %collective-permute-start.24 = (bf16[160,1024]{1,0:T(8,128)(2,1)S(1)}, bf16[160,1024]{1,0:T(8,128)(2,1)S(1)}, u32[]{:S(2)}, u32[]{:S(2)}) collective-permute-start(bf16[160,1024]{1,0:T(8,128)(2,1)S(1)} %get-tuple-element.172), channel_id=1, source_target_pairs={{0,8},{1,9},{2,10},{3,11},{4,12},{5,13},{6,14},{7,15},{8,0},{9,1},... | collective-permute-start | bytes 983048 | tf_op jit(solution)/shard_map/ppermute | solution.py:491
  89.7 6.3 %collective-permute-done.26.c = bf16[4,160,256]{2,1,0:T(8,128)(2,1)S(1)} collective-permute-done((bf16[4,160,256]{2,1,0:T(8,128)(2,1)S(1)}, bf16[4,160,256]{2,1,0:T(8,128)(2,1)S(1)}, u32[]{:S(2)}, u32[]{:S(2)}) %collective-permute-start.26) | collective-permute-done | bytes 327712 | tf_op jit(solution)/shard_map/ppermute | solution.py:495
  96.0 4.4 %collective-permute-done.27.d = bf16[4,160,256]{2,1,0:T(8,128)(2,1)S(1)} collective-permute-done((bf16[4,160,256]{2,1,0:T(8,128)(2,1)S(1)}, bf16[4,160,256]{2,1,0:T(8,128)(2,1)S(1)}, u32[]{:S(2)}, u32[]{:S(2)}) %collective-permute-start.27) | collective-permute-done | bytes 327712 | tf_op jit(solution)/shard_map/ppermute | solution.py:495
  100.4 1.5 %collective-permute-done.25.b = bf16[4,160,256]{2,1,0:T(8,128)(2,1)S(1)} collective-permute-done((bf16[4,160,256]{2,1,0:T(8,128)(2,1)S(1)}, bf16[4,160,256]{2,1,0:T(8,128)(2,1)S(1)}, u32[]{:S(2)}, u32[]{:S(2)}) %collective-permute-start.25) | collective-permute-done | bytes 327712 | tf_op jit(solution)/shard_map/ppermute | solution.py:495
  102.0 0.2 fold_sums.1
  102.1 0.2 pad_maximum_fusion.1.mine
  102.3 0.6 collective-permute-start.28
  102.9 0.9 collective-permute-start.29
  103.8 2.1 %collective-permute-start.30 = (bf16[160,256]{1,0:T(8,128)(2,1)S(1)}, bf16[160,256]{1,0:T(8,128)(2,1)S(1)}, u32[]{:S(2)}, u32[]{:S(2)}) collective-permute-start(bf16[160,256]{1,0:T(8,128)(2,1)S(1)} %get-tuple-element.182), channel_id=1, source_target_pairs={{0,8},{1,9},{2,10},{3,11},{4,12},{5,13},{6,14},{7,15},{8,0},{9,1},... | collective-permute-start | bytes 245768 | tf_op jit(solution)/shard_map/ppermute | solution.py:491
  105.9 1.0 collective-permute-start.31
  106.9 2.4 %finish_q.1 = bf16[128,8192]{1,0:T(8,128)(2,1)} custom-call(s32[3]{0:T(128)S(1)} %pad_add_fusion.info, bf16[4,160,1024]{2,1,0:T(8,128)(2,1)S(1)} %pad_maximum_fusion.1.mine, bf16[4,160,1024]{2,1,0:T(8,128)(2,1)S(1)} %collective-permute-done.28.theirs, s32[1,128]{1,0:T(1,128)S(1)} %copy-done.4), custom_call_target="tpu_custom_call" | custom-call | tf_op jit(solution)/shard_map/finish_q/pallas_call | solution.py:428
  109.3 1.9 %settle.1 = bf16[128,8192]{1,0:T(8,128)(2,1)} custom-call(bf16[128,8192]{1,0:T(8,128)(2,1)S(1)} %collective-permute-done.21.x), custom_call_target="tpu_custom_call" | custom-call | tf_op jit(solution)/shard_map/settle/pallas_call | solution.py:448
  111.3 1.6 %collective-permute-start.32 = (bf16[4,160,256]{2,1,0:T(8,128)(2,1)S(1)}, bf16[4,160,256]{2,1,0:T(8,128)(2,1)S(1)}, u32[]{:S(2)}, u32[]{:S(2)}) collective-permute-start(bf16[4,160,256]{2,1,0:T(8,128)(2,1)S(1)} %pad_maximum_fusion.3.sums), channel_id=1, source_target_pairs={{0,16},{16,0},{32,48},{48,32},{64,80},{80,64},{96,112},{112,96},{1... | collective-permute-start | bytes 983048 | tf_op jit(solution)/shard_map/ppermute | solution.py:499
  112.9 1.3 %collective-permute-done.32.sums_in = bf16[4,160,256]{2,1,0:T(8,128)(2,1)S(1)} collective-permute-done((bf16[4,160,256]{2,1,0:T(8,128)(2,1)S(1)}, bf16[4,160,256]{2,1,0:T(8,128)(2,1)S(1)}, u32[]{:S(2)}, u32[]{:S(2)}) %collective-permute-start.32) | collective-permute-done | bytes 327712 | tf_op jit(solution)/shard_map/ppermute | solution.py:499
  114.1 1.4 %finish_kv.1 = (bf16[128,1024]{1,0:T(8,128)(2,1)}, bf16[128,1024]{1,0:T(8,128)(2,1)}) custom-call(s32[3]{0:T(128)S(1)} %pad_add_fusion.info, bf16[4,160,256]{2,1,0:T(8,128)(2,1)S(1)} %pad_maximum_fusion.3.sums, bf16[4,160,256]{2,1,0:T(8,128)(2,1)S(1)} %collective-permute-done.32.sums_in, s32[1,128]{1,0:T(1,128)S(1)} %copy-done.4), custom_call_target="tpu_custom_call" | custom-call | tf_op jit(solution)/shard_map/finish_kv/pallas_call | solution.py:480
  (39 shorter events, 0.2 us)
Async XLA Ops:
  0.6 4.2 %collective-permute-start = (bf16[128,1024]{1,0:T(8,128)(2,1)}, bf16[128,1024]{1,0:T(8,128)(2,1)S(1)}, u32[]{:S(2)}, u32[]{:S(2)}) collective-permute-start(bf16[128,1024]{1,0:T(8,128)(2,1)} %bitcast.33), channel_id=1, source_target_pairs={{0,16},{16,0},{32,48},{48,32},{64,80},{80,64},{96,112},{112,96},{1... | collective-permute-start | bytes 786440 | tf_op jit(solution)/shard_map/ppermute | solution.py:499
  2.1 2.7 %collective-permute-start.1 = (bf16[128,1024]{1,0:T(8,128)(2,1)}, bf16[128,1024]{1,0:T(8,128)(2,1)S(1)}, u32[]{:S(2)}, u32[]{:S(2)}) collective-permute-start(bf16[128,1024]{1,0:T(8,128)(2,1)} %bitcast.35), channel_id=1, source_target_pairs={{0,16},{16,0},{32,48},{48,32},{64,80},{80,64},{96,112},{112,96},{1... | collective-permute-start | bytes 786440 | tf_op jit(solution)/shard_map/ppermute | solution.py:499
  3.5 9.8 %copy-start.3 = (s32[1,128]{1,0:T(1,128)}, s32[1,128]{1,0:T(1,128)S(1)}, u32[]{:S(2)}) copy-start(s32[1,128]{1,0:T(1,128)S(1)} %compare_select_fusion.sel) | copy-start | bytes 1540
  3.5 1.2 %collective-permute-start.2 = (s32[1,128]{1,0:T(1,128)S(1)}, s32[1,128]{1,0:T(1,128)S(1)}, u32[]{:S(2)}, u32[]{:S(2)}) collective-permute-start(s32[1,128]{1,0:T(1,128)S(1)} %compare_select_fusion.sel), channel_id=1, source_target_pairs={{0,16},{16,0},{32,48},{48,32},{64,80},{80,64},{96,112},{112,96},{1... | collective-permute-start | bytes 1544 | tf_op jit(solution)/shard_map/ppermute | solution.py:499
  4.8 8.6 %copy-start.5 = (s32[1,128]{1,0:T(1,128)}, s32[1,128]{1,0:T(1,128)S(1)}, u32[]{:S(2)}) copy-start(s32[1,128]{1,0:T(1,128)S(1)} %collective-permute-done.2.sel_in) | copy-start | bytes 1540
  4.8 8.6 %collective-permute-start.3 = (bf16[128,8192]{1,0:T(8,128)(2,1)}, bf16[128,8192]{1,0:T(8,128)(2,1)}, u32[]{:S(2)}, u32[]{:S(2)}) collective-permute-start(bf16[128,8192]{1,0:T(8,128)(2,1)} %bitcast.39), channel_id=1, source_target_pairs={{0,16},{16,0},{32,48},{48,32},{64,80},{80,64},{96,112},{112,96},{1... | collective-permute-start | bytes 6291464 | tf_op jit(solution)/shard_map/ppermute | solution.py:499
  5.2 11.8 %collective-permute-start.7 = (bf16[128,8192]{1,0:T(8,128)(2,1)}, bf16[128,8192]{1,0:T(8,128)(2,1)S(1)}, u32[]{:S(2)}, u32[]{:S(2)}) collective-permute-start(bf16[128,8192]{1,0:T(8,128)(2,1)} %bitcast.41), channel_id=1, source_target_pairs={{0,16},{16,0},{32,48},{48,32},{64,80},{80,64},{96,112},{112,96},{1... | collective-permute-start | bytes 6291464 | tf_op jit(solution)/shard_map/ppermute | solution.py:499
  5.4 0.9 copy-start.1
  6.3 0.9 copy-start.2
  7.5 9.4 %collective-permute-start.4 = (bf16[160,256]{1,0:T(8,128)(2,1)S(1)}, bf16[160,256]{1,0:T(8,128)(2,1)S(1)}, u32[]{:S(2)}, u32[]{:S(2)}) collective-permute-start(bf16[160,256]{1,0:T(8,128)(2,1)S(1)} %get-tuple-element.100), channel_id=1, source_target_pairs={{0,4},{1,5},{2,6},{3,7},{4,8},{5,9},{6,10},{7,11},{8,12},{9,13},{1... | collective-permute-start | bytes 245768 | tf_op jit(solution)/shard_map/ppermute | solution.py:491
  9.3 7.6 %collective-permute-start.5 = (bf16[160,256]{1,0:T(8,128)(2,1)S(1)}, bf16[160,256]{1,0:T(8,128)(2,1)S(1)}, u32[]{:S(2)}, u32[]{:S(2)}) collective-permute-start(bf16[160,256]{1,0:T(8,128)(2,1)S(1)} %get-tuple-element.101), channel_id=1, source_target_pairs={{0,8},{1,9},{2,10},{3,11},{4,12},{5,13},{6,14},{7,15},{8,0},{9,1},... | collective-permute-start | bytes 245768 | tf_op jit(solution)/shard_map/ppermute | solution.py:491
  12.6 4.3 %collective-permute-start.6 = (bf16[160,256]{1,0:T(8,128)(2,1)S(1)}, bf16[160,256]{1,0:T(8,128)(2,1)S(1)}, u32[]{:S(2)}, u32[]{:S(2)}) collective-permute-start(bf16[160,256]{1,0:T(8,128)(2,1)S(1)} %get-tuple-element.102), channel_id=1, source_target_pairs={{0,12},{1,13},{2,14},{3,15},{4,0},{5,1},{6,2},{7,3},{8,4},{9,5},{1... | collective-permute-start | bytes 245768 | tf_op jit(solution)/shard_map/ppermute | solution.py:491
  17.0 1.3 %copy-start.8 = (bf16[128,8192]{1,0:T(8,128)(2,1)}, bf16[128,8192]{1,0:T(8,128)(2,1)S(1)}, u32[]{:S(2)}) copy-start(bf16[128,8192]{1,0:T(8,128)(2,1)S(1)} %collective-permute-done.7.come) | copy-start | bytes 6291460
  18.4 11.5 %collective-permute-start.8 = (bf16[160,1024]{1,0:T(8,128)(2,1)}, bf16[160,1024]{1,0:T(8,128)(2,1)S(1)}, u32[]{:S(2)}, u32[]{:S(2)}) collective-permute-start(bf16[160,1024]{1,0:T(8,128)(2,1)} %get-tuple-element.115), channel_id=1, source_target_pairs={{0,4},{1,5},{2,6},{3,7},{4,8},{5,9},{6,10},{7,11},{8,12},{9,13},{1... | collective-permute-start | bytes 983048 | tf_op jit(solution)/shard_map/ppermute | solution.py:491
  19.3 10.7 %collective-permute-start.9 = (bf16[160,1024]{1,0:T(8,128)(2,1)}, bf16[160,1024]{1,0:T(8,128)(2,1)S(1)}, u32[]{:S(2)}, u32[]{:S(2)}) collective-permute-start(bf16[160,1024]{1,0:T(8,128)(2,1)} %get-tuple-element.116), channel_id=1, source_target_pairs={{0,12},{1,13},{2,14},{3,15},{4,0},{5,1},{6,2},{7,3},{8,4},{9,5},{1... | collective-permute-start | bytes 983048 | tf_op jit(solution)/shard_map/ppermute | solution.py:491
  21.1 9.4 %collective-permute-start.10 = (bf16[4,160,256]{2,1,0:T(8,128)(2,1)S(1)}, bf16[4,160,256]{2,1,0:T(8,128)(2,1)S(1)}, u32[]{:S(2)}, u32[]{:S(2)}) collective-permute-start(bf16[4,160,256]{2,1,0:T(8,128)(2,1)S(1)} %pad_maximum_fusion.2.refs_1_), channel_id=1, source_target_pairs={{0,1},{1,2},{2,3},{3,0},{4,5},{5,6},{6,7},{7,4},{8,9},{9,10},{10,1... | collective-permute-start | bytes 983048 | tf_op jit(solution)/shard_map/ppermute | solution.py:495
  22.4 15.7 %collective-permute-start.11 = (bf16[4,160,256]{2,1,0:T(8,128)(2,1)S(1)}, bf16[4,160,256]{2,1,0:T(8,128)(2,1)S(1)}, u32[]{:S(2)}, u32[]{:S(2)}) collective-permute-start(bf16[4,160,256]{2,1,0:T(8,128)(2,1)S(1)} %pad_maximum_fusion.2.refs_1_), channel_id=1, source_target_pairs={{0,2},{1,3},{2,0},{3,1},{4,6},{5,7},{6,4},{7,5},{8,10},{9,11},{10,... | collective-permute-start | bytes 983048 | tf_op jit(solution)/shard_map/ppermute | solution.py:495
  25.0 13.6 %collective-permute-start.12 = (bf16[4,160,256]{2,1,0:T(8,128)(2,1)S(1)}, bf16[4,160,256]{2,1,0:T(8,128)(2,1)S(1)}, u32[]{:S(2)}, u32[]{:S(2)}) collective-permute-start(bf16[4,160,256]{2,1,0:T(8,128)(2,1)S(1)} %pad_maximum_fusion.2.refs_1_), channel_id=1, source_target_pairs={{0,3},{1,0},{2,1},{3,2},{4,7},{5,4},{6,5},{7,6},{8,11},{9,8},{10,9... | collective-permute-start | bytes 983048 | tf_op jit(solution)/shard_map/ppermute | solution.py:495
  26.2 3.7 %copy-start.9 = (bf16[160,1024]{1,0:T(8,128)(2,1)S(1)}, bf16[160,1024]{1,0:T(8,128)(2,1)}, u32[]{:S(2)}) copy-start(bf16[160,1024]{1,0:T(8,128)(2,1)} %get-tuple-element.121) | copy-start | bytes 983044
  26.2 12.4 %copy-start.6 = (bf16[160,1024]{1,0:T(8,128)(2,1)S(1)}, bf16[160,1024]{1,0:T(8,128)(2,1)}, u32[]{:S(2)}) copy-start(bf16[160,1024]{1,0:T(8,128)(2,1)} %get-tuple-element.117.refs_0_.refs_2_) | copy-start | bytes 983044
  29.9 11.6 %collective-permute-start.13 = (bf16[160,1024]{1,0:T(8,128)(2,1)S(1)}, bf16[160,1024]{1,0:T(8,128)(2,1)S(1)}, u32[]{:S(2)}, u32[]{:S(2)}) collective-permute-start(bf16[160,1024]{1,0:T(8,128)(2,1)S(1)} %copy-done.9), channel_id=1, source_target_pairs={{0,8},{1,9},{2,10},{3,11},{4,12},{5,13},{6,14},{7,15},{8,0},{9,1},... | collective-permute-start | bytes 983048 | tf_op jit(solution)/shard_map/ppermute | solution.py:491
  30.0 26.3 %collective-permute-start.17 = (bf16[160,1024]{1,0:T(8,128)(2,1)}, bf16[160,1024]{1,0:T(8,128)(2,1)S(1)}, u32[]{:S(2)}, u32[]{:S(2)}) collective-permute-start(bf16[160,1024]{1,0:T(8,128)(2,1)} %get-tuple-element.135), channel_id=1, source_target_pairs={{0,4},{1,5},{2,6},{3,7},{4,8},{5,9},{6,10},{7,11},{8,12},{9,13},{1... | collective-permute-start | bytes 983048 | tf_op jit(solution)/shard_map/ppermute | solution.py:491
  30.5 26.6 %collective-permute-start.18 = (bf16[160,1024]{1,0:T(8,128)(2,1)}, bf16[160,1024]{1,0:T(8,128)(2,1)S(1)}, u32[]{:S(2)}, u32[]{:S(2)}) collective-permute-start(bf16[160,1024]{1,0:T(8,128)(2,1)} %get-tuple-element.136), channel_id=1, source_target_pairs={{0,12},{1,13},{2,14},{3,15},{4,0},{5,1},{6,2},{7,3},{8,4},{9,5},{1... | collective-permute-start | bytes 983048 | tf_op jit(solution)/shard_map/ppermute | solution.py:491
  38.1 19.0 %collective-permute-start.19 = (bf16[160,1024]{1,0:T(8,128)(2,1)}, bf16[160,1024]{1,0:T(8,128)(2,1)S(1)}, u32[]{:S(2)}, u32[]{:S(2)}) collective-permute-start(bf16[160,1024]{1,0:T(8,128)(2,1)} %get-tuple-element.138), channel_id=1, source_target_pairs={{0,8},{1,9},{2,10},{3,11},{4,12},{5,13},{6,14},{7,15},{8,0},{9,1},... | collective-permute-start | bytes 983048 | tf_op jit(solution)/shard_map/ppermute | solution.py:491
  41.5 15.6 %copy-start.7 = (bf16[160,1024]{1,0:T(8,128)(2,1)S(1)}, bf16[160,1024]{1,0:T(8,128)(2,1)}, u32[]{:S(2)}) copy-start(bf16[160,1024]{1,0:T(8,128)(2,1)} %get-tuple-element.137.refs_6_) | copy-start | bytes 983044
  53.7 18.8 %collective-permute-start.14 = (bf16[160,1024]{1,0:T(8,128)(2,1)S(1)}, bf16[160,1024]{1,0:T(8,128)(2,1)S(1)}, u32[]{:S(2)}, u32[]{:S(2)}) collective-permute-start(bf16[160,1024]{1,0:T(8,128)(2,1)S(1)} %get-tuple-element.131), channel_id=1, source_target_pairs={{0,12},{1,13},{2,14},{3,15},{4,0},{5,1},{6,2},{7,3},{8,4},{9,5},{1... | collective-permute-start | bytes 983048 | tf_op jit(solution)/shard_map/ppermute | solution.py:491
  55.4 17.0 %collective-permute-start.15 = (bf16[160,1024]{1,0:T(8,128)(2,1)S(1)}, bf16[160,1024]{1,0:T(8,128)(2,1)S(1)}, u32[]{:S(2)}, u32[]{:S(2)}) collective-permute-start(bf16[160,1024]{1,0:T(8,128)(2,1)S(1)} %get-tuple-element.132), channel_id=1, source_target_pairs={{0,8},{1,9},{2,10},{3,11},{4,12},{5,13},{6,14},{7,15},{8,0},{9,1},... | collective-permute-start | bytes 983048 | tf_op jit(solution)/shard_map/ppermute | solution.py:491
  56.3 16.9 %collective-permute-start.16 = (bf16[160,1024]{1,0:T(8,128)(2,1)S(1)}, bf16[160,1024]{1,0:T(8,128)(2,1)S(1)}, u32[]{:S(2)}, u32[]{:S(2)}) collective-permute-start(bf16[160,1024]{1,0:T(8,128)(2,1)S(1)} %get-tuple-element.133), channel_id=1, source_target_pairs={{0,4},{1,5},{2,6},{3,7},{4,8},{5,9},{6,10},{7,11},{8,12},{9,13},{1... | collective-permute-start | bytes 983048 | tf_op jit(solution)/shard_map/ppermute | solution.py:491
  73.2 5.9 %copy-start = (bf16[1,128,8192]{2,1,0:T(8,128)(2,1)S(1)}, bf16[1,128,8192]{2,1,0:T(8,128)(2,1)}, u32[]{:S(2)}) copy-start(bf16[1,128,8192]{2,1,0:T(8,128)(2,1)} %param.7) | copy-start | bytes 6291460
  73.2 5.9 %copy-start.4 = (s32[1,128]{1,0:T(1,128)S(1)}, s32[1,128]{1,0:T(1,128)}, u32[]{:S(2)}) copy-start(s32[1,128]{1,0:T(1,128)} %copy-done.3) | copy-start | bytes 1540
  73.4 5.8 %collective-permute-start.20 = (bf16[4,160,1024]{2,1,0:T(8,128)(2,1)S(1)}, bf16[4,160,1024]{2,1,0:T(8,128)(2,1)S(1)}, u32[]{:S(2)}, u32[]{:S(2)}) collective-permute-start(bf16[4,160,1024]{2,1,0:T(8,128)(2,1)S(1)} %pad_maximum_fusion.mine), channel_id=1, source_target_pairs={{0,16},{16,0},{32,48},{48,32},{64,80},{80,64},{96,112},{112,96},{1... | collective-permute-start | bytes 3932168 | tf_op jit(solution)/shard_map/ppermute | solution.py:499
  76.5 9.4 %collective-permute-start.22 = (bf16[160,1024]{1,0:T(8,128)(2,1)S(1)}, bf16[160,1024]{1,0:T(8,128)(2,1)S(1)}, u32[]{:S(2)}, u32[]{:S(2)}) collective-permute-start(bf16[160,1024]{1,0:T(8,128)(2,1)S(1)} %get-tuple-element.168), channel_id=1, source_target_pairs={{0,12},{1,13},{2,14},{3,15},{4,0},{5,1},{6,2},{7,3},{8,4},{9,5},{1... | collective-permute-start | bytes 983048 | tf_op jit(solution)/shard_map/ppermute | solution.py:491
  78.2 10.2 %collective-permute-start.23 = (bf16[160,1024]{1,0:T(8,128)(2,1)S(1)}, bf16[160,1024]{1,0:T(8,128)(2,1)S(1)}, u32[]{:S(2)}, u32[]{:S(2)}) collective-permute-start(bf16[160,1024]{1,0:T(8,128)(2,1)S(1)} %get-tuple-element.169), channel_id=1, source_target_pairs={{0,4},{1,5},{2,6},{3,7},{4,8},{5,9},{6,10},{7,11},{8,12},{9,13},{1... | collective-permute-start | bytes 983048 | tf_op jit(solution)/shard_map/ppermute | solution.py:491
  80.7 28.6 %collective-permute-start.21 = (bf16[128,8192]{1,0:T(8,128)(2,1)S(1)}, bf16[128,8192]{1,0:T(8,128)(2,1)S(1)}, u32[]{:S(2)}, u32[]{:S(2)}) collective-permute-start(bf16[128,8192]{1,0:T(8,128)(2,1)S(1)} %update.1), channel_id=1, source_target_pairs={{0,16},{16,32},{32,48},{48,64},{64,80},{80,96},{96,112},{1,17},{17... | collective-permute-start | bytes 6291464 | tf_op jit(solution)/shard_map/ppermute | solution.py:503
  84.7 11.3 %collective-permute-start.26 = (bf16[4,160,256]{2,1,0:T(8,128)(2,1)S(1)}, bf16[4,160,256]{2,1,0:T(8,128)(2,1)S(1)}, u32[]{:S(2)}, u32[]{:S(2)}) collective-permute-start(bf16[4,160,256]{2,1,0:T(8,128)(2,1)S(1)} %get-tuple-element.175), channel_id=1, source_target_pairs={{0,2},{1,3},{2,0},{3,1},{4,6},{5,7},{6,4},{7,5},{8,10},{9,11},{10,... | collective-permute-start | bytes 983048 | tf_op jit(solution)/shard_map/ppermute | solution.py:495
  85.9 14.5 %collective-permute-start.27 = (bf16[4,160,256]{2,1,0:T(8,128)(2,1)S(1)}, bf16[4,160,256]{2,1,0:T(8,128)(2,1)S(1)}, u32[]{:S(2)}, u32[]{:S(2)}) collective-permute-start(bf16[4,160,256]{2,1,0:T(8,128)(2,1)S(1)} %get-tuple-element.176), channel_id=1, source_target_pairs={{0,3},{1,0},{2,1},{3,2},{4,7},{5,4},{6,5},{7,6},{8,11},{9,8},{10,9... | collective-permute-start | bytes 983048 | tf_op jit(solution)/shard_map/ppermute | solution.py:495
  88.3 13.6 %collective-permute-start.25 = (bf16[4,160,256]{2,1,0:T(8,128)(2,1)S(1)}, bf16[4,160,256]{2,1,0:T(8,128)(2,1)S(1)}, u32[]{:S(2)}, u32[]{:S(2)}) collective-permute-start(bf16[4,160,256]{2,1,0:T(8,128)(2,1)S(1)} %get-tuple-element.174), channel_id=1, source_target_pairs={{0,1},{1,2},{2,3},{3,0},{4,5},{5,6},{6,7},{7,4},{8,9},{9,10},{10,1... | collective-permute-start | bytes 983048 | tf_op jit(solution)/shard_map/ppermute | solution.py:495
  88.3 13.8 %collective-permute-start.24 = (bf16[160,1024]{1,0:T(8,128)(2,1)S(1)}, bf16[160,1024]{1,0:T(8,128)(2,1)S(1)}, u32[]{:S(2)}, u32[]{:S(2)}) collective-permute-start(bf16[160,1024]{1,0:T(8,128)(2,1)S(1)} %get-tuple-element.172), channel_id=1, source_target_pairs={{0,8},{1,9},{2,10},{3,11},{4,12},{5,13},{6,14},{7,15},{8,0},{9,1},... | collective-permute-start | bytes 983048 | tf_op jit(solution)/shard_map/ppermute | solution.py:491
  102.3 4.6 %collective-permute-start.28 = (bf16[4,160,1024]{2,1,0:T(8,128)(2,1)S(1)}, bf16[4,160,1024]{2,1,0:T(8,128)(2,1)S(1)}, u32[]{:S(2)}, u32[]{:S(2)}) collective-permute-start(bf16[4,160,1024]{2,1,0:T(8,128)(2,1)S(1)} %pad_maximum_fusion.1.mine), channel_id=1, source_target_pairs={{0,16},{16,0},{32,48},{48,32},{64,80},{80,64},{96,112},{112,96},{1... | collective-permute-start | bytes 3932168 | tf_op jit(solution)/shard_map/ppermute | solution.py:499
  102.9 8.4 %collective-permute-start.29 = (bf16[160,256]{1,0:T(8,128)(2,1)S(1)}, bf16[160,256]{1,0:T(8,128)(2,1)S(1)}, u32[]{:S(2)}, u32[]{:S(2)}) collective-permute-start(bf16[160,256]{1,0:T(8,128)(2,1)S(1)} %get-tuple-element.181), channel_id=1, source_target_pairs={{0,4},{1,5},{2,6},{3,7},{4,8},{5,9},{6,10},{7,11},{8,12},{9,13},{1... | collective-permute-start | bytes 245768 | tf_op jit(solution)/shard_map/ppermute | solution.py:491
  103.8 7.5 %collective-permute-start.30 = (bf16[160,256]{1,0:T(8,128)(2,1)S(1)}, bf16[160,256]{1,0:T(8,128)(2,1)S(1)}, u32[]{:S(2)}, u32[]{:S(2)}) collective-permute-start(bf16[160,256]{1,0:T(8,128)(2,1)S(1)} %get-tuple-element.182), channel_id=1, source_target_pairs={{0,8},{1,9},{2,10},{3,11},{4,12},{5,13},{6,14},{7,15},{8,0},{9,1},... | collective-permute-start | bytes 245768 | tf_op jit(solution)/shard_map/ppermute | solution.py:491
  105.9 5.4 %collective-permute-start.31 = (bf16[160,256]{1,0:T(8,128)(2,1)S(1)}, bf16[160,256]{1,0:T(8,128)(2,1)S(1)}, u32[]{:S(2)}, u32[]{:S(2)}) collective-permute-start(bf16[160,256]{1,0:T(8,128)(2,1)S(1)} %get-tuple-element.183), channel_id=1, source_target_pairs={{0,12},{1,13},{2,14},{3,15},{4,0},{5,1},{6,2},{7,3},{8,4},{9,5},{1... | collective-permute-start | bytes 245768 | tf_op jit(solution)/shard_map/ppermute | solution.py:491
  111.3 2.8 %collective-permute-start.32 = (bf16[4,160,256]{2,1,0:T(8,128)(2,1)S(1)}, bf16[4,160,256]{2,1,0:T(8,128)(2,1)S(1)}, u32[]{:S(2)}, u32[]{:S(2)}) collective-permute-start(bf16[4,160,256]{2,1,0:T(8,128)(2,1)S(1)} %pad_maximum_fusion.3.sums), channel_id=1, source_target_pairs={{0,16},{16,0},{32,48},{48,32},{64,80},{80,64},{96,112},{112,96},{1... | collective-permute-start | bytes 983048 | tf_op jit(solution)/shard_map/ppermute | solution.py:499

commit v4 on v3

--- a/solution.py
+++ b/solution.py
@@ -152,36 +152,36 @@
     return 2 * lax.rem(z + shift, 4) + core, core
 
 
-def pack_kv_kernel(k, v, k_in, v_in, sel, sel_in, *outs):
+def pack_kv_kernel(own, come, sel, sel_in, *outs):
     def fill(dense, few, few_sel):
         pick = compact(few_sel)
         mark = INVALID * (1.0 - jnp.sum(pick.astype(F32), axis=1, keepdims=True))
         for step, out in enumerate(outs):
-            here = pl.ds(pl.multiple_of(own_head(step)[0] * HEAD, HEAD), HEAD)
             for side in range(2):
+                here = pl.ds(pl.multiple_of(own_head(step)[0] * HEAD + side * HALF, HEAD), HEAD)
                 cols = slice(side * HEAD, (side + 1) * HEAD)
-                out[:ROWS, cols] = dense[side][:, here]
-                rows = dot(pick, few[side][:, here])
+                out[:ROWS, cols] = dense[:, here]
+                rows = dot(pick, few[:, here])
                 out[ROWS:, cols] = (rows if side else rows + mark).astype(BF)
 
     @pl.when(own_head(0)[1] == 1)
     def _():
-        fill((k, v), (k_in, v_in), sel_in)
+        fill(own, come, sel_in)
 
     @pl.when(own_head(0)[1] == 0)
     def _():
-        fill((k_in, v_in), (k, v), sel)
-
-
-def pack_kv(k, v, k_in, v_in, sel, sel_in):
+        fill(come, own, sel)
+
+
+def pack_kv(own, come, sel, sel_in):
     return list(pl.pallas_call(
         pack_kv_kernel,
         out_shape=[jax.ShapeDtypeStruct((SENT, KV), BF)] * 4,
-        in_specs=[VMEM] * 6,
+        in_specs=[VMEM] * 4,
         out_specs=[VMEM] * 4,
         compiler_params=PARAMS,
         name="pack_kv",
-    )(k, v, k_in, v_in, sel, sel_in))
+    )(own, come, sel, sel_in))
 
 
 def pack_kernel(own, come, sel, sel_in, o0, o1, o2, o3, held, sems):
@@ -208,14 +208,14 @@
             out[ROWS:, :] = dot(pick, held[step, 0]).astype(BF)
 
 
-def pack(own, come, sel, sel_in):
+def pack(own, come, sel, sel_in, params):
     return list(pl.pallas_call(
         pack_kernel,
         out_shape=[jax.ShapeDtypeStruct((SENT, HALF), BF)] * 4,
         in_specs=[ANY] * 2 + [VMEM] * 2,
         out_specs=[VMEM] * 4,
         scratch_shapes=[pltpu.VMEM((4, 2, ROWS, HALF), BF), pltpu.SemaphoreType.DMA((8,))],
-        compiler_params=WHOLE,
+        compiler_params=params,
         name="pack",
     )(own, come, sel, sel_in))
 
@@ -513,11 +513,12 @@
     seg, q, k, v, g = (x[0] for x in (segment_input, queries, keys, values, cotangent))
     sel = jnp.where(jnp.arange(ROWS, dtype=jnp.int32)[None, :] < counts, selected, -1)
 
-    k_in, v_in, sel_in = swap(k), swap(v), swap(sel)
-    kv = pack_kv(k, v, k_in, v_in, sel, sel_in)
-    q, g, *_ = both(q, g, k_in, v_in, sel_in)
+    own = jnp.concatenate([k, v], 1)
+    come, sel_in = swap(own), swap(sel)
+    kv = pack_kv(own, come, sel, sel_in)
+    q, g, *_ = both(q, g, come, sel_in)
     q_in, g_in = swap(q), swap(g)
-    qs = pack(q, q_in, sel, sel_in)
+    qs = pack(q, q_in, sel, sel_in, WHOLE)
     for by in (1, 3, 2):
         kv[by] = along_z(kv[by], by)
     kv[1], kv[2], kv[3], qs[1], qs[2], qs[3], g_in = both(kv[1], kv[2], kv[3], qs[1], qs[2], qs[3], g_in)
@@ -526,7 +527,7 @@
     qs[1], qs[2], qs[3], g_in, _ = both(qs[1], qs[2], qs[3], g_in, column)
     for by in (1, 3, 2):
         qs[by] = along_z(qs[by], by)
-    gs = pack(g, g_in, sel, sel_in)
+    gs = pack(g, g_in, sel, sel_in, PARAMS)
 
     qs[0], qs[1], qs[3] = both(qs[0], qs[1], qs[3])
     (own,), keyed = forward((0,), info, [qs[0]], kvs=kvs)

time: 116 us -> 114 us (0.983)
  local copies, waits for them, and re-layouts: 3.24 us -> 1.3 us
  Pallas kernels: 45.4 us -> 44.1 us
    unnamed x20 -> x18, local copies, waits for them, and re-layouts: 3.24 us -> 1.3 us
    pallas_call x2, Pallas kernels: 7.23 us -> 5.59 us  [pack(): pl.pallas_call(pack_kernel, out_shape=[jax.ShapeDtypeStruct((SENT, HALF),...]
    ppermute x8 -> x7, starting transfers between devices: 7.85 us -> 7.46 us  [swap(): return lax.ppermute(x, 'section', [(i, i ^ 1) for i in range(8)])]
    ppermute x8 -> x7, waiting for transfers between devices: 3.1 us -> 3.31 us  [swap(): return lax.ppermute(x, 'section', [(i, i ^ 1) for i in range(8)])]
  transfers between devices with their start and end apart: 33 -> 32, of which waited for: 10 -> 9; matrix products, arithmetic and copies ran while one was open for 1% -> 1% of each run, Pallas kernels for 38% -> 38%
where the time goes in v4:
time: 114 us; the launch traced here: 113 us
  Pallas kernels  44.1 us (39%)
  starting transfers between devices  39.9 us (35%)
  waiting for transfers between devices  24.4 us (21%)
  other arithmetic  2.22 us (2%)
  between operations  1.5 us (1%)
  local copies, waits for them, and re-layouts  1.3 us (1%)
    ppermute x18, starting transfers between devices, along_z(): lax.ppermute(x, 'ctx', [(4 * z + y, 4 * ((z + by) % 4) + y) for z in rang...  22.2 us
    ppermute x6, waiting for transfers between devices, along_y(): lax.ppermute(x, 'ctx', [(4 * z + y, 4 * z + (y + by) % 4) for z in range(...  18.1 us
    pallas_call x2, Pallas kernels, forward(): pl.pallas_call(functools.partial(forward_kernel, shifts, first), out_shap...  15.6 us
    pallas_call x1, Pallas kernels, backward(): pl.pallas_call(functools.partial(backward_kernel, shifts), out_shape=shap...  15.2 us
    ppermute x7, starting transfers between devices, swap(): return lax.ppermute(x, 'section', [(i, i ^ 1) for i in range(8)])  7.46 us
    ppermute x6, starting transfers between devices, along_y(): lax.ppermute(x, 'ctx', [(4 * z + y, 4 * z + (y + by) % 4) for z in range(...  6.23 us
    pallas_call x2, Pallas kernels, pack(): pl.pallas_call(pack_kernel, out_shape=[jax.ShapeDtypeStruct((SENT, HALF),...  5.59 us
    ppermute x1, starting transfers between devices, onward(): return lax.ppermute(x, 'section', [(i, i + 1) for i in range(7)])  3.96 us
  transfers between devices with their start and end apart: 32, of which 9 were waited for; matrix products, arithmetic and copies ran while one was open for 1% of the time, Pallas kernels for 38%

profile of v4, /device:TPU:1, one launch (start us, length us, event | category | flops | bytes accessed | tf_op | source)
XLA Modules:
  0.0 113.4 jit_solution(632945100920012086)
XLA Ops:
  0.6 1.1 pad_maximum_fusion.2.own
  1.7 1.5 %collective-permute-start = (bf16[128,2048]{1,0:T(8,128)(2,1)S(1)}, bf16[128,2048]{1,0:T(8,128)(2,1)S(1)}, u32[]{:S(2)}, u32[]{:S(2)}) collective-permute-start(bf16[128,2048]{1,0:T(8,128)(2,1)S(1)} %pad_maximum_fusion.2.own), channel_id=1, source_target_pairs={{0,16},{16,0},{32,48},{48,32},{64,80},{80,64},{96,112},{112,96},{1... | collective-permute-start | bytes 1572872 | tf_op jit(solution)/shard_map/ppermute | solution.py:499
  3.9 0.7 compare_select_fusion.sel
  4.5 0.0 collective-permute-start.1
  4.5 1.1 collective-permute-done.1.sel_in
  5.6 0.0 collective-permute-done.come
  5.6 0.2 collective-permute-start.2
  5.9 0.3 collective-permute-start.6
  6.2 0.3 pack_kv.1
  6.4 1.8 %collective-permute-start.3 = (bf16[160,256]{1,0:T(8,128)(2,1)S(1)}, bf16[160,256]{1,0:T(8,128)(2,1)S(1)}, u32[]{:S(2)}, u32[]{:S(2)}) collective-permute-start(bf16[160,256]{1,0:T(8,128)(2,1)S(1)} %get-tuple-element.100), channel_id=1, source_target_pairs={{0,4},{1,5},{2,6},{3,7},{4,8},{5,9},{6,10},{7,11},{8,12},{9,13},{1... | collective-permute-start | bytes 245768 | tf_op jit(solution)/shard_map/ppermute | solution.py:491
  8.2 3.3 %collective-permute-start.4 = (bf16[160,256]{1,0:T(8,128)(2,1)S(1)}, bf16[160,256]{1,0:T(8,128)(2,1)S(1)}, u32[]{:S(2)}, u32[]{:S(2)}) collective-permute-start(bf16[160,256]{1,0:T(8,128)(2,1)S(1)} %get-tuple-element.101), channel_id=1, source_target_pairs={{0,8},{1,9},{2,10},{3,11},{4,12},{5,13},{6,14},{7,15},{8,0},{9,1},... | collective-permute-start | bytes 245768 | tf_op jit(solution)/shard_map/ppermute | solution.py:491
  11.5 0.7 collective-permute-start.5
  12.2 0.0 copy-start
  12.3 3.7 %pack.2 = (bf16[160,1024]{1,0:T(8,128)(2,1)}, bf16[160,1024]{1,0:T(8,128)(2,1)}, bf16[160,1024]{1,0:T(8,128)(2,1)}, bf16[160,1024]{1,0:T(8,128)(2,1)}) custom-call(bf16[128,8192]{1,0:T(8,128)(2,1)} %bitcast.38, bf16[128,8192]{1,0:T(8,128)(2,1)} %collective-permute-done.2.come, s32[1,128]{1,0:T(1,128)} %copy-done.2, s32[1,128]{1,0:T(1,128)} %copy-done.5), custom_call_target="tpu_custom_call" | custom-call | tf_op jit(solution)/shard_map/pack/pallas_call | solution.py:212
  16.0 0.0 collective-permute-done.3
  16.0 0.0 collective-permute-done.5
  16.0 0.0 collective-permute-done.6.come
  16.1 0.8 collective-permute-start.7
  16.9 1.9 %collective-permute-start.8 = (bf16[160,1024]{1,0:T(8,128)(2,1)}, bf16[160,1024]{1,0:T(8,128)(2,1)S(1)}, u32[]{:S(2)}, u32[]{:S(2)}) collective-permute-start(bf16[160,1024]{1,0:T(8,128)(2,1)} %get-tuple-element.116), channel_id=1, source_target_pairs={{0,12},{1,13},{2,14},{3,15},{4,0},{5,1},{6,2},{7,3},{8,4},{9,5},{1... | collective-permute-start | bytes 983048 | tf_op jit(solution)/shard_map/ppermute | solution.py:491
  18.9 1.3 %collective-permute-start.9 = (bf16[4,160,256]{2,1,0:T(8,128)(2,1)S(1)}, bf16[4,160,256]{2,1,0:T(8,128)(2,1)S(1)}, u32[]{:S(2)}, u32[]{:S(2)}) collective-permute-start(bf16[4,160,256]{2,1,0:T(8,128)(2,1)S(1)} %pad_maximum_fusion.3.refs_1_), channel_id=1, source_target_pairs={{0,1},{1,2},{2,3},{3,0},{4,5},{5,6},{6,7},{7,4},{8,9},{9,10},{10,1... | collective-permute-start | bytes 983048 | tf_op jit(solution)/shard_map/ppermute | solution.py:495
  20.2 2.6 %collective-permute-start.10 = (bf16[4,160,256]{2,1,0:T(8,128)(2,1)S(1)}, bf16[4,160,256]{2,1,0:T(8,128)(2,1)}, u32[]{:S(2)}, u32[]{:S(2)}) collective-permute-start(bf16[4,160,256]{2,1,0:T(8,128)(2,1)S(1)} %pad_maximum_fusion.3.refs_1_), channel_id=1, source_target_pairs={{0,2},{1,3},{2,0},{3,1},{4,6},{5,7},{6,4},{7,5},{8,10},{9,11},{10,... | collective-permute-start | bytes 983048 | tf_op jit(solution)/shard_map/ppermute | solution.py:495
  22.8 1.1 collective-permute-start.11
  23.8 0.1 pad_add_fusion.info
  23.9 0.6 copy-done.3
  24.5 0.7 copy-done.6
  25.2 1.8 %pack.3 = (bf16[160,1024]{1,0:T(8,128)(2,1)S(1)}, bf16[160,1024]{1,0:T(8,128)(2,1)S(1)}, bf16[160,1024]{1,0:T(8,128)(2,1)S(1)}, bf16[160,1024]{1,0:T(8,128)(2,1)S(1)}) custom-call(bf16[128,8192]{1,0:T(8,128)(2,1)S(1)} %bitcast.31, bf16[128,8192]{1,0:T(8,128)(2,1)} %collective-permute-done.6.come, s32[1,128]{1,0:T(1,128)S(1)} %copy-done.3, s32[1,128]{1,0:T(1,128)S(1)} %copy-done.6), custom_call_target="tpu_custom_call" | custom-call | tf_op jit(solution)/shard_map/pack/pallas_call | solution.py:212
  27.1 0.4 collective-permute-start.12
  27.5 0.0 collective-permute-done.8.refs_1_
  27.5 0.7 collective-permute-start.16
  28.2 0.0 collective-permute-done.9.refs_2_
  28.3 1.9 %collective-permute-start.17 = (bf16[160,1024]{1,0:T(8,128)(2,1)S(1)}, bf16[160,1024]{1,0:T(8,128)(2,1)S(1)}, u32[]{:S(2)}, u32[]{:S(2)}) collective-permute-start(bf16[160,1024]{1,0:T(8,128)(2,1)S(1)} %get-tuple-element.136), channel_id=1, source_target_pairs={{0,12},{1,13},{2,14},{3,15},{4,0},{5,1},{6,2},{7,3},{8,4},{9,5},{1... | collective-permute-start | bytes 983048 | tf_op jit(solution)/shard_map/ppermute | solution.py:491
  30.2 5.8 %collective-permute-done.10.refs_3_ = bf16[4,160,256]{2,1,0:T(8,128)(2,1)} collective-permute-done((bf16[4,160,256]{2,1,0:T(8,128)(2,1)S(1)}, bf16[4,160,256]{2,1,0:T(8,128)(2,1)}, u32[]{:S(2)}, u32[]{:S(2)}) %collective-permute-start.10) | collective-permute-done | bytes 327712 | tf_op jit(solution)/shard_map/ppermute | solution.py:495
  36.0 0.5 collective-permute-start.18
  36.5 3.4 %forward.2 = (bf16[160,1024]{1,0:T(8,128)(2,1)S(1)}, bf16[2048,1024]{1,0:T(8,128)(2,1)S(1)}, f32[8,1024]{1,0:T(8,128)S(1)}, f32[128,1024]{1,0:T(8,128)S(1)}, bf1...) custom-call(s32[3]{0:T(128)S(1)} %pad_add_fusion.info, ...), custom_call_target="tpu_custom_call" | custom-call | flops 4000000000 | bytes 4194304 | tf_op jit(solution)/shard_map/forward/pallas_call | solution.py:319
  40.0 12.1 %forward.3 = (bf16[160,1024]{1,0:T(8,128)(2,1)S(1)}, bf16[2048,1024]{1,0:T(8,128)(2,1)S(1)}, f32[8,1024]{1,0:T(8,128)S(1)}, f32[128,1024]{1,0:T(8,128)S(1)}, bf1...) custom-call(s32[3]{0:T(128)S(1)} %pad_add_fusion.info, ...), custom_call_target="tpu_custom_call" | custom-call | flops 12000000000 | bytes 4194304 | tf_op jit(solution)/shard_map/forward/pallas_call | solution.py:319
  52.1 1.5 %collective-permute-start.13 = (bf16[160,1024]{1,0:T(8,128)(2,1)S(1)}, bf16[160,1024]{1,0:T(8,128)(2,1)S(1)}, u32[]{:S(2)}, u32[]{:S(2)}) collective-permute-start(bf16[160,1024]{1,0:T(8,128)(2,1)S(1)} %get-tuple-element.131), channel_id=1, source_target_pairs={{0,12},{1,13},{2,14},{3,15},{4,0},{5,1},{6,2},{7,3},{8,4},{9,5},{1... | collective-permute-start | bytes 983048 | tf_op jit(solution)/shard_map/ppermute | solution.py:491
  53.6 1.2 %collective-permute-start.14 = (bf16[160,1024]{1,0:T(8,128)(2,1)S(1)}, bf16[160,1024]{1,0:T(8,128)(2,1)S(1)}, u32[]{:S(2)}, u32[]{:S(2)}) collective-permute-start(bf16[160,1024]{1,0:T(8,128)(2,1)S(1)} %get-tuple-element.132), channel_id=1, source_target_pairs={{0,8},{1,9},{2,10},{3,11},{4,12},{5,13},{6,14},{7,15},{8,0},{9,1},... | collective-permute-start | bytes 983048 | tf_op jit(solution)/shard_map/ppermute | solution.py:491
  54.8 0.8 collective-permute-start.15
  55.5 15.2 %backward.1 = (bf16[160,1024]{1,0:T(8,128)(2,1)S(1)}, bf16[160,1024]{1,0:T(8,128)(2,1)S(1)}, bf16[160,1024]{1,0:T(8,128)(2,1)S(1)}, bf16[160,1024]{1,0:T(8,128)(...) custom-call(s32[3]{0:T(128)S(1)} %pad_add_fusion.info, ...), custom_call_target="tpu_custom_call" | custom-call | flops 24000000000 | bytes 4194304 | tf_op jit(solution)/shard_map/backward/pallas_call | solution.py:366
  70.8 0.5 collective-permute-done.15
  71.3 0.2 pad_maximum_fusion.mine
  71.4 3.3 %collective-permute-start.19 = (bf16[4,160,1024]{2,1,0:T(8,128)(2,1)S(1)}, bf16[4,160,1024]{2,1,0:T(8,128)(2,1)S(1)}, u32[]{:S(2)}, u32[]{:S(2)}) collective-permute-start(bf16[4,160,1024]{2,1,0:T(8,128)(2,1)S(1)} %pad_maximum_fusion.mine), channel_id=1, source_target_pairs={{0,16},{16,0},{32,48},{48,32},{64,80},{80,64},{96,112},{112,96},{1... | collective-permute-start | bytes 3932168 | tf_op jit(solution)/shard_map/ppermute | solution.py:499
  74.7 1.7 %collective-permute-start.21 = (bf16[160,1024]{1,0:T(8,128)(2,1)S(1)}, bf16[160,1024]{1,0:T(8,128)(2,1)S(1)}, u32[]{:S(2)}, u32[]{:S(2)}) collective-permute-start(bf16[160,1024]{1,0:T(8,128)(2,1)S(1)} %get-tuple-element.168), channel_id=1, source_target_pairs={{0,12},{1,13},{2,14},{3,15},{4,0},{5,1},{6,2},{7,3},{8,4},{9,5},{1... | collective-permute-start | bytes 983048 | tf_op jit(solution)/shard_map/ppermute | solution.py:491
  76.4 0.0 collective-permute-start.22
  76.4 0.9 collective-permute-done.19.theirs
  77.4 1.5 %update.1 = bf16[128,8192]{1,0:T(8,128)(2,1)S(1)} custom-call(s32[3]{0:T(128)S(1)} %pad_add_fusion.info, bf16[128,8192]{1,0:T(8,128)(2,1)S(1)} %bitcast.32, bf16[4,160,1024]{2,1,0:T(8,128)(2,1)S(1)} %pad_maximum_fusion.mine, bf16[4,160,1024]{2,1,0:T(8,128)(2,1)S(1)} %collective-permute-done.19.theirs, s32[1,128]{1,0:T(1,128)S(1)} %copy-done.4), custom_call_target="tpu_custom_call" | custom-call | tf_op jit(solution)/shard_map/update/pallas_call | solution.py:428
  78.9 4.0 %collective-permute-start.20 = (bf16[128,8192]{1,0:T(8,128)(2,1)S(1)}, bf16[128,8192]{1,0:T(8,128)(2,1)S(1)}, u32[]{:S(2)}, u32[]{:S(2)}) collective-permute-start(bf16[128,8192]{1,0:T(8,128)(2,1)S(1)} %update.1), channel_id=1, source_target_pairs={{0,16},{16,32},{32,48},{48,64},{64,80},{80,96},{96,112},{1,17},{17... | collective-permute-start | bytes 6291464 | tf_op jit(solution)/shard_map/ppermute | solution.py:503
  82.9 1.2 %collective-permute-start.25 = (bf16[4,160,256]{2,1,0:T(8,128)(2,1)S(1)}, bf16[4,160,256]{2,1,0:T(8,128)(2,1)S(1)}, u32[]{:S(2)}, u32[]{:S(2)}) collective-permute-start(bf16[4,160,256]{2,1,0:T(8,128)(2,1)S(1)} %get-tuple-element.175), channel_id=1, source_target_pairs={{0,2},{1,3},{2,0},{3,1},{4,6},{5,7},{6,4},{7,5},{8,10},{9,11},{10,... | collective-permute-start | bytes 983048 | tf_op jit(solution)/shard_map/ppermute | solution.py:495
  84.1 2.5 %collective-permute-done.22 = bf16[160,1024]{1,0:T(8,128)(2,1)S(1)} collective-permute-done((bf16[160,1024]{1,0:T(8,128)(2,1)S(1)}, bf16[160,1024]{1,0:T(8,128)(2,1)S(1)}, u32[]{:S(2)}, u32[]{:S(2)}) %collective-permute-start.22) | collective-permute-done | bytes 327712 | tf_op jit(solution)/shard_map/ppermute | solution.py:491
  86.6 1.3 %collective-permute-start.23 = (bf16[160,1024]{1,0:T(8,128)(2,1)S(1)}, bf16[160,1024]{1,0:T(8,128)(2,1)S(1)}, u32[]{:S(2)}, u32[]{:S(2)}) collective-permute-start(bf16[160,1024]{1,0:T(8,128)(2,1)S(1)} %get-tuple-element.172), channel_id=1, source_target_pairs={{0,8},{1,9},{2,10},{3,11},{4,12},{5,13},{6,14},{7,15},{8,0},{9,1},... | collective-permute-start | bytes 983048 | tf_op jit(solution)/shard_map/ppermute | solution.py:491
  87.9 6.3 %collective-permute-done.25.c = bf16[4,160,256]{2,1,0:T(8,128)(2,1)S(1)} collective-permute-done((bf16[4,160,256]{2,1,0:T(8,128)(2,1)S(1)}, bf16[4,160,256]{2,1,0:T(8,128)(2,1)S(1)}, u32[]{:S(2)}, u32[]{:S(2)}) %collective-permute-start.25) | collective-permute-done | bytes 327712 | tf_op jit(solution)/shard_map/ppermute | solution.py:495
  94.2 3.9 %collective-permute-done.26.d = bf16[4,160,256]{2,1,0:T(8,128)(2,1)S(1)} collective-permute-done((bf16[4,160,256]{2,1,0:T(8,128)(2,1)S(1)}, bf16[4,160,256]{2,1,0:T(8,128)(2,1)S(1)}, u32[]{:S(2)}, u32[]{:S(2)}) %collective-permute-start.26) | collective-permute-done | bytes 327712 | tf_op jit(solution)/shard_map/ppermute | solution.py:495
  98.1 2.0 %collective-permute-done.24.b = bf16[4,160,256]{2,1,0:T(8,128)(2,1)S(1)} collective-permute-done((bf16[4,160,256]{2,1,0:T(8,128)(2,1)S(1)}, bf16[4,160,256]{2,1,0:T(8,128)(2,1)S(1)}, u32[]{:S(2)}, u32[]{:S(2)}) %collective-permute-start.24) | collective-permute-done | bytes 327712 | tf_op jit(solution)/shard_map/ppermute | solution.py:495
  100.2 0.2 fold_sums.1
  100.3 0.2 pad_maximum_fusion.1.mine
  100.5 0.6 collective-permute-start.27
  101.1 0.7 collective-permute-start.28
  101.8 2.3 %collective-permute-start.29 = (bf16[160,256]{1,0:T(8,128)(2,1)S(1)}, bf16[160,256]{1,0:T(8,128)(2,1)S(1)}, u32[]{:S(2)}, u32[]{:S(2)}) collective-permute-start(bf16[160,256]{1,0:T(8,128)(2,1)S(1)} %get-tuple-element.182), channel_id=1, source_target_pairs={{0,8},{1,9},{2,10},{3,11},{4,12},{5,13},{6,14},{7,15},{8,0},{9,1},... | collective-permute-start | bytes 245768 | tf_op jit(solution)/shard_map/ppermute | solution.py:491
  104.1 0.6 collective-permute-start.30
  104.7 2.4 %finish_q.1 = bf16[128,8192]{1,0:T(8,128)(2,1)} custom-call(s32[3]{0:T(128)S(1)} %pad_add_fusion.info, bf16[4,160,1024]{2,1,0:T(8,128)(2,1)S(1)} %pad_maximum_fusion.1.mine, bf16[4,160,1024]{2,1,0:T(8,128)(2,1)S(1)} %collective-permute-done.27.theirs, s32[1,128]{1,0:T(1,128)S(1)} %copy-done.4), custom_call_target="tpu_custom_call" | custom-call | tf_op jit(solution)/shard_map/finish_q/pallas_call | solution.py:428
  107.2 1.9 %settle.1 = bf16[128,8192]{1,0:T(8,128)(2,1)} custom-call(bf16[128,8192]{1,0:T(8,128)(2,1)S(1)} %collective-permute-done.20.x), custom_call_target="tpu_custom_call" | custom-call | tf_op jit(solution)/shard_map/settle/pallas_call | solution.py:448
  109.2 1.6 %collective-permute-start.31 = (bf16[4,160,256]{2,1,0:T(8,128)(2,1)S(1)}, bf16[4,160,256]{2,1,0:T(8,128)(2,1)S(1)}, u32[]{:S(2)}, u32[]{:S(2)}) collective-permute-start(bf16[4,160,256]{2,1,0:T(8,128)(2,1)S(1)} %pad_maximum_fusion.4.sums), channel_id=1, source_target_pairs={{0,16},{16,0},{32,48},{48,32},{64,80},{80,64},{96,112},{112,96},{1... | collective-permute-start | bytes 983048 | tf_op jit(solution)/shard_map/ppermute | solution.py:499
  110.8 1.3 %collective-permute-done.31.sums_in = bf16[4,160,256]{2,1,0:T(8,128)(2,1)S(1)} collective-permute-done((bf16[4,160,256]{2,1,0:T(8,128)(2,1)S(1)}, bf16[4,160,256]{2,1,0:T(8,128)(2,1)S(1)}, u32[]{:S(2)}, u32[]{:S(2)}) %collective-permute-start.31) | collective-permute-done | bytes 327712 | tf_op jit(solution)/shard_map/ppermute | solution.py:499
  112.0 1.4 %finish_kv.1 = (bf16[128,1024]{1,0:T(8,128)(2,1)}, bf16[128,1024]{1,0:T(8,128)(2,1)}) custom-call(s32[3]{0:T(128)S(1)} %pad_add_fusion.info, bf16[4,160,256]{2,1,0:T(8,128)(2,1)S(1)} %pad_maximum_fusion.4.sums, bf16[4,160,256]{2,1,0:T(8,128)(2,1)S(1)} %collective-permute-done.31.sums_in, s32[1,128]{1,0:T(1,128)S(1)} %copy-done.4), custom_call_target="tpu_custom_call" | custom-call | tf_op jit(solution)/shard_map/finish_kv/pallas_call | solution.py:480
  (36 shorter events, 0.2 us)
Async XLA Ops:
  1.7 3.9 %collective-permute-start = (bf16[128,2048]{1,0:T(8,128)(2,1)S(1)}, bf16[128,2048]{1,0:T(8,128)(2,1)S(1)}, u32[]{:S(2)}, u32[]{:S(2)}) collective-permute-start(bf16[128,2048]{1,0:T(8,128)(2,1)S(1)} %pad_maximum_fusion.2.own), channel_id=1, source_target_pairs={{0,16},{16,0},{32,48},{48,32},{64,80},{80,64},{96,112},{112,96},{1... | collective-permute-start | bytes 1572872 | tf_op jit(solution)/shard_map/ppermute | solution.py:499
  4.5 7.7 %copy-start.2 = (s32[1,128]{1,0:T(1,128)}, s32[1,128]{1,0:T(1,128)S(1)}, u32[]{:S(2)}) copy-start(s32[1,128]{1,0:T(1,128)S(1)} %compare_select_fusion.sel) | copy-start | bytes 1540
  4.5 1.1 collective-permute-start.1
  5.6 6.6 %copy-start.5 = (s32[1,128]{1,0:T(1,128)}, s32[1,128]{1,0:T(1,128)S(1)}, u32[]{:S(2)}) copy-start(s32[1,128]{1,0:T(1,128)S(1)} %collective-permute-done.1.sel_in) | copy-start | bytes 1540
  5.6 6.6 %collective-permute-start.2 = (bf16[128,8192]{1,0:T(8,128)(2,1)}, bf16[128,8192]{1,0:T(8,128)(2,1)}, u32[]{:S(2)}, u32[]{:S(2)}) collective-permute-start(bf16[128,8192]{1,0:T(8,128)(2,1)} %bitcast.37), channel_id=1, source_target_pairs={{0,16},{16,0},{32,48},{48,32},{64,80},{80,64},{96,112},{112,96},{1... | collective-permute-start | bytes 6291464 | tf_op jit(solution)/shard_map/ppermute | solution.py:499
  5.9 10.2 %collective-permute-start.6 = (bf16[128,8192]{1,0:T(8,128)(2,1)}, bf16[128,8192]{1,0:T(8,128)(2,1)}, u32[]{:S(2)}, u32[]{:S(2)}) collective-permute-start(bf16[128,8192]{1,0:T(8,128)(2,1)} %bitcast.30), channel_id=1, source_target_pairs={{0,16},{16,0},{32,48},{48,32},{64,80},{80,64},{96,112},{112,96},{1... | collective-permute-start | bytes 6291464 | tf_op jit(solution)/shard_map/ppermute | solution.py:499
  6.4 9.6 %collective-permute-start.3 = (bf16[160,256]{1,0:T(8,128)(2,1)S(1)}, bf16[160,256]{1,0:T(8,128)(2,1)S(1)}, u32[]{:S(2)}, u32[]{:S(2)}) collective-permute-start(bf16[160,256]{1,0:T(8,128)(2,1)S(1)} %get-tuple-element.100), channel_id=1, source_target_pairs={{0,4},{1,5},{2,6},{3,7},{4,8},{5,9},{6,10},{7,11},{8,12},{9,13},{1... | collective-permute-start | bytes 245768 | tf_op jit(solution)/shard_map/ppermute | solution.py:491
  8.2 7.8 %collective-permute-start.4 = (bf16[160,256]{1,0:T(8,128)(2,1)S(1)}, bf16[160,256]{1,0:T(8,128)(2,1)S(1)}, u32[]{:S(2)}, u32[]{:S(2)}) collective-permute-start(bf16[160,256]{1,0:T(8,128)(2,1)S(1)} %get-tuple-element.101), channel_id=1, source_target_pairs={{0,8},{1,9},{2,10},{3,11},{4,12},{5,13},{6,14},{7,15},{8,0},{9,1},... | collective-permute-start | bytes 245768 | tf_op jit(solution)/shard_map/ppermute | solution.py:491
  11.5 4.5 %collective-permute-start.5 = (bf16[160,256]{1,0:T(8,128)(2,1)S(1)}, bf16[160,256]{1,0:T(8,128)(2,1)S(1)}, u32[]{:S(2)}, u32[]{:S(2)}) collective-permute-start(bf16[160,256]{1,0:T(8,128)(2,1)S(1)} %get-tuple-element.102), channel_id=1, source_target_pairs={{0,12},{1,13},{2,14},{3,15},{4,0},{5,1},{6,2},{7,3},{8,4},{9,5},{1... | collective-permute-start | bytes 245768 | tf_op jit(solution)/shard_map/ppermute | solution.py:491
  12.2 11.7 %copy-start = (bf16[1,128,8192]{2,1,0:T(8,128)(2,1)S(1)}, bf16[1,128,8192]{2,1,0:T(8,128)(2,1)}, u32[]{:S(2)}) copy-start(bf16[1,128,8192]{2,1,0:T(8,128)(2,1)} %param.11) | copy-start | bytes 6291460
  16.1 10.9 %collective-permute-start.7 = (bf16[160,1024]{1,0:T(8,128)(2,1)}, bf16[160,1024]{1,0:T(8,128)(2,1)S(1)}, u32[]{:S(2)}, u32[]{:S(2)}) collective-permute-start(bf16[160,1024]{1,0:T(8,128)(2,1)} %get-tuple-element.115), channel_id=1, source_target_pairs={{0,4},{1,5},{2,6},{3,7},{4,8},{5,9},{6,10},{7,11},{8,12},{9,13},{1... | collective-permute-start | bytes 983048 | tf_op jit(solution)/shard_map/ppermute | solution.py:491
  16.9 10.6 %collective-permute-start.8 = (bf16[160,1024]{1,0:T(8,128)(2,1)}, bf16[160,1024]{1,0:T(8,128)(2,1)S(1)}, u32[]{:S(2)}, u32[]{:S(2)}) collective-permute-start(bf16[160,1024]{1,0:T(8,128)(2,1)} %get-tuple-element.116), channel_id=1, source_target_pairs={{0,12},{1,13},{2,14},{3,15},{4,0},{5,1},{6,2},{7,3},{8,4},{9,5},{1... | collective-permute-start | bytes 983048 | tf_op jit(solution)/shard_map/ppermute | solution.py:491
  18.9 9.4 %collective-permute-start.9 = (bf16[4,160,256]{2,1,0:T(8,128)(2,1)S(1)}, bf16[4,160,256]{2,1,0:T(8,128)(2,1)S(1)}, u32[]{:S(2)}, u32[]{:S(2)}) collective-permute-start(bf16[4,160,256]{2,1,0:T(8,128)(2,1)S(1)} %pad_maximum_fusion.3.refs_1_), channel_id=1, source_target_pairs={{0,1},{1,2},{2,3},{3,0},{4,5},{5,6},{6,7},{7,4},{8,9},{9,10},{10,1... | collective-permute-start | bytes 983048 | tf_op jit(solution)/shard_map/ppermute | solution.py:495
  20.2 15.9 %collective-permute-start.10 = (bf16[4,160,256]{2,1,0:T(8,128)(2,1)S(1)}, bf16[4,160,256]{2,1,0:T(8,128)(2,1)}, u32[]{:S(2)}, u32[]{:S(2)}) collective-permute-start(bf16[4,160,256]{2,1,0:T(8,128)(2,1)S(1)} %pad_maximum_fusion.3.refs_1_), channel_id=1, source_target_pairs={{0,2},{1,3},{2,0},{3,1},{4,6},{5,7},{6,4},{7,5},{8,10},{9,11},{10,... | collective-permute-start | bytes 983048 | tf_op jit(solution)/shard_map/ppermute | solution.py:495
  22.8 13.7 %collective-permute-start.11 = (bf16[4,160,256]{2,1,0:T(8,128)(2,1)S(1)}, bf16[4,160,256]{2,1,0:T(8,128)(2,1)}, u32[]{:S(2)}, u32[]{:S(2)}) collective-permute-start(bf16[4,160,256]{2,1,0:T(8,128)(2,1)S(1)} %pad_maximum_fusion.3.refs_1_), channel_id=1, source_target_pairs={{0,3},{1,0},{2,1},{3,2},{4,7},{5,4},{6,5},{7,6},{8,11},{9,8},{10,9... | collective-permute-start | bytes 983048 | tf_op jit(solution)/shard_map/ppermute | solution.py:495
  23.9 0.6 copy-start.3
  24.5 0.7 copy-start.6
  25.2 1.9 %copy-start.8 = (bf16[160,1024]{1,0:T(8,128)(2,1)S(1)}, bf16[160,1024]{1,0:T(8,128)(2,1)}, u32[]{:S(2)}) copy-start(bf16[160,1024]{1,0:T(8,128)(2,1)} %get-tuple-element.121) | copy-start | bytes 983044
  25.2 11.3 %copy-start.7 = (bf16[160,1024]{1,0:T(8,128)(2,1)S(1)}, bf16[160,1024]{1,0:T(8,128)(2,1)}, u32[]{:S(2)}) copy-start(bf16[160,1024]{1,0:T(8,128)(2,1)} %get-tuple-element.117.refs_0_.refs_2_) | copy-start | bytes 983044
  27.1 12.9 %collective-permute-start.12 = (bf16[160,1024]{1,0:T(8,128)(2,1)S(1)}, bf16[160,1024]{1,0:T(8,128)(2,1)S(1)}, u32[]{:S(2)}, u32[]{:S(2)}) collective-permute-start(bf16[160,1024]{1,0:T(8,128)(2,1)S(1)} %copy-done.8), channel_id=1, source_target_pairs={{0,8},{1,9},{2,10},{3,11},{4,12},{5,13},{6,14},{7,15},{8,0},{9,1},... | collective-permute-start | bytes 983048 | tf_op jit(solution)/shard_map/ppermute | solution.py:491
  27.5 27.3 %collective-permute-start.16 = (bf16[160,1024]{1,0:T(8,128)(2,1)S(1)}, bf16[160,1024]{1,0:T(8,128)(2,1)S(1)}, u32[]{:S(2)}, u32[]{:S(2)}) collective-permute-start(bf16[160,1024]{1,0:T(8,128)(2,1)S(1)} %get-tuple-element.135), channel_id=1, source_target_pairs={{0,4},{1,5},{2,6},{3,7},{4,8},{5,9},{6,10},{7,11},{8,12},{9,13},{1... | collective-permute-start | bytes 983048 | tf_op jit(solution)/shard_map/ppermute | solution.py:491
  28.3 27.3 %collective-permute-start.17 = (bf16[160,1024]{1,0:T(8,128)(2,1)S(1)}, bf16[160,1024]{1,0:T(8,128)(2,1)S(1)}, u32[]{:S(2)}, u32[]{:S(2)}) collective-permute-start(bf16[160,1024]{1,0:T(8,128)(2,1)S(1)} %get-tuple-element.136), channel_id=1, source_target_pairs={{0,12},{1,13},{2,14},{3,15},{4,0},{5,1},{6,2},{7,3},{8,4},{9,5},{1... | collective-permute-start | bytes 983048 | tf_op jit(solution)/shard_map/ppermute | solution.py:491
  36.0 19.5 %collective-permute-start.18 = (bf16[160,1024]{1,0:T(8,128)(2,1)S(1)}, bf16[160,1024]{1,0:T(8,128)(2,1)S(1)}, u32[]{:S(2)}, u32[]{:S(2)}) collective-permute-start(bf16[160,1024]{1,0:T(8,128)(2,1)S(1)} %get-tuple-element.138), channel_id=1, source_target_pairs={{0,8},{1,9},{2,10},{3,11},{4,12},{5,13},{6,14},{7,15},{8,0},{9,1},... | collective-permute-start | bytes 983048 | tf_op jit(solution)/shard_map/ppermute | solution.py:491
  52.1 18.7 %collective-permute-start.13 = (bf16[160,1024]{1,0:T(8,128)(2,1)S(1)}, bf16[160,1024]{1,0:T(8,128)(2,1)S(1)}, u32[]{:S(2)}, u32[]{:S(2)}) collective-permute-start(bf16[160,1024]{1,0:T(8,128)(2,1)S(1)} %get-tuple-element.131), channel_id=1, source_target_pairs={{0,12},{1,13},{2,14},{3,15},{4,0},{5,1},{6,2},{7,3},{8,4},{9,5},{1... | collective-permute-start | bytes 983048 | tf_op jit(solution)/shard_map/ppermute | solution.py:491
  53.6 17.2 %collective-permute-start.14 = (bf16[160,1024]{1,0:T(8,128)(2,1)S(1)}, bf16[160,1024]{1,0:T(8,128)(2,1)S(1)}, u32[]{:S(2)}, u32[]{:S(2)}) collective-permute-start(bf16[160,1024]{1,0:T(8,128)(2,1)S(1)} %get-tuple-element.132), channel_id=1, source_target_pairs={{0,8},{1,9},{2,10},{3,11},{4,12},{5,13},{6,14},{7,15},{8,0},{9,1},... | collective-permute-start | bytes 983048 | tf_op jit(solution)/shard_map/ppermute | solution.py:491
  54.8 16.5 %collective-permute-start.15 = (bf16[160,1024]{1,0:T(8,128)(2,1)S(1)}, bf16[160,1024]{1,0:T(8,128)(2,1)S(1)}, u32[]{:S(2)}, u32[]{:S(2)}) collective-permute-start(bf16[160,1024]{1,0:T(8,128)(2,1)S(1)} %get-tuple-element.133), channel_id=1, source_target_pairs={{0,4},{1,5},{2,6},{3,7},{4,8},{5,9},{6,10},{7,11},{8,12},{9,13},{1... | collective-permute-start | bytes 983048 | tf_op jit(solution)/shard_map/ppermute | solution.py:491
  71.2 6.1 %copy-start.1 = (bf16[1,128,8192]{2,1,0:T(8,128)(2,1)S(1)}, bf16[1,128,8192]{2,1,0:T(8,128)(2,1)}, u32[]{:S(2)}) copy-start(bf16[1,128,8192]{2,1,0:T(8,128)(2,1)} %param.7) | copy-start | bytes 6291460
  71.3 6.1 %copy-start.4 = (s32[1,128]{1,0:T(1,128)S(1)}, s32[1,128]{1,0:T(1,128)}, u32[]{:S(2)}) copy-start(s32[1,128]{1,0:T(1,128)} %copy-done.2) | copy-start | bytes 1540
  71.4 6.0 %collective-permute-start.19 = (bf16[4,160,1024]{2,1,0:T(8,128)(2,1)S(1)}, bf16[4,160,1024]{2,1,0:T(8,128)(2,1)S(1)}, u32[]{:S(2)}, u32[]{:S(2)}) collective-permute-start(bf16[4,160,1024]{2,1,0:T(8,128)(2,1)S(1)} %pad_maximum_fusion.mine), channel_id=1, source_target_pairs={{0,16},{16,0},{32,48},{48,32},{64,80},{80,64},{96,112},{112,96},{1... | collective-permute-start | bytes 3932168 | tf_op jit(solution)/shard_map/ppermute | solution.py:499
  74.7 9.4 %collective-permute-start.21 = (bf16[160,1024]{1,0:T(8,128)(2,1)S(1)}, bf16[160,1024]{1,0:T(8,128)(2,1)S(1)}, u32[]{:S(2)}, u32[]{:S(2)}) collective-permute-start(bf16[160,1024]{1,0:T(8,128)(2,1)S(1)} %get-tuple-element.168), channel_id=1, source_target_pairs={{0,12},{1,13},{2,14},{3,15},{4,0},{5,1},{6,2},{7,3},{8,4},{9,5},{1... | collective-permute-start | bytes 983048 | tf_op jit(solution)/shard_map/ppermute | solution.py:491
  76.4 10.2 %collective-permute-start.22 = (bf16[160,1024]{1,0:T(8,128)(2,1)S(1)}, bf16[160,1024]{1,0:T(8,128)(2,1)S(1)}, u32[]{:S(2)}, u32[]{:S(2)}) collective-permute-start(bf16[160,1024]{1,0:T(8,128)(2,1)S(1)} %get-tuple-element.169), channel_id=1, source_target_pairs={{0,4},{1,5},{2,6},{3,7},{4,8},{5,9},{6,10},{7,11},{8,12},{9,13},{1... | collective-permute-start | bytes 983048 | tf_op jit(solution)/shard_map/ppermute | solution.py:491
  78.9 28.3 %collective-permute-start.20 = (bf16[128,8192]{1,0:T(8,128)(2,1)S(1)}, bf16[128,8192]{1,0:T(8,128)(2,1)S(1)}, u32[]{:S(2)}, u32[]{:S(2)}) collective-permute-start(bf16[128,8192]{1,0:T(8,128)(2,1)S(1)} %update.1), channel_id=1, source_target_pairs={{0,16},{16,32},{32,48},{48,64},{64,80},{80,96},{96,112},{1,17},{17... | collective-permute-start | bytes 6291464 | tf_op jit(solution)/shard_map/ppermute | solution.py:503
  82.9 11.3 %collective-permute-start.25 = (bf16[4,160,256]{2,1,0:T(8,128)(2,1)S(1)}, bf16[4,160,256]{2,1,0:T(8,128)(2,1)S(1)}, u32[]{:S(2)}, u32[]{:S(2)}) collective-permute-start(bf16[4,160,256]{2,1,0:T(8,128)(2,1)S(1)} %get-tuple-element.175), channel_id=1, source_target_pairs={{0,2},{1,3},{2,0},{3,1},{4,6},{5,7},{6,4},{7,5},{8,10},{9,11},{10,... | collective-permute-start | bytes 983048 | tf_op jit(solution)/shard_map/ppermute | solution.py:495
  84.1 14.0 %collective-permute-start.26 = (bf16[4,160,256]{2,1,0:T(8,128)(2,1)S(1)}, bf16[4,160,256]{2,1,0:T(8,128)(2,1)S(1)}, u32[]{:S(2)}, u32[]{:S(2)}) collective-permute-start(bf16[4,160,256]{2,1,0:T(8,128)(2,1)S(1)} %get-tuple-element.176), channel_id=1, source_target_pairs={{0,3},{1,0},{2,1},{3,2},{4,7},{5,4},{6,5},{7,6},{8,11},{9,8},{10,9... | collective-permute-start | bytes 983048 | tf_op jit(solution)/shard_map/ppermute | solution.py:495
  86.6 13.6 %collective-permute-start.24 = (bf16[4,160,256]{2,1,0:T(8,128)(2,1)S(1)}, bf16[4,160,256]{2,1,0:T(8,128)(2,1)S(1)}, u32[]{:S(2)}, u32[]{:S(2)}) collective-permute-start(bf16[4,160,256]{2,1,0:T(8,128)(2,1)S(1)} %get-tuple-element.174), channel_id=1, source_target_pairs={{0,1},{1,2},{2,3},{3,0},{4,5},{5,6},{6,7},{7,4},{8,9},{9,10},{10,1... | collective-permute-start | bytes 983048 | tf_op jit(solution)/shard_map/ppermute | solution.py:495
  86.6 13.7 %collective-permute-start.23 = (bf16[160,1024]{1,0:T(8,128)(2,1)S(1)}, bf16[160,1024]{1,0:T(8,128)(2,1)S(1)}, u32[]{:S(2)}, u32[]{:S(2)}) collective-permute-start(bf16[160,1024]{1,0:T(8,128)(2,1)S(1)} %get-tuple-element.172), channel_id=1, source_target_pairs={{0,8},{1,9},{2,10},{3,11},{4,12},{5,13},{6,14},{7,15},{8,0},{9,1},... | collective-permute-start | bytes 983048 | tf_op jit(solution)/shard_map/ppermute | solution.py:491
  100.5 4.2 %collective-permute-start.27 = (bf16[4,160,1024]{2,1,0:T(8,128)(2,1)S(1)}, bf16[4,160,1024]{2,1,0:T(8,128)(2,1)S(1)}, u32[]{:S(2)}, u32[]{:S(2)}) collective-permute-start(bf16[4,160,1024]{2,1,0:T(8,128)(2,1)S(1)} %pad_maximum_fusion.1.mine), channel_id=1, source_target_pairs={{0,16},{16,0},{32,48},{48,32},{64,80},{80,64},{96,112},{112,96},{1... | collective-permute-start | bytes 3932168 | tf_op jit(solution)/shard_map/ppermute | solution.py:499
  101.1 8.0 %collective-permute-start.28 = (bf16[160,256]{1,0:T(8,128)(2,1)S(1)}, bf16[160,256]{1,0:T(8,128)(2,1)S(1)}, u32[]{:S(2)}, u32[]{:S(2)}) collective-permute-start(bf16[160,256]{1,0:T(8,128)(2,1)S(1)} %get-tuple-element.181), channel_id=1, source_target_pairs={{0,4},{1,5},{2,6},{3,7},{4,8},{5,9},{6,10},{7,11},{8,12},{9,13},{1... | collective-permute-start | bytes 245768 | tf_op jit(solution)/shard_map/ppermute | solution.py:491
  101.8 7.3 %collective-permute-start.29 = (bf16[160,256]{1,0:T(8,128)(2,1)S(1)}, bf16[160,256]{1,0:T(8,128)(2,1)S(1)}, u32[]{:S(2)}, u32[]{:S(2)}) collective-permute-start(bf16[160,256]{1,0:T(8,128)(2,1)S(1)} %get-tuple-element.182), channel_id=1, source_target_pairs={{0,8},{1,9},{2,10},{3,11},{4,12},{5,13},{6,14},{7,15},{8,0},{9,1},... | collective-permute-start | bytes 245768 | tf_op jit(solution)/shard_map/ppermute | solution.py:491
  104.1 5.0 %collective-permute-start.30 = (bf16[160,256]{1,0:T(8,128)(2,1)S(1)}, bf16[160,256]{1,0:T(8,128)(2,1)S(1)}, u32[]{:S(2)}, u32[]{:S(2)}) collective-permute-start(bf16[160,256]{1,0:T(8,128)(2,1)S(1)} %get-tuple-element.183), channel_id=1, source_target_pairs={{0,12},{1,13},{2,14},{3,15},{4,0},{5,1},{6,2},{7,3},{8,4},{9,5},{1... | collective-permute-start | bytes 245768 | tf_op jit(solution)/shard_map/ppermute | solution.py:491
  109.2 2.8 %collective-permute-start.31 = (bf16[4,160,256]{2,1,0:T(8,128)(2,1)S(1)}, bf16[4,160,256]{2,1,0:T(8,128)(2,1)S(1)}, u32[]{:S(2)}, u32[]{:S(2)}) collective-permute-start(bf16[4,160,256]{2,1,0:T(8,128)(2,1)S(1)} %pad_maximum_fusion.4.sums), channel_id=1, source_target_pairs={{0,16},{16,0},{32,48},{48,32},{64,80},{80,64},{96,112},{112,96},{1... | collective-permute-start | bytes 983048 | tf_op jit(solution)/shard_map/ppermute | solution.py:499

commit v5 on v4

--- a/solution.py
+++ b/solution.py
@@ -128,6 +128,10 @@
     return (lax.broadcasted_iota(jnp.int32, (ROWS, ROWS), 0) == sel[0:1, :]).astype(F32)
 
 
+def held_slots(sel, count):
+    return jnp.where(lax.broadcasted_iota(jnp.int32, (1, ROWS), 1) < count[...], sel[...], -1)
+
+
 def compact(sel):
     return chooser(sel).T[:SLOTS, :].astype(BF)
 
@@ -152,39 +156,44 @@
     return 2 * lax.rem(z + shift, 4) + core, core
 
 
-def pack_kv_kernel(own, come, sel, sel_in, *outs):
+def pack_kv_kernel(own, k_in, v_in, sel, sel_in, count, count_in, *outs):
+    def mine(side, head):
+        return own[:, pl.ds(pl.multiple_of(head * HEAD + side * HALF, HEAD), HEAD)]
+
+    def theirs(side, head):
+        return (k_in, v_in)[side][:, pl.ds(pl.multiple_of(head * HEAD, HEAD), HEAD)]
+
     def fill(dense, few, few_sel):
         pick = compact(few_sel)
         mark = INVALID * (1.0 - jnp.sum(pick.astype(F32), axis=1, keepdims=True))
         for step, out in enumerate(outs):
             for side in range(2):
-                here = pl.ds(pl.multiple_of(own_head(step)[0] * HEAD + side * HALF, HEAD), HEAD)
                 cols = slice(side * HEAD, (side + 1) * HEAD)
-                out[:ROWS, cols] = dense[:, here]
-                rows = dot(pick, few[:, here])
+                out[:ROWS, cols] = dense(side, own_head(step)[0])
+                rows = dot(pick, few(side, own_head(step)[0]))
                 out[ROWS:, cols] = (rows if side else rows + mark).astype(BF)
 
     @pl.when(own_head(0)[1] == 1)
     def _():
-        fill(own, come, sel_in)
+        fill(mine, theirs, held_slots(sel_in, count_in))
 
     @pl.when(own_head(0)[1] == 0)
     def _():
-        fill(come, own, sel)
-
-
-def pack_kv(own, come, sel, sel_in):
+        fill(theirs, mine, held_slots(sel, count))
+
+
+def pack_kv(own, k_in, v_in, *slots):
     return list(pl.pallas_call(
         pack_kv_kernel,
         out_shape=[jax.ShapeDtypeStruct((SENT, KV), BF)] * 4,
-        in_specs=[VMEM] * 4,
+        in_specs=[VMEM] * 7,
         out_specs=[VMEM] * 4,
         compiler_params=PARAMS,
         name="pack_kv",
-    )(own, come, sel, sel_in))
-
-
-def pack_kernel(own, come, sel, sel_in, o0, o1, o2, o3, held, sems):
+    )(own, k_in, v_in, *slots))
+
+
+def pack_kernel(own, come, sel, sel_in, count, count_in, o0, o1, o2, o3, held, sems):
     core = own_head(0)[1]
     outs, copies = (o0, o1, o2, o3), []
     for step in range(4):
@@ -192,7 +201,7 @@
         for i, ref in enumerate((own, come)):
             copies.append(pltpu.make_async_copy(ref.at[:, here], held.at[step, i], sems.at[2 * step + i]))
             copies[-1].start()
-    pick = compact(jnp.where(core == 1, sel_in[...], sel[...]))
+    pick = compact(jnp.where(core == 1, held_slots(sel_in, count_in), held_slots(sel, count)))
     for step, out in enumerate(outs):
         copies[2 * step].wait()
         copies[2 * step + 1].wait()
@@ -208,16 +217,16 @@
             out[ROWS:, :] = dot(pick, held[step, 0]).astype(BF)
 
 
-def pack(own, come, sel, sel_in, params):
+def pack(own, come, slots, params):
     return list(pl.pallas_call(
         pack_kernel,
         out_shape=[jax.ShapeDtypeStruct((SENT, HALF), BF)] * 4,
-        in_specs=[ANY] * 2 + [VMEM] * 2,
+        in_specs=[ANY] * 2 + [VMEM] * 4,
         out_specs=[VMEM] * 4,
         scratch_shapes=[pltpu.VMEM((4, 2, ROWS, HALF), BF), pltpu.SemaphoreType.DMA((8,))],
         compiler_params=params,
         name="pack",
-    )(own, come, sel, sel_in))
+    )(own, come, *slots))
 
 
 FORTH = pltpu.CompilerParams(vmem_limit_bytes=12 << 20)
@@ -514,11 +523,12 @@
     sel = jnp.where(jnp.arange(ROWS, dtype=jnp.int32)[None, :] < counts, selected, -1)
 
     own = jnp.concatenate([k, v], 1)
-    come, sel_in = swap(own), swap(sel)
-    kv = pack_kv(own, come, sel, sel_in)
-    q, g, *_ = both(q, g, come, sel_in)
+    k_in, v_in = swap(k), swap(v)
+    slots = selected, swap(selected), counts, swap(counts)
+    kv = pack_kv(own, k_in, v_in, *slots)
+    q, g, *_ = both(q, g, k_in, v_in, slots[1], slots[3])
     q_in, g_in = swap(q), swap(g)
-    qs = pack(q, q_in, sel, sel_in, WHOLE)
+    qs = pack(q, q_in, slots, WHOLE)
     for by in (1, 3, 2):
         kv[by] = along_z(kv[by], by)
     kv[1], kv[2], kv[3], qs[1], qs[2], qs[3], g_in = both(kv[1], kv[2], kv[3], qs[1], qs[2], qs[3], g_in)
@@ -527,7 +537,7 @@
     qs[1], qs[2], qs[3], g_in, _ = both(qs[1], qs[2], qs[3], g_in, column)
     for by in (1, 3, 2):
         qs[by] = along_z(qs[by], by)
-    gs = pack(g, g_in, sel, sel_in, PARAMS)
+    gs = pack(g, g_in, slots, PARAMS)
 
     qs[0], qs[1], qs[3] = both(qs[0], qs[1], qs[3])
     (own,), keyed = forward((0,), info, [qs[0]], kvs=kvs)

time: 114 us -> 115 us (level)
  Pallas kernels: 44.1 us -> 45.9 us
    ppermute x7 -> x9, starting transfers between devices: 7.46 us -> 8.22 us  [swap(): return lax.ppermute(x, 'section', [(i, i ^ 1) for i in range(8)])]
    ppermute x7 -> x9, waiting for transfers between devices: 3.31 us -> 3.59 us  [swap(): return lax.ppermute(x, 'section', [(i, i ^ 1) for i in range(8)])]
  transfers between devices with their start and end apart: 32 -> 34, of which waited for: 9 -> 11; matrix products, arithmetic and copies ran while one was open for 1% -> 1% of each run, Pallas kernels for 38% -> 39%
where the time goes in v5:
time: 115 us
  Pallas kernels  45.9 us (40%)
  starting transfers between devices  40.9 us (36%)
  waiting for transfers between devices  23.9 us (21%)
  other arithmetic  1.57 us (1%)
  between operations  1.52 us (1%)
  local copies, waits for them, and re-layouts  1.28 us (1%)
    ppermute x18, starting transfers between devices, along_z(): lax.ppermute(x, 'ctx', [(4 * z + y, 4 * ((z + by) % 4) + y) for z in rang...  21.8 us
    ppermute x6, waiting for transfers between devices, along_y(): lax.ppermute(x, 'ctx', [(4 * z + y, 4 * z + (y + by) % 4) for z in range(...  18.3 us
    pallas_call x2, Pallas kernels, forward(): pl.pallas_call(functools.partial(forward_kernel, shifts, first), out_shap...  15.6 us
    pallas_call x1, Pallas kernels, backward(): pl.pallas_call(functools.partial(backward_kernel, shifts), out_shape=shap...  15.2 us
    ppermute x9, starting transfers between devices, swap(): return lax.ppermute(x, 'section', [(i, i ^ 1) for i in range(8)])  8.22 us
    ppermute x6, starting transfers between devices, along_y(): lax.ppermute(x, 'ctx', [(4 * z + y, 4 * z + (y + by) % 4) for z in range(...  6.9 us
    pallas_call x2, Pallas kernels, pack(): pl.pallas_call(pack_kernel, out_shape=[jax.ShapeDtypeStruct((SENT, HALF),...  6.73 us
    ppermute x1, starting transfers between devices, onward(): return lax.ppermute(x, 'section', [(i, i + 1) for i in range(7)])  3.97 us
  transfers between devices with their start and end apart: 34, of which 11 were waited for; matrix products, arithmetic and copies ran while one was open for 1% of the time, Pallas kernels for 39%

profile of v5, /device:TPU:1, one launch (start us, length us, event | category | flops | bytes accessed | tf_op | source)
XLA Modules:
  0.0 115.1 jit_solution(3513732589878511411)
XLA Ops:
  0.6 1.5 %collective-permute-start = (bf16[128,1024]{1,0:T(8,128)(2,1)}, bf16[128,1024]{1,0:T(8,128)(2,1)S(1)}, u32[]{:S(2)}, u32[]{:S(2)}) collective-permute-start(bf16[128,1024]{1,0:T(8,128)(2,1)} %bitcast.49), channel_id=1, source_target_pairs={{0,16},{16,0},{32,48},{48,32},{64,80},{80,64},{96,112},{112,96},{1... | collective-permute-start | bytes 786440 | tf_op jit(solution)/shard_map/ppermute | solution.py:508
  2.1 0.1 collective-permute-start.1
  2.2 0.4 collective-permute-start.2
  2.6 0.1 collective-permute-start.3
  2.7 1.3 %collective-permute-done.3.count_in = s32[1,1]{1,0:T(1,128)} collective-permute-done((s32[1,1]{1,0:T(1,128)}, s32[1,1]{1,0:T(1,128)}, u32[]{:S(2)}, u32[]{:S(2)}) %collective-permute-start.3) | collective-permute-done | bytes 36 | tf_op jit(solution)/shard_map/ppermute | solution.py:508
  4.0 0.0 collective-permute-done.2.sel_in
  4.0 0.0 collective-permute-done.k_in
  4.1 0.3 collective-permute-start.4
  4.4 0.3 collective-permute-start.8
  5.3 1.1 pad_maximum_fusion.2.own
  6.4 0.0 copy-start.2
  6.4 0.6 copy-done.2
  7.0 0.9 pack_kv.1
  7.9 1.8 %collective-permute-start.5 = (bf16[160,256]{1,0:T(8,128)(2,1)S(1)}, bf16[160,256]{1,0:T(8,128)(2,1)S(1)}, u32[]{:S(2)}, u32[]{:S(2)}) collective-permute-start(bf16[160,256]{1,0:T(8,128)(2,1)S(1)} %get-tuple-element.100), channel_id=1, source_target_pairs={{0,4},{1,5},{2,6},{3,7},{4,8},{5,9},{6,10},{7,11},{8,12},{9,13},{1... | collective-permute-start | bytes 245768 | tf_op jit(solution)/shard_map/ppermute | solution.py:500
  9.7 3.3 %collective-permute-start.6 = (bf16[160,256]{1,0:T(8,128)(2,1)S(1)}, bf16[160,256]{1,0:T(8,128)(2,1)S(1)}, u32[]{:S(2)}, u32[]{:S(2)}) collective-permute-start(bf16[160,256]{1,0:T(8,128)(2,1)S(1)} %get-tuple-element.101), channel_id=1, source_target_pairs={{0,8},{1,9},{2,10},{3,11},{4,12},{5,13},{6,14},{7,15},{8,0},{9,1},... | collective-permute-start | bytes 245768 | tf_op jit(solution)/shard_map/ppermute | solution.py:500
  13.0 0.7 collective-permute-start.7
  13.7 0.0 collective-permute-done.4.come
  13.8 4.3 %pack.2 = (bf16[160,1024]{1,0:T(8,128)(2,1)}, bf16[160,1024]{1,0:T(8,128)(2,1)}, bf16[160,1024]{1,0:T(8,128)(2,1)}, bf16[160,1024]{1,0:T(8,128)(2,1)}) custom-call(bf16[128,8192]{1,0:T(8,128)(2,1)} %bitcast.40, bf16[128,8192]{1,0:T(8,128)(2,1)} %collective-permute-done.4.come, s32[1,128]{1,0:T(1,128)} %sel.5, s32[1,128]{1,0:T(1,128)} %copy-done.4, ...), custom_call_target="tpu_custom_call" | custom-call | tf_op jit(solution)/shard_map/pack/pallas_call | solution.py:221
  18.1 0.8 collective-permute-start.9
  19.0 1.9 %collective-permute-start.10 = (bf16[160,1024]{1,0:T(8,128)(2,1)}, bf16[160,1024]{1,0:T(8,128)(2,1)S(1)}, u32[]{:S(2)}, u32[]{:S(2)}) collective-permute-start(bf16[160,1024]{1,0:T(8,128)(2,1)} %get-tuple-element.116), channel_id=1, source_target_pairs={{0,12},{1,13},{2,14},{3,15},{4,0},{5,1},{6,2},{7,3},{8,4},{9,5},{1... | collective-permute-start | bytes 983048 | tf_op jit(solution)/shard_map/ppermute | solution.py:500
  20.9 1.3 %collective-permute-start.11 = (bf16[4,160,256]{2,1,0:T(8,128)(2,1)S(1)}, bf16[4,160,256]{2,1,0:T(8,128)(2,1)S(1)}, u32[]{:S(2)}, u32[]{:S(2)}) collective-permute-start(bf16[4,160,256]{2,1,0:T(8,128)(2,1)S(1)} %pad_maximum_fusion.3.refs_1_), channel_id=1, source_target_pairs={{0,1},{1,2},{2,3},{3,0},{4,5},{5,6},{6,7},{7,4},{8,9},{9,10},{10,1... | collective-permute-start | bytes 983048 | tf_op jit(solution)/shard_map/ppermute | solution.py:504
  22.2 2.6 %collective-permute-start.12 = (bf16[4,160,256]{2,1,0:T(8,128)(2,1)S(1)}, bf16[4,160,256]{2,1,0:T(8,128)(2,1)}, u32[]{:S(2)}, u32[]{:S(2)}) collective-permute-start(bf16[4,160,256]{2,1,0:T(8,128)(2,1)S(1)} %pad_maximum_fusion.3.refs_1_), channel_id=1, source_target_pairs={{0,2},{1,3},{2,0},{3,1},{4,6},{5,7},{6,4},{7,5},{8,10},{9,11},{10,... | collective-permute-start | bytes 983048 | tf_op jit(solution)/shard_map/ppermute | solution.py:504
  24.8 1.1 collective-permute-start.13
  25.9 0.1 pad_add_fusion.info
  26.0 0.6 copy-done.5
  26.6 2.4 %pack.3 = (bf16[160,1024]{1,0:T(8,128)(2,1)S(1)}, bf16[160,1024]{1,0:T(8,128)(2,1)S(1)}, bf16[160,1024]{1,0:T(8,128)(2,1)S(1)}, bf16[160,1024]{1,0:T(8,128)(2,1)S(1)}) custom-call(bf16[128,8192]{1,0:T(8,128)(2,1)S(1)} %bitcast.32, bf16[128,8192]{1,0:T(8,128)(2,1)} %collective-permute-done.8.come, s32[1,128]{1,0:T(1,128)S(1)} %copy-done.3, ...), custom_call_target="tpu_custom_call" | custom-call | tf_op jit(solution)/shard_map/pack/pallas_call | solution.py:221
  29.0 0.1 collective-permute-start.14
  29.1 0.6 collective-permute-start.18
  29.7 0.1 collective-permute-done.11.refs_2_
  29.8 2.1 %collective-permute-start.19 = (bf16[160,1024]{1,0:T(8,128)(2,1)S(1)}, bf16[160,1024]{1,0:T(8,128)(2,1)S(1)}, u32[]{:S(2)}, u32[]{:S(2)}) collective-permute-start(bf16[160,1024]{1,0:T(8,128)(2,1)S(1)} %get-tuple-element.136), channel_id=1, source_target_pairs={{0,12},{1,13},{2,14},{3,15},{4,0},{5,1},{6,2},{7,3},{8,4},{9,5},{1... | collective-permute-start | bytes 983048 | tf_op jit(solution)/shard_map/ppermute | solution.py:500
  31.9 6.1 %collective-permute-done.12.refs_3_ = bf16[4,160,256]{2,1,0:T(8,128)(2,1)} collective-permute-done((bf16[4,160,256]{2,1,0:T(8,128)(2,1)S(1)}, bf16[4,160,256]{2,1,0:T(8,128)(2,1)}, u32[]{:S(2)}, u32[]{:S(2)}) %collective-permute-start.12) | collective-permute-done | bytes 327712 | tf_op jit(solution)/shard_map/ppermute | solution.py:504
  38.0 0.2 collective-permute-start.20
  38.2 0.2 collective-permute-done.13.refs_4_
  38.4 3.4 %forward.2 = (bf16[160,1024]{1,0:T(8,128)(2,1)S(1)}, bf16[2048,1024]{1,0:T(8,128)(2,1)S(1)}, f32[8,1024]{1,0:T(8,128)S(1)}, f32[128,1024]{1,0:T(8,128)S(1)}, bf1...) custom-call(s32[3]{0:T(128)S(1)} %pad_add_fusion.info, ...), custom_call_target="tpu_custom_call" | custom-call | flops 4000000000 | bytes 4194304 | tf_op jit(solution)/shard_map/forward/pallas_call | solution.py:328
  41.8 12.1 %forward.3 = (bf16[160,1024]{1,0:T(8,128)(2,1)S(1)}, bf16[2048,1024]{1,0:T(8,128)(2,1)S(1)}, f32[8,1024]{1,0:T(8,128)S(1)}, f32[128,1024]{1,0:T(8,128)S(1)}, bf1...) custom-call(s32[3]{0:T(128)S(1)} %pad_add_fusion.info, ...), custom_call_target="tpu_custom_call" | custom-call | flops 12000000000 | bytes 4194304 | tf_op jit(solution)/shard_map/forward/pallas_call | solution.py:328
  54.0 1.7 %collective-permute-start.15 = (bf16[160,1024]{1,0:T(8,128)(2,1)S(1)}, bf16[160,1024]{1,0:T(8,128)(2,1)S(1)}, u32[]{:S(2)}, u32[]{:S(2)}) collective-permute-start(bf16[160,1024]{1,0:T(8,128)(2,1)S(1)} %get-tuple-element.131), channel_id=1, source_target_pairs={{0,12},{1,13},{2,14},{3,15},{4,0},{5,1},{6,2},{7,3},{8,4},{9,5},{1... | collective-permute-start | bytes 983048 | tf_op jit(solution)/shard_map/ppermute | solution.py:500
  55.6 1.2 %collective-permute-start.16 = (bf16[160,1024]{1,0:T(8,128)(2,1)S(1)}, bf16[160,1024]{1,0:T(8,128)(2,1)S(1)}, u32[]{:S(2)}, u32[]{:S(2)}) collective-permute-start(bf16[160,1024]{1,0:T(8,128)(2,1)S(1)} %get-tuple-element.132), channel_id=1, source_target_pairs={{0,8},{1,9},{2,10},{3,11},{4,12},{5,13},{6,14},{7,15},{8,0},{9,1},... | collective-permute-start | bytes 983048 | tf_op jit(solution)/shard_map/ppermute | solution.py:500
  56.8 0.8 collective-permute-start.17
  57.5 15.2 %backward.1 = (bf16[160,1024]{1,0:T(8,128)(2,1)S(1)}, bf16[160,1024]{1,0:T(8,128)(2,1)S(1)}, bf16[160,1024]{1,0:T(8,128)(2,1)S(1)}, bf16[160,1024]{1,0:T(8,128)(...) custom-call(s32[3]{0:T(128)S(1)} %pad_add_fusion.info, ...), custom_call_target="tpu_custom_call" | custom-call | flops 24000000000 | bytes 4194304 | tf_op jit(solution)/shard_map/backward/pallas_call | solution.py:375
  72.8 0.5 collective-permute-done.17
  73.3 0.2 pad_maximum_fusion.mine
  73.4 3.3 %collective-permute-start.21 = (bf16[4,160,1024]{2,1,0:T(8,128)(2,1)S(1)}, bf16[4,160,1024]{2,1,0:T(8,128)(2,1)S(1)}, u32[]{:S(2)}, u32[]{:S(2)}) collective-permute-start(bf16[4,160,1024]{2,1,0:T(8,128)(2,1)S(1)} %pad_maximum_fusion.mine), channel_id=1, source_target_pairs={{0,16},{16,0},{32,48},{48,32},{64,80},{80,64},{96,112},{112,96},{1... | collective-permute-start | bytes 3932168 | tf_op jit(solution)/shard_map/ppermute | solution.py:508
  76.7 1.6 %collective-permute-start.23 = (bf16[160,1024]{1,0:T(8,128)(2,1)S(1)}, bf16[160,1024]{1,0:T(8,128)(2,1)S(1)}, u32[]{:S(2)}, u32[]{:S(2)}) collective-permute-start(bf16[160,1024]{1,0:T(8,128)(2,1)S(1)} %get-tuple-element.168), channel_id=1, source_target_pairs={{0,12},{1,13},{2,14},{3,15},{4,0},{5,1},{6,2},{7,3},{8,4},{9,5},{1... | collective-permute-start | bytes 983048 | tf_op jit(solution)/shard_map/ppermute | solution.py:500
  78.4 1.0 collective-permute-done.21.theirs
  79.4 1.5 %update.1 = bf16[128,8192]{1,0:T(8,128)(2,1)S(1)} custom-call(s32[3]{0:T(128)S(1)} %pad_add_fusion.info, bf16[128,8192]{1,0:T(8,128)(2,1)S(1)} %bitcast.30, bf16[4,160,1024]{2,1,0:T(8,128)(2,1)S(1)} %pad_maximum_fusion.mine, bf16[4,160,1024]{2,1,0:T(8,128)(2,1)S(1)} %collective-permute-done.21.theirs, s32[1,128]{1,0:T(1,128)S(1)} %compare_select_fusion.sel), custom_call_target="tpu_custom_call" | custom-call | tf_op jit(solution)/shard_map/update/pallas_call | solution.py:437
  80.9 4.0 %collective-permute-start.22 = (bf16[128,8192]{1,0:T(8,128)(2,1)S(1)}, bf16[128,8192]{1,0:T(8,128)(2,1)S(1)}, u32[]{:S(2)}, u32[]{:S(2)}) collective-permute-start(bf16[128,8192]{1,0:T(8,128)(2,1)S(1)} %update.1), channel_id=1, source_target_pairs={{0,16},{16,32},{32,48},{48,64},{64,80},{80,96},{96,112},{1,17},{17... | collective-permute-start | bytes 6291464 | tf_op jit(solution)/shard_map/ppermute | solution.py:512
  84.9 1.9 %collective-permute-start.27 = (bf16[4,160,256]{2,1,0:T(8,128)(2,1)S(1)}, bf16[4,160,256]{2,1,0:T(8,128)(2,1)S(1)}, u32[]{:S(2)}, u32[]{:S(2)}) collective-permute-start(bf16[4,160,256]{2,1,0:T(8,128)(2,1)S(1)} %get-tuple-element.175), channel_id=1, source_target_pairs={{0,2},{1,3},{2,0},{3,1},{4,6},{5,7},{6,4},{7,5},{8,10},{9,11},{10,... | collective-permute-start | bytes 983048 | tf_op jit(solution)/shard_map/ppermute | solution.py:504
  86.8 1.5 %collective-permute-done.24 = bf16[160,1024]{1,0:T(8,128)(2,1)S(1)} collective-permute-done((bf16[160,1024]{1,0:T(8,128)(2,1)S(1)}, bf16[160,1024]{1,0:T(8,128)(2,1)S(1)}, u32[]{:S(2)}, u32[]{:S(2)}) %collective-permute-start.24) | collective-permute-done | bytes 327712 | tf_op jit(solution)/shard_map/ppermute | solution.py:500
  88.3 0.0 collective-permute-start.26
  88.3 2.0 %collective-permute-start.25 = (bf16[160,1024]{1,0:T(8,128)(2,1)S(1)}, bf16[160,1024]{1,0:T(8,128)(2,1)S(1)}, u32[]{:S(2)}, u32[]{:S(2)}) collective-permute-start(bf16[160,1024]{1,0:T(8,128)(2,1)S(1)} %get-tuple-element.172), channel_id=1, source_target_pairs={{0,8},{1,9},{2,10},{3,11},{4,12},{5,13},{6,14},{7,15},{8,0},{9,1},... | collective-permute-start | bytes 983048 | tf_op jit(solution)/shard_map/ppermute | solution.py:500
  90.2 5.3 %collective-permute-done.27.c = bf16[4,160,256]{2,1,0:T(8,128)(2,1)S(1)} collective-permute-done((bf16[4,160,256]{2,1,0:T(8,128)(2,1)S(1)}, bf16[4,160,256]{2,1,0:T(8,128)(2,1)S(1)}, u32[]{:S(2)}, u32[]{:S(2)}) %collective-permute-start.27) | collective-permute-done | bytes 327712 | tf_op jit(solution)/shard_map/ppermute | solution.py:504
  95.5 5.9 %collective-permute-done.28.d = bf16[4,160,256]{2,1,0:T(8,128)(2,1)S(1)} collective-permute-done((bf16[4,160,256]{2,1,0:T(8,128)(2,1)S(1)}, bf16[4,160,256]{2,1,0:T(8,128)(2,1)S(1)}, u32[]{:S(2)}, u32[]{:S(2)}) %collective-permute-start.28) | collective-permute-done | bytes 327712 | tf_op jit(solution)/shard_map/ppermute | solution.py:504
  101.4 0.8 collective-permute-done.26.b
  102.2 0.2 fold_sums.1
  102.4 0.2 pad_maximum_fusion.1.mine
  102.5 0.6 collective-permute-start.29
  103.1 0.8 collective-permute-start.30
  103.9 2.4 %collective-permute-start.31 = (bf16[160,256]{1,0:T(8,128)(2,1)S(1)}, bf16[160,256]{1,0:T(8,128)(2,1)S(1)}, u32[]{:S(2)}, u32[]{:S(2)}) collective-permute-start(bf16[160,256]{1,0:T(8,128)(2,1)S(1)} %get-tuple-element.182), channel_id=1, source_target_pairs={{0,8},{1,9},{2,10},{3,11},{4,12},{5,13},{6,14},{7,15},{8,0},{9,1},... | collective-permute-start | bytes 245768 | tf_op jit(solution)/shard_map/ppermute | solution.py:500
  106.3 0.0 collective-permute-start.32
  106.3 2.4 %finish_q.1 = bf16[128,8192]{1,0:T(8,128)(2,1)} custom-call(s32[3]{0:T(128)S(1)} %pad_add_fusion.info, bf16[4,160,1024]{2,1,0:T(8,128)(2,1)S(1)} %pad_maximum_fusion.1.mine, bf16[4,160,1024]{2,1,0:T(8,128)(2,1)S(1)} %collective-permute-done.29.theirs, s32[1,128]{1,0:T(1,128)S(1)} %compare_select_fusion.sel), custom_call_target="tpu_custom_call" | custom-call | tf_op jit(solution)/shard_map/finish_q/pallas_call | solution.py:437
  108.7 1.9 %settle.1 = bf16[128,8192]{1,0:T(8,128)(2,1)} custom-call(bf16[128,8192]{1,0:T(8,128)(2,1)S(1)} %collective-permute-done.22.x), custom_call_target="tpu_custom_call" | custom-call | tf_op jit(solution)/shard_map/settle/pallas_call | solution.py:457
  110.7 1.6 %collective-permute-start.33 = (bf16[4,160,256]{2,1,0:T(8,128)(2,1)S(1)}, bf16[4,160,256]{2,1,0:T(8,128)(2,1)S(1)}, u32[]{:S(2)}, u32[]{:S(2)}) collective-permute-start(bf16[4,160,256]{2,1,0:T(8,128)(2,1)S(1)} %pad_maximum_fusion.4.sums), channel_id=1, source_target_pairs={{0,16},{16,0},{32,48},{48,32},{64,80},{80,64},{96,112},{112,96},{1... | collective-permute-start | bytes 983048 | tf_op jit(solution)/shard_map/ppermute | solution.py:508
  112.4 1.3 %collective-permute-done.33.sums_in = bf16[4,160,256]{2,1,0:T(8,128)(2,1)S(1)} collective-permute-done((bf16[4,160,256]{2,1,0:T(8,128)(2,1)S(1)}, bf16[4,160,256]{2,1,0:T(8,128)(2,1)S(1)}, u32[]{:S(2)}, u32[]{:S(2)}) %collective-permute-start.33) | collective-permute-done | bytes 327712 | tf_op jit(solution)/shard_map/ppermute | solution.py:508
  113.7 1.4 %finish_kv.1 = (bf16[128,1024]{1,0:T(8,128)(2,1)}, bf16[128,1024]{1,0:T(8,128)(2,1)}) custom-call(s32[3]{0:T(128)S(1)} %pad_add_fusion.info, bf16[4,160,256]{2,1,0:T(8,128)(2,1)S(1)} %pad_maximum_fusion.4.sums, bf16[4,160,256]{2,1,0:T(8,128)(2,1)S(1)} %collective-permute-done.33.sums_in, s32[1,128]{1,0:T(1,128)S(1)} %compare_select_fusion.sel), custom_call_target="tpu_custom_call" | custom-call | tf_op jit(solution)/shard_map/finish_kv/pallas_call | solution.py:489
  (38 shorter events, 0.2 us)
Async XLA Ops:
  0.6 3.4 %collective-permute-start = (bf16[128,1024]{1,0:T(8,128)(2,1)}, bf16[128,1024]{1,0:T(8,128)(2,1)S(1)}, u32[]{:S(2)}, u32[]{:S(2)}) collective-permute-start(bf16[128,1024]{1,0:T(8,128)(2,1)} %bitcast.49), channel_id=1, source_target_pairs={{0,16},{16,0},{32,48},{48,32},{64,80},{80,64},{96,112},{112,96},{1... | collective-permute-start | bytes 786440 | tf_op jit(solution)/shard_map/ppermute | solution.py:508
  2.1 1.9 %collective-permute-start.1 = (bf16[128,1024]{1,0:T(8,128)(2,1)}, bf16[128,1024]{1,0:T(8,128)(2,1)S(1)}, u32[]{:S(2)}, u32[]{:S(2)}) collective-permute-start(bf16[128,1024]{1,0:T(8,128)(2,1)} %bitcast.47), channel_id=1, source_target_pairs={{0,16},{16,0},{32,48},{48,32},{64,80},{80,64},{96,112},{112,96},{1... | collective-permute-start | bytes 786440 | tf_op jit(solution)/shard_map/ppermute | solution.py:508
  2.2 1.8 %collective-permute-start.2 = (s32[1,128]{1,0:T(1,128)}, s32[1,128]{1,0:T(1,128)S(1)}, u32[]{:S(2)}, u32[]{:S(2)}) collective-permute-start(s32[1,128]{1,0:T(1,128)} %sel.5), channel_id=1, source_target_pairs={{0,16},{16,0},{32,48},{48,32},{64,80},{80,64},{96,112},{112,96},{1... | collective-permute-start | bytes 1544 | tf_op jit(solution)/shard_map/ppermute | solution.py:508
  2.6 1.4 %collective-permute-start.3 = (s32[1,1]{1,0:T(1,128)}, s32[1,1]{1,0:T(1,128)}, u32[]{:S(2)}, u32[]{:S(2)}) collective-permute-start(s32[1,1]{1,0:T(1,128)} %param.13), channel_id=1, source_target_pairs={{0,16},{16,0},{32,48},{48,32},{64,80},{80,64},{96,112},{112,96},{1... | collective-permute-start | bytes 20 | tf_op jit(solution)/shard_map/ppermute | solution.py:508
  4.0 9.7 %copy-start.4 = (s32[1,128]{1,0:T(1,128)}, s32[1,128]{1,0:T(1,128)S(1)}, u32[]{:S(2)}) copy-start(s32[1,128]{1,0:T(1,128)S(1)} %collective-permute-done.2.sel_in) | copy-start | bytes 1540
  4.1 9.7 %collective-permute-start.4 = (bf16[128,8192]{1,0:T(8,128)(2,1)}, bf16[128,8192]{1,0:T(8,128)(2,1)}, u32[]{:S(2)}, u32[]{:S(2)}) collective-permute-start(bf16[128,8192]{1,0:T(8,128)(2,1)} %bitcast.39), channel_id=1, source_target_pairs={{0,16},{16,0},{32,48},{48,32},{64,80},{80,64},{96,112},{112,96},{1... | collective-permute-start | bytes 6291464 | tf_op jit(solution)/shard_map/ppermute | solution.py:508
  4.4 13.7 %collective-permute-start.8 = (bf16[128,8192]{1,0:T(8,128)(2,1)}, bf16[128,8192]{1,0:T(8,128)(2,1)}, u32[]{:S(2)}, u32[]{:S(2)}) collective-permute-start(bf16[128,8192]{1,0:T(8,128)(2,1)} %bitcast.31), channel_id=1, source_target_pairs={{0,16},{16,0},{32,48},{48,32},{64,80},{80,64},{96,112},{112,96},{1... | collective-permute-start | bytes 6291464 | tf_op jit(solution)/shard_map/ppermute | solution.py:508
  6.4 0.7 copy-start.2
  7.9 10.1 %collective-permute-start.5 = (bf16[160,256]{1,0:T(8,128)(2,1)S(1)}, bf16[160,256]{1,0:T(8,128)(2,1)S(1)}, u32[]{:S(2)}, u32[]{:S(2)}) collective-permute-start(bf16[160,256]{1,0:T(8,128)(2,1)S(1)} %get-tuple-element.100), channel_id=1, source_target_pairs={{0,4},{1,5},{2,6},{3,7},{4,8},{5,9},{6,10},{7,11},{8,12},{9,13},{1... | collective-permute-start | bytes 245768 | tf_op jit(solution)/shard_map/ppermute | solution.py:500
  9.7 8.4 %collective-permute-start.6 = (bf16[160,256]{1,0:T(8,128)(2,1)S(1)}, bf16[160,256]{1,0:T(8,128)(2,1)S(1)}, u32[]{:S(2)}, u32[]{:S(2)}) collective-permute-start(bf16[160,256]{1,0:T(8,128)(2,1)S(1)} %get-tuple-element.101), channel_id=1, source_target_pairs={{0,8},{1,9},{2,10},{3,11},{4,12},{5,13},{6,14},{7,15},{8,0},{9,1},... | collective-permute-start | bytes 245768 | tf_op jit(solution)/shard_map/ppermute | solution.py:500
  13.0 12.9 %copy-start.3 = (s32[1,128]{1,0:T(1,128)S(1)}, s32[1,128]{1,0:T(1,128)}, u32[]{:S(2)}) copy-start(s32[1,128]{1,0:T(1,128)} %sel.5) | copy-start | bytes 1540
  13.0 5.1 %collective-permute-start.7 = (bf16[160,256]{1,0:T(8,128)(2,1)S(1)}, bf16[160,256]{1,0:T(8,128)(2,1)S(1)}, u32[]{:S(2)}, u32[]{:S(2)}) collective-permute-start(bf16[160,256]{1,0:T(8,128)(2,1)S(1)} %get-tuple-element.102), channel_id=1, source_target_pairs={{0,12},{1,13},{2,14},{3,15},{4,0},{5,1},{6,2},{7,3},{8,4},{9,5},{1... | collective-permute-start | bytes 245768 | tf_op jit(solution)/shard_map/ppermute | solution.py:500
  13.7 12.2 %copy-start.1 = (bf16[1,128,8192]{2,1,0:T(8,128)(2,1)S(1)}, bf16[1,128,8192]{2,1,0:T(8,128)(2,1)}, u32[]{:S(2)}) copy-start(bf16[1,128,8192]{2,1,0:T(8,128)(2,1)} %param.11) | copy-start | bytes 6291460
  18.1 10.9 %collective-permute-start.9 = (bf16[160,1024]{1,0:T(8,128)(2,1)}, bf16[160,1024]{1,0:T(8,128)(2,1)S(1)}, u32[]{:S(2)}, u32[]{:S(2)}) collective-permute-start(bf16[160,1024]{1,0:T(8,128)(2,1)} %get-tuple-element.115), channel_id=1, source_target_pairs={{0,4},{1,5},{2,6},{3,7},{4,8},{5,9},{6,10},{7,11},{8,12},{9,13},{1... | collective-permute-start | bytes 983048 | tf_op jit(solution)/shard_map/ppermute | solution.py:500
  19.0 10.2 %collective-permute-start.10 = (bf16[160,1024]{1,0:T(8,128)(2,1)}, bf16[160,1024]{1,0:T(8,128)(2,1)S(1)}, u32[]{:S(2)}, u32[]{:S(2)}) collective-permute-start(bf16[160,1024]{1,0:T(8,128)(2,1)} %get-tuple-element.116), channel_id=1, source_target_pairs={{0,12},{1,13},{2,14},{3,15},{4,0},{5,1},{6,2},{7,3},{8,4},{9,5},{1... | collective-permute-start | bytes 983048 | tf_op jit(solution)/shard_map/ppermute | solution.py:500
  20.9 8.9 %collective-permute-start.11 = (bf16[4,160,256]{2,1,0:T(8,128)(2,1)S(1)}, bf16[4,160,256]{2,1,0:T(8,128)(2,1)S(1)}, u32[]{:S(2)}, u32[]{:S(2)}) collective-permute-start(bf16[4,160,256]{2,1,0:T(8,128)(2,1)S(1)} %pad_maximum_fusion.3.refs_1_), channel_id=1, source_target_pairs={{0,1},{1,2},{2,3},{3,0},{4,5},{5,6},{6,7},{7,4},{8,9},{9,10},{10,1... | collective-permute-start | bytes 983048 | tf_op jit(solution)/shard_map/ppermute | solution.py:504
  22.2 15.8 %collective-permute-start.12 = (bf16[4,160,256]{2,1,0:T(8,128)(2,1)S(1)}, bf16[4,160,256]{2,1,0:T(8,128)(2,1)}, u32[]{:S(2)}, u32[]{:S(2)}) collective-permute-start(bf16[4,160,256]{2,1,0:T(8,128)(2,1)S(1)} %pad_maximum_fusion.3.refs_1_), channel_id=1, source_target_pairs={{0,2},{1,3},{2,0},{3,1},{4,6},{5,7},{6,4},{7,5},{8,10},{9,11},{10,... | collective-permute-start | bytes 983048 | tf_op jit(solution)/shard_map/ppermute | solution.py:504
  24.8 13.6 %collective-permute-start.13 = (bf16[4,160,256]{2,1,0:T(8,128)(2,1)S(1)}, bf16[4,160,256]{2,1,0:T(8,128)(2,1)}, u32[]{:S(2)}, u32[]{:S(2)}) collective-permute-start(bf16[4,160,256]{2,1,0:T(8,128)(2,1)S(1)} %pad_maximum_fusion.3.refs_1_), channel_id=1, source_target_pairs={{0,3},{1,0},{2,1},{3,2},{4,7},{5,4},{6,5},{7,6},{8,11},{9,8},{10,9... | collective-permute-start | bytes 983048 | tf_op jit(solution)/shard_map/ppermute | solution.py:504
  26.0 0.6 copy-start.5
  26.6 2.5 %copy-start.7 = (bf16[160,1024]{1,0:T(8,128)(2,1)S(1)}, bf16[160,1024]{1,0:T(8,128)(2,1)}, u32[]{:S(2)}) copy-start(bf16[160,1024]{1,0:T(8,128)(2,1)} %get-tuple-element.121) | copy-start | bytes 983044
  26.6 11.8 %copy-start.6 = (bf16[160,1024]{1,0:T(8,128)(2,1)S(1)}, bf16[160,1024]{1,0:T(8,128)(2,1)}, u32[]{:S(2)}) copy-start(bf16[160,1024]{1,0:T(8,128)(2,1)} %get-tuple-element.117.refs_0_.refs_2_) | copy-start | bytes 983044
  29.0 12.8 %collective-permute-start.14 = (bf16[160,1024]{1,0:T(8,128)(2,1)S(1)}, bf16[160,1024]{1,0:T(8,128)(2,1)S(1)}, u32[]{:S(2)}, u32[]{:S(2)}) collective-permute-start(bf16[160,1024]{1,0:T(8,128)(2,1)S(1)} %copy-done.7), channel_id=1, source_target_pairs={{0,8},{1,9},{2,10},{3,11},{4,12},{5,13},{6,14},{7,15},{8,0},{9,1},... | collective-permute-start | bytes 983048 | tf_op jit(solution)/shard_map/ppermute | solution.py:500
  29.1 27.6 %collective-permute-start.18 = (bf16[160,1024]{1,0:T(8,128)(2,1)S(1)}, bf16[160,1024]{1,0:T(8,128)(2,1)S(1)}, u32[]{:S(2)}, u32[]{:S(2)}) collective-permute-start(bf16[160,1024]{1,0:T(8,128)(2,1)S(1)} %get-tuple-element.135), channel_id=1, source_target_pairs={{0,4},{1,5},{2,6},{3,7},{4,8},{5,9},{6,10},{7,11},{8,12},{9,13},{1... | collective-permute-start | bytes 983048 | tf_op jit(solution)/shard_map/ppermute | solution.py:500
  29.8 27.7 %collective-permute-start.19 = (bf16[160,1024]{1,0:T(8,128)(2,1)S(1)}, bf16[160,1024]{1,0:T(8,128)(2,1)S(1)}, u32[]{:S(2)}, u32[]{:S(2)}) collective-permute-start(bf16[160,1024]{1,0:T(8,128)(2,1)S(1)} %get-tuple-element.136), channel_id=1, source_target_pairs={{0,12},{1,13},{2,14},{3,15},{4,0},{5,1},{6,2},{7,3},{8,4},{9,5},{1... | collective-permute-start | bytes 983048 | tf_op jit(solution)/shard_map/ppermute | solution.py:500
  38.0 19.5 %collective-permute-start.20 = (bf16[160,1024]{1,0:T(8,128)(2,1)S(1)}, bf16[160,1024]{1,0:T(8,128)(2,1)S(1)}, u32[]{:S(2)}, u32[]{:S(2)}) collective-permute-start(bf16[160,1024]{1,0:T(8,128)(2,1)S(1)} %get-tuple-element.138), channel_id=1, source_target_pairs={{0,8},{1,9},{2,10},{3,11},{4,12},{5,13},{6,14},{7,15},{8,0},{9,1},... | collective-permute-start | bytes 983048 | tf_op jit(solution)/shard_map/ppermute | solution.py:500
  54.0 18.8 %collective-permute-start.15 = (bf16[160,1024]{1,0:T(8,128)(2,1)S(1)}, bf16[160,1024]{1,0:T(8,128)(2,1)S(1)}, u32[]{:S(2)}, u32[]{:S(2)}) collective-permute-start(bf16[160,1024]{1,0:T(8,128)(2,1)S(1)} %get-tuple-element.131), channel_id=1, source_target_pairs={{0,12},{1,13},{2,14},{3,15},{4,0},{5,1},{6,2},{7,3},{8,4},{9,5},{1... | collective-permute-start | bytes 983048 | tf_op jit(solution)/shard_map/ppermute | solution.py:500
  55.6 17.2 %collective-permute-start.16 = (bf16[160,1024]{1,0:T(8,128)(2,1)S(1)}, bf16[160,1024]{1,0:T(8,128)(2,1)S(1)}, u32[]{:S(2)}, u32[]{:S(2)}) collective-permute-start(bf16[160,1024]{1,0:T(8,128)(2,1)S(1)} %get-tuple-element.132), channel_id=1, source_target_pairs={{0,8},{1,9},{2,10},{3,11},{4,12},{5,13},{6,14},{7,15},{8,0},{9,1},... | collective-permute-start | bytes 983048 | tf_op jit(solution)/shard_map/ppermute | solution.py:500
  56.8 16.5 %collective-permute-start.17 = (bf16[160,1024]{1,0:T(8,128)(2,1)S(1)}, bf16[160,1024]{1,0:T(8,128)(2,1)S(1)}, u32[]{:S(2)}, u32[]{:S(2)}) collective-permute-start(bf16[160,1024]{1,0:T(8,128)(2,1)S(1)} %get-tuple-element.133), channel_id=1, source_target_pairs={{0,4},{1,5},{2,6},{3,7},{4,8},{5,9},{6,10},{7,11},{8,12},{9,13},{1... | collective-permute-start | bytes 983048 | tf_op jit(solution)/shard_map/ppermute | solution.py:500
  73.3 6.1 %copy-start = (bf16[1,128,8192]{2,1,0:T(8,128)(2,1)S(1)}, bf16[1,128,8192]{2,1,0:T(8,128)(2,1)}, u32[]{:S(2)}) copy-start(bf16[1,128,8192]{2,1,0:T(8,128)(2,1)} %param.7) | copy-start | bytes 6291460
  73.4 6.0 %collective-permute-start.21 = (bf16[4,160,1024]{2,1,0:T(8,128)(2,1)S(1)}, bf16[4,160,1024]{2,1,0:T(8,128)(2,1)S(1)}, u32[]{:S(2)}, u32[]{:S(2)}) collective-permute-start(bf16[4,160,1024]{2,1,0:T(8,128)(2,1)S(1)} %pad_maximum_fusion.mine), channel_id=1, source_target_pairs={{0,16},{16,0},{32,48},{48,32},{64,80},{80,64},{96,112},{112,96},{1... | collective-permute-start | bytes 3932168 | tf_op jit(solution)/shard_map/ppermute | solution.py:508
  76.7 10.1 %collective-permute-start.23 = (bf16[160,1024]{1,0:T(8,128)(2,1)S(1)}, bf16[160,1024]{1,0:T(8,128)(2,1)S(1)}, u32[]{:S(2)}, u32[]{:S(2)}) collective-permute-start(bf16[160,1024]{1,0:T(8,128)(2,1)S(1)} %get-tuple-element.168), channel_id=1, source_target_pairs={{0,12},{1,13},{2,14},{3,15},{4,0},{5,1},{6,2},{7,3},{8,4},{9,5},{1... | collective-permute-start | bytes 983048 | tf_op jit(solution)/shard_map/ppermute | solution.py:500
  78.4 9.9 %collective-permute-start.24 = (bf16[160,1024]{1,0:T(8,128)(2,1)S(1)}, bf16[160,1024]{1,0:T(8,128)(2,1)S(1)}, u32[]{:S(2)}, u32[]{:S(2)}) collective-permute-start(bf16[160,1024]{1,0:T(8,128)(2,1)S(1)} %get-tuple-element.169), channel_id=1, source_target_pairs={{0,4},{1,5},{2,6},{3,7},{4,8},{5,9},{6,10},{7,11},{8,12},{9,13},{1... | collective-permute-start | bytes 983048 | tf_op jit(solution)/shard_map/ppermute | solution.py:500
  80.9 27.8 %collective-permute-start.22 = (bf16[128,8192]{1,0:T(8,128)(2,1)S(1)}, bf16[128,8192]{1,0:T(8,128)(2,1)S(1)}, u32[]{:S(2)}, u32[]{:S(2)}) collective-permute-start(bf16[128,8192]{1,0:T(8,128)(2,1)S(1)} %update.1), channel_id=1, source_target_pairs={{0,16},{16,32},{32,48},{48,64},{64,80},{80,96},{96,112},{1,17},{17... | collective-permute-start | bytes 6291464 | tf_op jit(solution)/shard_map/ppermute | solution.py:512
  84.9 10.6 %collective-permute-start.27 = (bf16[4,160,256]{2,1,0:T(8,128)(2,1)S(1)}, bf16[4,160,256]{2,1,0:T(8,128)(2,1)S(1)}, u32[]{:S(2)}, u32[]{:S(2)}) collective-permute-start(bf16[4,160,256]{2,1,0:T(8,128)(2,1)S(1)} %get-tuple-element.175), channel_id=1, source_target_pairs={{0,2},{1,3},{2,0},{3,1},{4,6},{5,7},{6,4},{7,5},{8,10},{9,11},{10,... | collective-permute-start | bytes 983048 | tf_op jit(solution)/shard_map/ppermute | solution.py:504
  86.8 14.6 %collective-permute-start.28 = (bf16[4,160,256]{2,1,0:T(8,128)(2,1)S(1)}, bf16[4,160,256]{2,1,0:T(8,128)(2,1)S(1)}, u32[]{:S(2)}, u32[]{:S(2)}) collective-permute-start(bf16[4,160,256]{2,1,0:T(8,128)(2,1)S(1)} %get-tuple-element.176), channel_id=1, source_target_pairs={{0,3},{1,0},{2,1},{3,2},{4,7},{5,4},{6,5},{7,6},{8,11},{9,8},{10,9... | collective-permute-start | bytes 983048 | tf_op jit(solution)/shard_map/ppermute | solution.py:504
  88.3 13.9 %collective-permute-start.26 = (bf16[4,160,256]{2,1,0:T(8,128)(2,1)S(1)}, bf16[4,160,256]{2,1,0:T(8,128)(2,1)S(1)}, u32[]{:S(2)}, u32[]{:S(2)}) collective-permute-start(bf16[4,160,256]{2,1,0:T(8,128)(2,1)S(1)} %get-tuple-element.174), channel_id=1, source_target_pairs={{0,1},{1,2},{2,3},{3,0},{4,5},{5,6},{6,7},{7,4},{8,9},{9,10},{10,1... | collective-permute-start | bytes 983048 | tf_op jit(solution)/shard_map/ppermute | solution.py:504
  88.3 14.1 %collective-permute-start.25 = (bf16[160,1024]{1,0:T(8,128)(2,1)S(1)}, bf16[160,1024]{1,0:T(8,128)(2,1)S(1)}, u32[]{:S(2)}, u32[]{:S(2)}) collective-permute-start(bf16[160,1024]{1,0:T(8,128)(2,1)S(1)} %get-tuple-element.172), channel_id=1, source_target_pairs={{0,8},{1,9},{2,10},{3,11},{4,12},{5,13},{6,14},{7,15},{8,0},{9,1},... | collective-permute-start | bytes 983048 | tf_op jit(solution)/shard_map/ppermute | solution.py:500
  102.5 3.8 %collective-permute-start.29 = (bf16[4,160,1024]{2,1,0:T(8,128)(2,1)S(1)}, bf16[4,160,1024]{2,1,0:T(8,128)(2,1)S(1)}, u32[]{:S(2)}, u32[]{:S(2)}) collective-permute-start(bf16[4,160,1024]{2,1,0:T(8,128)(2,1)S(1)} %pad_maximum_fusion.1.mine), channel_id=1, source_target_pairs={{0,16},{16,0},{32,48},{48,32},{64,80},{80,64},{96,112},{112,96},{1... | collective-permute-start | bytes 3932168 | tf_op jit(solution)/shard_map/ppermute | solution.py:508
  103.1 7.6 %collective-permute-start.30 = (bf16[160,256]{1,0:T(8,128)(2,1)S(1)}, bf16[160,256]{1,0:T(8,128)(2,1)S(1)}, u32[]{:S(2)}, u32[]{:S(2)}) collective-permute-start(bf16[160,256]{1,0:T(8,128)(2,1)S(1)} %get-tuple-element.181), channel_id=1, source_target_pairs={{0,4},{1,5},{2,6},{3,7},{4,8},{5,9},{6,10},{7,11},{8,12},{9,13},{1... | collective-permute-start | bytes 245768 | tf_op jit(solution)/shard_map/ppermute | solution.py:500
  103.9 6.8 %collective-permute-start.31 = (bf16[160,256]{1,0:T(8,128)(2,1)S(1)}, bf16[160,256]{1,0:T(8,128)(2,1)S(1)}, u32[]{:S(2)}, u32[]{:S(2)}) collective-permute-start(bf16[160,256]{1,0:T(8,128)(2,1)S(1)} %get-tuple-element.182), channel_id=1, source_target_pairs={{0,8},{1,9},{2,10},{3,11},{4,12},{5,13},{6,14},{7,15},{8,0},{9,1},... | collective-permute-start | bytes 245768 | tf_op jit(solution)/shard_map/ppermute | solution.py:500
  106.3 4.4 %collective-permute-start.32 = (bf16[160,256]{1,0:T(8,128)(2,1)S(1)}, bf16[160,256]{1,0:T(8,128)(2,1)S(1)}, u32[]{:S(2)}, u32[]{:S(2)}) collective-permute-start(bf16[160,256]{1,0:T(8,128)(2,1)S(1)} %get-tuple-element.183), channel_id=1, source_target_pairs={{0,12},{1,13},{2,14},{3,15},{4,0},{5,1},{6,2},{7,3},{8,4},{9,5},{1... | collective-permute-start | bytes 245768 | tf_op jit(solution)/shard_map/ppermute | solution.py:500
  110.7 2.9 %collective-permute-start.33 = (bf16[4,160,256]{2,1,0:T(8,128)(2,1)S(1)}, bf16[4,160,256]{2,1,0:T(8,128)(2,1)S(1)}, u32[]{:S(2)}, u32[]{:S(2)}) collective-permute-start(bf16[4,160,256]{2,1,0:T(8,128)(2,1)S(1)} %pad_maximum_fusion.4.sums), channel_id=1, source_target_pairs={{0,16},{16,0},{32,48},{48,32},{64,80},{80,64},{96,112},{112,96},{1... | collective-permute-start | bytes 983048 | tf_op jit(solution)/shard_map/ppermute | solution.py:508
